TPU v7x, 32 devices: a whole 2x2x4 slice. The times are simulated.
32 devices in a mesh: seq: 4 (over z), ctx: 8 (over y, x, core).
Axes of the slice: x: 2, y: 2, z: 4, core: 2. Of those that a mesh axis runs over, the one named last changes fastest.
Arguments:
- tokens_in: bfloat16 [4, 2048, 1600], P('seq', 'ctx'), may hold values from -6 to 6
- block_index: int32 [16], replicated, may hold values from 0 to 15, each once
- norm_gains: float32 [2, 1600], replicated, may hold values from 0.1 to 1.9
- norm_shifts: float32 [2, 1600], replicated, may hold values from -1.75 to 1.75
- w_qkv: bfloat16 [4800, 1600], P('seq'), may hold values from -0.15625 to 0.15625
- bias_model: float32 [4, 1600], replicated, may hold values from -1.75 to 1.75
- w_out: bfloat16 [1600, 1600], P('seq'), may hold values from -0.625 to 0.625
- w_up: bfloat16 [6400, 1600], P('seq'), may hold values from -0.15625 to 0.15625
- bias_up: float32 [6400], replicated, may hold values from -1.75 to 1.75
- w_down: bfloat16 [1600, 6400], P('seq'), may hold values from -0.078125 to 0.078125
- cotangent: bfloat16 [4, 2048, 1600], P('seq', 'ctx'), may hold values from -6 to 6
Outputs:
- tokens_out: bfloat16 [4, 2048, 1600], P('seq', 'ctx')
- grad_tokens: float32 [4, 2048, 1600], P('seq', 'ctx')
- grad_norm_gains: float32 [2, 1600], replicated
- grad_norm_shifts: float32 [2, 1600], replicated
- grad_w_qkv: float32 [4800, 1600], P('seq')
- grad_bias_model: float32 [4, 1600], replicated
- grad_w_out: float32 [1600, 1600], P('seq')
- grad_w_up: float32 [6400, 1600], P('seq')
- grad_bias_up: float32 [6400], replicated
- grad_w_down: float32 [1600, 6400], P('seq')
Inputs may be any that keep to these rules, and one draw needn't show every extreme that they name: Stored half-block b, rows b * 128 to (b + 1) * 128 - 1 of a sequence, holds positions block_index[b] * 128 onward; each number appears once.
All inputs are finite; a program needn't handle non-finite values.
Results may differ from a plain program's by a relative error of at most 0.017.
Values may be sent and summed in bfloat16 or wider, within the bound.
No kernel may reach another device: no remote copies, remote signals or barrier semaphores. Data moves between devices by JAX's collectives and lax.ppermute only.
A program may use at most 320 MiB of HBM per device.

v0:
```python
import math

import jax
import jax.numpy as jnp
from jax import lax
from jax.sharding import PartitionSpec as P

HEADS = 25
HEAD_DIM = 64


NEGATIVE = -1e30


def shifted(value, axis, by):
    count = lax.axis_size(axis)
    return lax.ppermute(value, axis, [(i, (i + by) % count) for i in range(count)])


def layer_norm(values, gain_row, offset):
    middle = jnp.mean(values, axis=-1, keepdims=True)
    centered = values - middle
    spread = jnp.mean(centered * centered, axis=-1, keepdims=True)
    return centered * lax.rsqrt(spread + 1e-05) * gain_row + offset


def contract_last(left, right):
    return lax.dot_general(
        left, right, (((1,), (1,)), ((), ())), preferred_element_type=jnp.float32
    )


def token_places(block_index, first_row, row_count, half_rows):
    row_ids = first_row + jnp.arange(row_count, dtype=jnp.int32)
    owners = row_ids // half_rows
    matches = owners[:, None] == jnp.arange(block_index.shape[0], dtype=jnp.int32)[None, :]
    first_place = jnp.sum(jnp.where(matches, block_index[None, :], 0), axis=1)
    return first_place * half_rows + row_ids % half_rows


def forward_project(acts, weight):
    return (contract_last(acts, lax.all_gather(weight, "seq", axis=0, tiled=True)), weight)


def backward_project(grad_rows, stored):
    return jnp.dot(
        grad_rows,
        lax.all_gather(stored, "seq", axis=0, tiled=True),
        preferred_element_type=jnp.float32,
    )


def weight_grad(grad_rows, acts):
    return lax.psum_scatter(
        lax.dot_general(
            grad_rows, acts, (((0,), (0,)), ((), ())), preferred_element_type=jnp.float32
        ).astype(jnp.bfloat16),
        "seq",
        scatter_dimension=0,
        tiled=True,
    ).astype(jnp.float32)


def per_device(
    tokens_in,
    block_index,
    norm_gains,
    norm_shifts,
    w_qkv,
    bias_model,
    w_out,
    w_up,
    bias_up,
    w_down,
    cotangent,
):
    tok_rows = tokens_in.shape[1]
    half_rows = tok_rows // 2
    width = tokens_in.shape[2]
    cycle_size = lax.axis_size("ctx")
    cycle_pos = lax.axis_index("ctx")
    my_places = token_places(block_index, cycle_pos * tok_rows, tok_rows, half_rows)
    tokens = tokens_in[0].astype(jnp.float32)
    normed1 = layer_norm(tokens, norm_gains[0], norm_shifts[0]).astype(jnp.bfloat16)
    qkv_pre, qkv_store = forward_project(normed1, w_qkv)
    no_key = jnp.zeros((width,), jnp.float32)
    qkv_rows = (qkv_pre + jnp.concatenate([bias_model[0], no_key, bias_model[1]])).astype(
        jnp.bfloat16
    )
    query_rows = qkv_rows[:, :width]
    key_rows = qkv_rows[:, width : 2 * width]
    value_rows = qkv_rows[:, 2 * width :]
    queries = query_rows.reshape(tok_rows, HEADS, HEAD_DIM)
    starting = (
        jnp.full((HEADS, tok_rows), NEGATIVE, jnp.float32),
        jnp.zeros((HEADS, tok_rows), jnp.float32),
        jnp.zeros((HEADS, tok_rows, HEAD_DIM), jnp.float32),
    )
    key_part = lax.all_gather(key_rows, "ctx", axis=0, tiled=True)
    value_part = lax.all_gather(value_rows, "ctx", axis=0, tiled=True)
    row_count = key_part.shape[0]
    step_rows = math.gcd(row_count, 512)

    def inner(index, state):
        offset = index * step_rows
        key_slice = lax.dynamic_slice_in_dim(key_part, offset, step_rows, 0).reshape(
            step_rows, HEADS, HEAD_DIM
        )
        value_slice = lax.dynamic_slice_in_dim(value_part, offset, step_rows, 0).reshape(
            step_rows, HEADS, HEAD_DIM
        )
        key_places = token_places(block_index, offset, step_rows, half_rows)
        row_max, row_sum, accum = state
        scores = (
            jnp.einsum("qhd,khd->hqk", queries, key_slice, preferred_element_type=jnp.float32)
            * 0.125
        )
        visible = key_places[None, None, :] <= my_places[None, :, None]
        scores = jnp.where(visible, scores, NEGATIVE)
        new_max = jnp.maximum(row_max, jnp.max(scores, axis=2))
        raised = jnp.exp(scores - new_max[:, :, None])
        decay = jnp.exp(row_max - new_max)
        new_sum = row_sum * decay + jnp.sum(raised, axis=2)
        added = jnp.einsum(
            "hqk,khd->hqd",
            raised.astype(jnp.bfloat16),
            value_slice,
            preferred_element_type=jnp.float32,
        )
        return (new_max, new_sum, accum * decay[:, :, None] + added)

    row_max, row_sum, accum = lax.fori_loop(0, row_count // step_rows, inner, starting)
    attended_heads = jnp.transpose(accum / row_sum[:, :, None], (1, 0, 2))
    log_total = row_max + jnp.log(row_sum)
    attended_low = attended_heads.reshape(tok_rows, width).astype(jnp.bfloat16)
    attn_pre, out_store = forward_project(attended_low, w_out)
    resid = tokens + attn_pre + bias_model[2]
    normed2 = layer_norm(resid, norm_gains[1], norm_shifts[1]).astype(jnp.bfloat16)
    up_raw, up_store = forward_project(normed2, w_up)
    up_pre = up_raw + bias_up
    act = jax.nn.gelu(up_pre, approximate=True).astype(jnp.bfloat16)
    down_pre, down_store = forward_project(act, w_down)
    tokens_out = (resid + down_pre + bias_model[3]).astype(jnp.bfloat16)[None]
    seq_cotangent = cotangent[0]
    cotangent_f = seq_cotangent.astype(jnp.float32)
    grad_down_bias = jnp.sum(cotangent_f, axis=0)
    grad_w_down = weight_grad(seq_cotangent, act)
    d_act = backward_project(seq_cotangent, down_store)
    gelu_back = jax.vjp(lambda inner_up: jax.nn.gelu(inner_up, approximate=True), up_pre)[1]
    d_up = gelu_back(d_act)[0].astype(jnp.bfloat16)
    grad_up_bias = jnp.sum(d_up.astype(jnp.float32), axis=0)
    grad_w_up = weight_grad(d_up, normed2)
    d_normed2 = backward_project(d_up, up_store)
    norm_back2 = jax.vjp(layer_norm, resid, norm_gains[1], norm_shifts[1])[1]
    d_resid_norm, grad_gain2, grad_shift2 = norm_back2(d_normed2)
    d_resid = cotangent_f + d_resid_norm
    d_branch = d_resid.astype(jnp.bfloat16)
    grad_out_bias = jnp.sum(d_branch.astype(jnp.float32), axis=0)
    grad_w_out = weight_grad(d_branch, attended_low)
    d_attended = backward_project(d_branch, out_store).astype(jnp.bfloat16)
    d_att_heads = d_attended.reshape(tok_rows, HEADS, HEAD_DIM)
    row_dot = jnp.einsum("qhd,qhd->hq", d_att_heads.astype(jnp.float32), attended_heads)

    def back_step(index, state):
        key_now, value_now, key_grad, value_grad, query_grad = state
        owner = (cycle_pos - index) % cycle_size
        key_places = token_places(block_index, owner * tok_rows, tok_rows, half_rows)
        grads = (key_grad, value_grad, query_grad)
        key_acc, value_acc, query_acc = grads
        key_heads = key_now.reshape(tok_rows, HEADS, HEAD_DIM)
        value_heads = value_now.reshape(tok_rows, HEADS, HEAD_DIM)
        scores = (
            jnp.einsum("qhd,khd->hqk", queries, key_heads, preferred_element_type=jnp.float32)
            * 0.125
        )
        visible = key_places[None, None, :] <= my_places[None, :, None]
        scores = jnp.where(visible, scores, NEGATIVE)
        weights = jnp.exp(scores - log_total[:, :, None])
        d_weights = jnp.einsum(
            "qhd,khd->hqk", d_att_heads, value_heads, preferred_element_type=jnp.float32
        )
        d_scores = (weights * (d_weights - row_dot[:, :, None])).astype(jnp.bfloat16)
        value_add = jnp.einsum(
            "hqk,qhd->khd",
            weights.astype(jnp.bfloat16),
            d_att_heads,
            preferred_element_type=jnp.float32,
        )
        key_add = (
            jnp.einsum("hqk,qhd->khd", d_scores, queries, preferred_element_type=jnp.float32)
            * 0.125
        )
        query_add = (
            jnp.einsum("hqk,khd->qhd", d_scores, key_heads, preferred_element_type=jnp.float32)
            * 0.125
        )
        grads = (
            key_acc + key_add.reshape(tok_rows, width),
            value_acc + value_add.reshape(tok_rows, width),
            query_acc + query_add.reshape(tok_rows, width),
        )
        key_grad, value_grad, query_grad = grads
        key_grad, value_grad = (
            shifted(key_grad.astype(jnp.bfloat16), "ctx", 1).astype(key_grad.dtype),
            shifted(value_grad.astype(jnp.bfloat16), "ctx", 1).astype(value_grad.dtype),
        )
        key_now, value_now = shifted((key_now, value_now), "ctx", 1)
        return (key_now, value_now, key_grad, value_grad, query_grad)

    zero_rows = jnp.zeros((tok_rows, width), jnp.float32)
    cycle_state = (key_rows, value_rows, zero_rows, zero_rows, zero_rows)
    cycle_state = lax.fori_loop(0, cycle_size, back_step, cycle_state)
    d_qkv = jnp.concatenate([cycle_state[4], cycle_state[2], cycle_state[3]], axis=1).astype(
        jnp.bfloat16
    )
    d_qkv_f = d_qkv.astype(jnp.float32)
    grad_query_bias = jnp.sum(d_qkv_f[:, :width], axis=0)
    grad_value_bias = jnp.sum(d_qkv_f[:, 2 * width :], axis=0)
    grad_w_qkv = weight_grad(d_qkv, normed1)
    d_normed1 = backward_project(d_qkv, qkv_store)
    norm_back1 = jax.vjp(layer_norm, tokens, norm_gains[0], norm_shifts[0])[1]
    d_tokens_norm, grad_gain1, grad_shift1 = norm_back1(d_normed1)
    grad_tokens = (d_resid + d_tokens_norm)[None]
    grad_w_qkv, grad_w_out, grad_w_up, grad_w_down = (
        lax.psum(grad_w_qkv.astype(jnp.bfloat16), "ctx").astype(jnp.float32),
        lax.psum(grad_w_out.astype(jnp.bfloat16), "ctx").astype(jnp.float32),
        lax.psum(grad_w_up.astype(jnp.bfloat16), "ctx").astype(jnp.float32),
        lax.psum(grad_w_down.astype(jnp.bfloat16), "ctx").astype(jnp.float32),
    )
    gain_grads = jnp.stack([grad_gain1, grad_gain2])
    shift_grads = jnp.stack([grad_shift1, grad_shift2])
    bias_grads = jnp.stack([grad_query_bias, grad_value_bias, grad_out_bias, grad_down_bias])
    gain_grads, shift_grads, bias_grads, grad_up_bias = lax.psum(
        (gain_grads, shift_grads, bias_grads, grad_up_bias), ("seq", "ctx")
    )
    return (
        tokens_out,
        grad_tokens,
        gain_grads,
        shift_grads,
        grad_w_qkv,
        bias_grads,
        grad_w_out,
        grad_w_up,
        grad_up_bias,
        grad_w_down,
    )


def solution(mesh):
    placed = (
        P("seq", "ctx", None),
        P(),
        P(),
        P(),
        P("seq", None),
        P(),
        P("seq", None),
        P("seq", None),
        P(),
        P("seq", None),
        P("seq", "ctx", None),
    )
    return jax.shard_map(
        per_device,
        mesh=mesh,
        in_specs=placed,
        out_specs=(
            P("seq", "ctx", None),
            P("seq", "ctx", None),
            P(),
            P(),
            P("seq", None),
            P(),
            P("seq", None),
            P("seq", None),
            P(),
            P("seq", None),
        ),
        check_vma=False,
    )
```

profile of v0, /device:TPU:0, one launch (start us, length us, event | category | flops | bytes accessed | tf_op | source)
XLA Modules:
  0.0 2950.0 jit_solution(15682655611996508811)
XLA Ops:
  9.4 276.6 %all-gather.7.cloned.1.call-done = bf16[4800,1600]{1,0:T(8,128)(2,1)} async-done(((bf16[1200,1600]{1,0:T(8,128)(2,1)}), bf16[4800,1600]{1,0:T(8,128)(2,1)}) %all-gather.7.cloned.1.call-update) | async-done | bytes 15360016 | tf_op jit(solution)/shard_map/all_gather | solution.py:42
  286.0 10.4 fusion.34
  301.0 42.9 %all-gather.9.cloned.1.call-done = bf16[2048,1600]{0,1:T(8,128)(2,1)} async-done(((bf16[256,1600]{0,1:T(8,128)(2,1)}), bf16[2048,1600]{0,1:T(8,128)(2,1)}) %all-gather.9.cloned.1.call-update) | async-done | bytes 6553616 | tf_op jit(solution)/shard_map/all_gather | solution.py:99
  344.0 49.7 %all-gather.11.cloned.1.call-done = bf16[2048,1600]{0,1:T(8,128)(2,1)} async-done(((bf16[256,1600]{0,1:T(8,128)(2,1)}), bf16[2048,1600]{0,1:T(8,128)(2,1)}) %all-gather.11.cloned.1.call-update) | async-done | bytes 6553616 | tf_op jit(solution)/shard_map/all_gather | solution.py:100
  393.7 90.3 %while.45 = (s32[]{:T(128)}, f32[25,256]{1,0:T(8,128)S(1)}, f32[25,256]{1,0:T(8,128)S(1)}, f32[25,256,64]{1,2,0:T(8,128)}, s32[16]{0:T(128)S(1)}, /*index=5*/s32...) while((s32[]{:T(128)}, f32[25,256]{1,0:T(8,128)S(1)}, ...), condition=%wide.region_7.8_spmd.clone, body=%wide.region_3.7_spmd.clone.sunk | while | flops 863229696 | bytes 106362152 | solution.py:132
  396.1 7.4 fusion.129
  403.5 7.5 fusion.130
  418.3 7.0 fusion.129
  425.3 7.0 fusion.130
  433.9 4.8 fusion.132
  441.1 7.0 fusion.129
  448.0 7.0 fusion.130
  456.6 4.8 fusion.132
  463.8 7.0 fusion.129
  470.8 7.0 fusion.130
  479.3 4.8 fusion.132
  486.5 8.0 all-gather.13.cloned.1.call-done
  494.6 4.7 fusion.72
  499.6 357.0 %all-gather.15.cloned.1.call-done = bf16[6400,1600]{1,0:T(8,128)(2,1)} async-done(((bf16[1600,1600]{1,0:T(8,128)(2,1)}), bf16[6400,1600]{1,0:T(8,128)(2,1)}) %all-gather.15.cloned.1.call-update) | async-done | bytes 20480016 | tf_op jit(solution)/shard_map/all_gather | solution.py:42
  856.6 13.7 convolution_add_fusion
  870.3 335.1 %all-gather.17.cloned.1.call-done = bf16[1600,6400]{1,0:T(8,128)(2,1)} async-done(((bf16[400,6400]{1,0:T(8,128)(2,1)}), bf16[1600,6400]{1,0:T(8,128)(2,1)}) %all-gather.17.cloned.1.call-update) | async-done | bytes 20480016 | tf_op jit(solution)/shard_map/all_gather | solution.py:42
  1205.4 17.7 convert_reduce_fusion
  1223.1 16.9 multiply_reduce_fusion
  1244.2 4.1 convolution_convert_fusion.3
  1248.3 4.9 convolution_convert_fusion.4
  1253.7 357.1 %while.46 = (s32[]{:T(128)}, bf16[256,1600]{0,1:T(8,128)(2,1)}, bf16[256,1600]{0,1:T(8,128)(2,1)}, f32[256,1600]{0,1:T(8,128)}, f32[256,1600]{0,1:T(8,128)}, /*i...) while((s32[]{:T(128)}, bf16[256,1600]{0,1:T(8,128)(2,1)}, ...), condition=%wide.region_14.15_spmd.clone, body=%wide.region_12.14_spmd.clone.sunk | while | flops 1069960448 | bytes 114150144 | solution.py:212
  1263.2 4.0 multiply_convert_fusion.5
  1278.8 8.6 collective-permute-done.2
  1289.8 6.3 collective-permute-done.3
  1306.7 4.0 multiply_convert_fusion.5
  1323.1 8.8 collective-permute-done.2
  1334.4 6.3 collective-permute-done.3
  1350.6 4.0 multiply_convert_fusion.5
  1367.7 8.9 collective-permute-done.2
  1379.0 6.3 collective-permute-done.3
  1395.2 4.0 multiply_convert_fusion.5
  1412.3 8.9 collective-permute-done.2
  1423.6 6.3 collective-permute-done.3
  1439.7 4.0 multiply_convert_fusion.5
  1456.8 8.9 collective-permute-done.2
  1468.2 6.3 collective-permute-done.3
  1484.3 4.0 multiply_convert_fusion.5
  1501.4 8.9 collective-permute-done.2
  1512.8 6.3 collective-permute-done.3
  1528.9 4.0 multiply_convert_fusion.5
  1546.0 8.9 collective-permute-done.2
  1557.4 6.3 collective-permute-done.3
  1573.5 4.0 multiply_convert_fusion.5
  1590.6 8.9 collective-permute-done.2
  1601.9 6.3 collective-permute-done.3
  1614.4 13.9 convolution_convert_fusion.2
  1629.7 12.8 convolution_convert_fusion.1
  1643.7 11.9 fusion.26
  1655.7 237.5 %reduce-scatter.13.cloned.1.call-done = bf16[1200,1600]{1,0:T(8,128)(2,1)} async-done(((bf16[4800,1600]{1,0:T(8,128)(2,1)}), bf16[1200,1600]{1,0:T(8,128)(2,1)}) %reduce-scatter.13.cloned.1.call-update) | async-done | bytes 3840016
  1893.2 357.0 %reduce-scatter.9.cloned.1.call-done = bf16[1600,1600]{1,0:T(8,128)(2,1)} async-done(((bf16[6400,1600]{1,0:T(8,128)(2,1)}), bf16[1600,1600]{1,0:T(8,128)(2,1)}) %reduce-scatter.9.cloned.1.call-update) | async-done | bytes 5120016 | tf_op jit(solution)/shard_map/reduce_scatter | solution.py:54
  2250.3 343.5 %reduce-scatter.11.cloned.1.call-done = bf16[400,6400]{1,0:T(8,128)(2,1)} async-done(((bf16[1600,6400]{1,0:T(8,128)(2,1)}), bf16[400,6400]{1,0:T(8,128)(2,1)}) %reduce-scatter.11.cloned.1.call-update) | async-done | bytes 5120016 | tf_op jit(solution)/shard_map/reduce_scatter | solution.py:54
  2594.1 13.8 fusion.67
  2610.5 3.5 convert_reduce_fusion.1
  2616.9 16.3 fusion.38
  2633.2 174.4 %all-reduce.8.cloned.1.call-done = (bf16[1200,1600]{1,0:T(8,128)(2,1)}, bf16[400,1600]{1,0:T(8,128)(2,1)}, bf16[1600,1600]{1,0:T(8,128)(2,1)}, bf16[400,6400]{1,0:T(8,128)(2,1)}) async-done(((bf16[1200,1600]{1,0:T(8,128)(2,1)}, bf16[400,1600]{1,0:T(8,128)(2,1)}, bf16[1600,1600]{1,0:T(8,128)(2,1)}, bf16[400,6400]{1,0:T(8,128)(2,1)}), (bf16[1200,1600]{1,0:T(8,128)(2,1)}, bf16[400,1600]{1,0:T(8,128)(2,1)}, ...) | async-done | bytes 15360016 | tf_op jit(solution)/shard_map/psum | solution.py:225
  2807.7 6.1 convert_element_type.175
  2815.4 4.8 convert_element_type.181
  2820.3 4.7 convert_element_type.185
  2824.9 112.5 %all-reduce.6.cloned.1.call-done = (f32[2,1600]{1,0:T(2,128)}, f32[2,1600]{1,0:T(2,128)}, f32[4,1600]{1,0:T(4,128)}, f32[6400]{0:T(1024)}) async-done(((f32[2,1600]{1,0:T(2,128)}, f32[2,1600]{1,0:T(2,128)}, f32[4,1600]{1,0:T(4,128)}, f32[6400]{0:T(1024)}), (f32[2,1600]{1,0:T(2,128)}, f32[2,1600]{1,0:T(2,128)}, f32[4,1600]{1,0:T(4,128)}, f32[6400]{0:T(1024)})) %all-reduce.6.cloned.1.call-update) | async-done | bytes 76816 | tf_op jit(solution)/shard_map/psum | solution.py:233
  (502 shorter events, 253.8 us)
Async XLA Ops:
  7.2 278.8 %all-gather.7.cloned.1.call-start = ((), (), s32[]{:S(2)}) async-start(), calls=%async_computation.4 | async-start | bytes 19968000 | tf_op jit(solution)/shard_map/all_gather | solution.py:42
  8.0 336.0 %all-gather.9.cloned.1.call-start = ((), (), s32[]{:S(2)}) async-start(), calls=%async_computation.5 | async-start | bytes 7372800 | tf_op jit(solution)/shard_map/all_gather | solution.py:99
  8.8 277.2 %copy-start.28 = (f32[1600]{0:T(1024)}, f32[1600]{0:T(1024)S(1)}, u32[]{:S(2)}) copy-start(f32[1600]{0:T(1024)S(1)} %get-tuple-element.757) | copy-start | bytes 19204
  8.8 277.2 %copy-start.45 = (f32[1600]{0:T(1024)}, f32[1600]{0:T(1024)S(1)}, u32[]{:S(2)}) copy-start(f32[1600]{0:T(1024)S(1)} %get-tuple-element.683) | copy-start | bytes 19204
  9.1 287.3 %copy-start.33 = (f32[256]{0:T(256)}, f32[256]{0:T(256)S(1)}, u32[]{:S(2)}) copy-start(f32[256]{0:T(256)S(1)} %broadcast_multiply_fusion.1) | copy-start | bytes 3076
  9.4 287.0 %copy-start.41 = (f32[256]{0:T(256)}, f32[256]{0:T(256)S(1)}, u32[]{:S(2)}) copy-start(f32[256]{0:T(256)S(1)} %fusion.49) | copy-start | bytes 3076
  9.4 287.0 %copy-start.37 = (f32[256]{0:T(256)}, f32[256]{0:T(256)S(1)}, u32[]{:S(2)}) copy-start(f32[256]{0:T(256)S(1)} %fusion.61) | copy-start | bytes 3076
  297.8 95.9 %all-gather.11.cloned.1.call-start = ((), (), s32[]{:S(2)}) async-start(), calls=%async_computation.6 | async-start | bytes 7372800 | tf_op jit(solution)/shard_map/all_gather | solution.py:100
  298.5 196.0 %all-gather.13.cloned.1.call-start = ((), (), s32[]{:S(2)}) async-start(), calls=%async_computation.7 | async-start | bytes 6656000 | tf_op jit(solution)/shard_map/all_gather | solution.py:42
  299.1 557.5 %all-gather.15.cloned.1.call-start = ((), (), s32[]{:S(2)}) async-start(), calls=%async_computation.8 | async-start | bytes 26624000 | tf_op jit(solution)/shard_map/all_gather | solution.py:42
  299.7 905.7 %all-gather.17.cloned.1.call-start = ((), (), s32[]{:S(2)}) async-start(), calls=%async_computation.9 | async-start | bytes 25600000 | tf_op jit(solution)/shard_map/all_gather | solution.py:42
  300.3 1355.5 %reduce-scatter.7.cloned.1.call-start = ((), (), s32[]{:S(2)}) async-start(), calls=%async_computation.10 | async-start | bytes 6656000 | tf_op jit(solution)/shard_map/reduce_scatter | solution.py:54
  494.6 362.0 %copy-start.47 = (f32[6400]{0:T(1024)S(1)}, f32[6400]{0:T(1024)}, u32[]{:S(2)}) copy-start(f32[6400]{0:T(1024)} %param.23) | copy-start | bytes 76804
  499.2 740.8 %copy-start.12 = (f32[256,1600]{0,1:T(8,128)}, f32[256,1600]{0,1:T(8,128)S(1)}, u32[]{:S(2)}) copy-start(f32[256,1600]{0,1:T(8,128)S(1)} %get-tuple-element.752) | copy-start | bytes 4915204
  1253.7 639.6 %reduce-scatter.13.cloned.1.call-start = ((), (), s32[]{:S(2)}) async-start(), calls=%async_computation.13 | async-start | bytes 19968000
  1256.8 41.8 %collective-permute-start = (bf16[256,1600]{0,1:T(8,128)(2,1)}, bf16[256,1600]{0,1:T(8,128)(2,1)}, u32[]{:S(2)}, u32[]{:S(2)}) collective-permute-start(bf16[256,1600]{0,1:T(8,128)(2,1)} %copy.51), channel_id=1, source_target_pairs={{0,1},{1,2},{2,3},{3,4},{4,5},{5,6},{6,7},{7,0},{8,9},{9,10},{10,1... | collective-permute-start | bytes 2457608 | tf_op jit(solution)/shard_map/while/body/eval_jaxpr/ppermute | solution.py:17
  1258.9 39.8 %collective-permute-start.1 = (bf16[256,1600]{0,1:T(8,128)(2,1)}, bf16[256,1600]{0,1:T(8,128)(2,1)}, u32[]{:S(2)}, u32[]{:S(2)}) collective-permute-start(bf16[256,1600]{0,1:T(8,128)(2,1)} %copy.52), channel_id=1, source_target_pairs={{0,1},{1,2},{2,3},{3,4},{4,5},{5,6},{6,7},{7,0},{8,9},{9,10},{10,1... | collective-permute-start | bytes 2457608 | tf_op jit(solution)/shard_map/while/body/eval_jaxpr/ppermute | solution.py:17
  1270.4 16.9 collective-permute-start.2
  1274.5 21.6 collective-permute-start.3
  1301.4 41.8 %collective-permute-start = (bf16[256,1600]{0,1:T(8,128)(2,1)}, bf16[256,1600]{0,1:T(8,128)(2,1)}, u32[]{:S(2)}, u32[]{:S(2)}) collective-permute-start(bf16[256,1600]{0,1:T(8,128)(2,1)} %copy.51), channel_id=1, source_target_pairs={{0,1},{1,2},{2,3},{3,4},{4,5},{5,6},{6,7},{7,0},{8,9},{9,10},{10,1... | collective-permute-start | bytes 2457608 | tf_op jit(solution)/shard_map/while/body/eval_jaxpr/ppermute | solution.py:17
  1303.5 39.7 %collective-permute-start.1 = (bf16[256,1600]{0,1:T(8,128)(2,1)}, bf16[256,1600]{0,1:T(8,128)(2,1)}, u32[]{:S(2)}, u32[]{:S(2)}) collective-permute-start(bf16[256,1600]{0,1:T(8,128)(2,1)} %copy.52), channel_id=1, source_target_pairs={{0,1},{1,2},{2,3},{3,4},{4,5},{5,6},{6,7},{7,0},{8,9},{9,10},{10,1... | collective-permute-start | bytes 2457608 | tf_op jit(solution)/shard_map/while/body/eval_jaxpr/ppermute | solution.py:17
  1313.9 18.0 collective-permute-start.2
  1318.0 22.7 collective-permute-start.3
  1346.0 41.8 %collective-permute-start = (bf16[256,1600]{0,1:T(8,128)(2,1)}, bf16[256,1600]{0,1:T(8,128)(2,1)}, u32[]{:S(2)}, u32[]{:S(2)}) collective-permute-start(bf16[256,1600]{0,1:T(8,128)(2,1)} %copy.51), channel_id=1, source_target_pairs={{0,1},{1,2},{2,3},{3,4},{4,5},{5,6},{6,7},{7,0},{8,9},{9,10},{10,1... | collective-permute-start | bytes 2457608 | tf_op jit(solution)/shard_map/while/body/eval_jaxpr/ppermute | solution.py:17
  1348.1 39.8 %collective-permute-start.1 = (bf16[256,1600]{0,1:T(8,128)(2,1)}, bf16[256,1600]{0,1:T(8,128)(2,1)}, u32[]{:S(2)}, u32[]{:S(2)}) collective-permute-start(bf16[256,1600]{0,1:T(8,128)(2,1)} %copy.52), channel_id=1, source_target_pairs={{0,1},{1,2},{2,3},{3,4},{4,5},{5,6},{6,7},{7,0},{8,9},{9,10},{10,1... | collective-permute-start | bytes 2457608 | tf_op jit(solution)/shard_map/while/body/eval_jaxpr/ppermute | solution.py:17
  1357.8 18.8 collective-permute-start.2
  1361.9 23.5 collective-permute-start.3
  1367.6 20.2 copy-start.8
  1367.6 20.2 copy-start.2
  1367.7 20.2 copy-start.27
  1390.6 41.8 %collective-permute-start = (bf16[256,1600]{0,1:T(8,128)(2,1)}, bf16[256,1600]{0,1:T(8,128)(2,1)}, u32[]{:S(2)}, u32[]{:S(2)}) collective-permute-start(bf16[256,1600]{0,1:T(8,128)(2,1)} %copy.51), channel_id=1, source_target_pairs={{0,1},{1,2},{2,3},{3,4},{4,5},{5,6},{6,7},{7,0},{8,9},{9,10},{10,1... | collective-permute-start | bytes 2457608 | tf_op jit(solution)/shard_map/while/body/eval_jaxpr/ppermute | solution.py:17
  1392.7 39.8 %collective-permute-start.1 = (bf16[256,1600]{0,1:T(8,128)(2,1)}, bf16[256,1600]{0,1:T(8,128)(2,1)}, u32[]{:S(2)}, u32[]{:S(2)}) collective-permute-start(bf16[256,1600]{0,1:T(8,128)(2,1)} %copy.52), channel_id=1, source_target_pairs={{0,1},{1,2},{2,3},{3,4},{4,5},{5,6},{6,7},{7,0},{8,9},{9,10},{10,1... | collective-permute-start | bytes 2457608 | tf_op jit(solution)/shard_map/while/body/eval_jaxpr/ppermute | solution.py:17
  1402.4 18.8 collective-permute-start.2
  1406.5 23.5 collective-permute-start.3
  1435.2 41.8 %collective-permute-start = (bf16[256,1600]{0,1:T(8,128)(2,1)}, bf16[256,1600]{0,1:T(8,128)(2,1)}, u32[]{:S(2)}, u32[]{:S(2)}) collective-permute-start(bf16[256,1600]{0,1:T(8,128)(2,1)} %copy.51), channel_id=1, source_target_pairs={{0,1},{1,2},{2,3},{3,4},{4,5},{5,6},{6,7},{7,0},{8,9},{9,10},{10,1... | collective-permute-start | bytes 2457608 | tf_op jit(solution)/shard_map/while/body/eval_jaxpr/ppermute | solution.py:17
  1437.3 39.8 %collective-permute-start.1 = (bf16[256,1600]{0,1:T(8,128)(2,1)}, bf16[256,1600]{0,1:T(8,128)(2,1)}, u32[]{:S(2)}, u32[]{:S(2)}) collective-permute-start(bf16[256,1600]{0,1:T(8,128)(2,1)} %copy.52), channel_id=1, source_target_pairs={{0,1},{1,2},{2,3},{3,4},{4,5},{5,6},{6,7},{7,0},{8,9},{9,10},{10,1... | collective-permute-start | bytes 2457608 | tf_op jit(solution)/shard_map/while/body/eval_jaxpr/ppermute | solution.py:17
  1447.0 18.8 collective-permute-start.2
  1451.0 23.5 collective-permute-start.3
  1456.8 20.2 copy-start.2
  1456.8 20.2 copy-start.27
  1479.8 41.8 %collective-permute-start = (bf16[256,1600]{0,1:T(8,128)(2,1)}, bf16[256,1600]{0,1:T(8,128)(2,1)}, u32[]{:S(2)}, u32[]{:S(2)}) collective-permute-start(bf16[256,1600]{0,1:T(8,128)(2,1)} %copy.51), channel_id=1, source_target_pairs={{0,1},{1,2},{2,3},{3,4},{4,5},{5,6},{6,7},{7,0},{8,9},{9,10},{10,1... | collective-permute-start | bytes 2457608 | tf_op jit(solution)/shard_map/while/body/eval_jaxpr/ppermute | solution.py:17
  1481.9 39.8 %collective-permute-start.1 = (bf16[256,1600]{0,1:T(8,128)(2,1)}, bf16[256,1600]{0,1:T(8,128)(2,1)}, u32[]{:S(2)}, u32[]{:S(2)}) collective-permute-start(bf16[256,1600]{0,1:T(8,128)(2,1)} %copy.52), channel_id=1, source_target_pairs={{0,1},{1,2},{2,3},{3,4},{4,5},{5,6},{6,7},{7,0},{8,9},{9,10},{10,1... | collective-permute-start | bytes 2457608 | tf_op jit(solution)/shard_map/while/body/eval_jaxpr/ppermute | solution.py:17
  1491.6 18.8 collective-permute-start.2
  1495.6 23.5 collective-permute-start.3
  1501.4 20.2 copy-start.8
  1501.4 20.2 copy-start.2
  1501.4 20.2 copy-start.27
  1524.4 41.8 %collective-permute-start = (bf16[256,1600]{0,1:T(8,128)(2,1)}, bf16[256,1600]{0,1:T(8,128)(2,1)}, u32[]{:S(2)}, u32[]{:S(2)}) collective-permute-start(bf16[256,1600]{0,1:T(8,128)(2,1)} %copy.51), channel_id=1, source_target_pairs={{0,1},{1,2},{2,3},{3,4},{4,5},{5,6},{6,7},{7,0},{8,9},{9,10},{10,1... | collective-permute-start | bytes 2457608 | tf_op jit(solution)/shard_map/while/body/eval_jaxpr/ppermute | solution.py:17
  1526.5 39.8 %collective-permute-start.1 = (bf16[256,1600]{0,1:T(8,128)(2,1)}, bf16[256,1600]{0,1:T(8,128)(2,1)}, u32[]{:S(2)}, u32[]{:S(2)}) collective-permute-start(bf16[256,1600]{0,1:T(8,128)(2,1)} %copy.52), channel_id=1, source_target_pairs={{0,1},{1,2},{2,3},{3,4},{4,5},{5,6},{6,7},{7,0},{8,9},{9,10},{10,1... | collective-permute-start | bytes 2457608 | tf_op jit(solution)/shard_map/while/body/eval_jaxpr/ppermute | solution.py:17
  1536.1 18.8 collective-permute-start.2
  1540.2 23.5 collective-permute-start.3
  1546.0 20.2 copy-start.8
  1546.0 20.2 copy-start.2
  1546.0 20.2 copy-start.27
  1569.0 41.8 %collective-permute-start = (bf16[256,1600]{0,1:T(8,128)(2,1)}, bf16[256,1600]{0,1:T(8,128)(2,1)}, u32[]{:S(2)}, u32[]{:S(2)}) collective-permute-start(bf16[256,1600]{0,1:T(8,128)(2,1)} %copy.51), channel_id=1, source_target_pairs={{0,1},{1,2},{2,3},{3,4},{4,5},{5,6},{6,7},{7,0},{8,9},{9,10},{10,1... | collective-permute-start | bytes 2457608 | tf_op jit(solution)/shard_map/while/body/eval_jaxpr/ppermute | solution.py:17
  1571.1 39.8 %collective-permute-start.1 = (bf16[256,1600]{0,1:T(8,128)(2,1)}, bf16[256,1600]{0,1:T(8,128)(2,1)}, u32[]{:S(2)}, u32[]{:S(2)}) collective-permute-start(bf16[256,1600]{0,1:T(8,128)(2,1)} %copy.52), channel_id=1, source_target_pairs={{0,1},{1,2},{2,3},{3,4},{4,5},{5,6},{6,7},{7,0},{8,9},{9,10},{10,1... | collective-permute-start | bytes 2457608 | tf_op jit(solution)/shard_map/while/body/eval_jaxpr/ppermute | solution.py:17
  1580.7 18.8 collective-permute-start.2
  1584.8 23.5 collective-permute-start.3
  1590.6 20.2 copy-start.2
  1590.6 20.2 copy-start.27
  1628.3 621.9 %reduce-scatter.9.cloned.1.call-start = ((), (), s32[]{:S(2)}) async-start(), calls=%async_computation.11 | async-start | bytes 26624000 | tf_op jit(solution)/shard_map/reduce_scatter | solution.py:54
  1642.6 951.2 %reduce-scatter.11.cloned.1.call-start = ((), (), s32[]{:S(2)}) async-start(), calls=%async_computation.12 | async-start | bytes 25600000 | tf_op jit(solution)/shard_map/reduce_scatter | solution.py:54
  1655.7 1152.0 %all-reduce.8.cloned.1.call-start = ((), (), s32[]{:S(2)}) async-start(), calls=%async_computation.15 | async-start | bytes 31539200 | tf_op jit(solution)/shard_map/psum | solution.py:225
  2593.8 343.6 %all-reduce.6.cloned.1.call-start = ((), (), s32[]{:S(2)}) async-start(), calls=%async_computation.14 | async-start | bytes 163840 | tf_op jit(solution)/shard_map/psum | solution.py:233
  (91 other events, 573.9 us)
Sparse Core Ops, SparseCore 0:
  9.6 276.3 all-gather.6
  297.9 46.0 all-gather.8
  345.8 47.8 all-gather.10
  395.1 99.4 all-gather.12
  496.0 360.5 all-gather.14
  858.0 347.3 all-gather.16
  1253.8 93.8 reduce-scatter.6
  1628.5 264.7 reduce-scatter.12
  1895.7 354.4 reduce-scatter.8
  2252.6 341.1 reduce-scatter.10
  2598.1 209.5 all-reduce.7
  2815.9 121.4 all-reduce.5
where the time goes:
time: 2960 us; the launch traced here: 2950 us
  waiting for transfers between devices  2420 us (82%)
  matrix products  295 us (10%)
  other arithmetic  128 us (4%)
  local copies, waits for them, and re-layouts  66.1 us (2%)
    all_gather x4, waiting for transfers between devices, forward_project(): lax.all_gather(weight, 'seq', axis=0, tiled=True)  977 us
    reduce_scatter x3, waiting for transfers between devices, weight_grad(): lax.psum_scatter(lax.dot_general(grad_rows, acts, (((0,), (0,)), ((), ())...  701 us
    unnamed x13, waiting for transfers between devices  241 us
    psum x1, waiting for transfers between devices, per_device(): lax.psum(grad_w_qkv.astype(jnp.bfloat16), 'ctx').astype(jnp.float32)  174 us
    ppermute x32, waiting for transfers between devices, shifted(): lax.ppermute(value, axis, [(i, (i + by) % count) for i in range(count)])  121 us
    psum x1, waiting for transfers between devices, per_device(): lax.psum((gain_grads, shift_grads, bias_grads, grad_up_bias), ('seq', 'ct...  112 us
  transfers between devices with their start and end apart: 44, of which 27 were waited for; matrix products, arithmetic and copies ran while one was open for 14% of the time, Pallas kernels for 0%

commit v1 on v0

v1 whole, which is shorter than its diff:
```python
import functools
import math

import jax
import jax.numpy as jnp
import numpy as np
from jax import lax
from jax.experimental import pallas as pl
from jax.experimental.pallas import tpu as pltpu
from jax.sharding import PartitionSpec as P

HEADS = 25
HEAD_DIM = 64
LOG2E = 1.4426950408889634
NEGATIVE = -1e30
VMEM_LIMIT = 56 * 1024 * 1024


def layer_norm(values, gain_row, offset):
    middle = jnp.mean(values, axis=-1, keepdims=True)
    centered = values - middle
    spread = jnp.mean(centered * centered, axis=-1, keepdims=True)
    return centered * lax.rsqrt(spread + 1e-05) * gain_row + offset


def contract_last(left, right):
    return lax.dot_general(
        left, right, (((1,), (1,)), ((), ())), preferred_element_type=jnp.float32
    )


def contract_first(left, right):
    return lax.dot_general(
        left, right, (((0,), (0,)), ((), ())), preferred_element_type=jnp.float32
    )


class HeadPlan:
    def __init__(self, seq_size, ctx_size, shard_rows, width):
        first = [HEADS * c // ctx_size for c in range(ctx_size + 1)]
        self.slots = max(first[c + 1] - first[c] for c in range(ctx_size))
        self.count = [first[c + 1] - first[c] for c in range(ctx_size)]
        self.window = [min(first[c], HEADS - self.slots) for c in range(ctx_size)]
        self.skip = [first[c] - self.window[c] for c in range(ctx_size)]
        self.rows = self.slots * HEAD_DIM
        rows = self.rows
        self.piece_start = np.zeros((seq_size, ctx_size), np.int32)
        self.range_from = np.zeros((ctx_size, 3), np.int32)
        self.piece_from = np.zeros((ctx_size, seq_size), np.int32)
        self.source_row = np.zeros((seq_size, shard_rows), np.int32)
        for c in range(ctx_size):
            for t in range(3):
                begin = t * width + self.window[c] * HEAD_DIM
                for z in range(seq_size):
                    low, high = z * shard_rows, (z + 1) * shard_rows
                    if begin + rows <= low or begin >= high:
                        continue
                    start = min(max(begin, low), high - rows)
                    self.piece_start[z, c] = start - low
                    self.piece_from[c, z] = rows + t * rows + start - begin
                    if low <= begin < high:
                        self.range_from[c, t] = z * rows + begin - start
                used = t * width + first[c] * HEAD_DIM
                for row in range(used, used + self.count[c] * HEAD_DIM):
                    z = row // shard_rows
                    inside = row - z * shard_rows
                    self.source_row[z, inside] = c * rows + inside - self.piece_start[z, c]


def attention_forward_kernel(order_ref, q_ref, k_ref, v_ref, out_ref, qs, ks, vs, *, half, tile):
    length = q_ref.shape[0]
    for p in range(length // half):
        rows = pl.ds(pl.multiple_of(order_ref[p] * half, half), half)
        here = slice(p * half, (p + 1) * half)
        qs[here, :] = q_ref[rows, :]
        ks[here, :] = k_ref[rows, :]
        vs[here, :] = v_ref[rows, :]
    visible = lax.broadcasted_iota(jnp.int32, (tile, tile), 1) <= lax.broadcasted_iota(
        jnp.int32, (tile, tile), 0
    )
    scale = 0.125 * LOG2E
    for i in range(length // tile):
        span = (i + 1) * tile
        outs = []
        for h in range(q_ref.shape[1] // HEAD_DIM):
            lanes = slice(h * HEAD_DIM, (h + 1) * HEAD_DIM)
            q = qs[i * tile : span, lanes]
            scores = contract_last(q, ks[:span, lanes])
            last = jnp.where(visible, scores[:, i * tile :], NEGATIVE)
            scores = jnp.concatenate([scores[:, : i * tile], last], axis=1) if i else last
            top = jnp.max(scores, axis=1, keepdims=True)
            raised = jnp.exp2(scores * scale - top * scale)
            total = jnp.sum(raised, axis=1, keepdims=True)
            weights = (raised * (1.0 / total)).astype(jnp.bfloat16)
            outs.append(
                jnp.dot(weights, vs[:span, lanes], preferred_element_type=jnp.float32)
            )
        merged = jnp.concatenate(outs, axis=1).astype(out_ref.dtype)
        for j in range(tile // half):
            rows = pl.ds(pl.multiple_of(order_ref[i * (tile // half) + j] * half, half), half)
            out_ref[rows, :] = merged[j * half : (j + 1) * half, :]


def attention_forward(order, qkv, half, window):
    length = qkv.shape[0]
    groups = window // 128
    tile = 2 * half
    spec = lambda t: pl.BlockSpec((length, 128), lambda g, order: (0, t * groups + g))
    pairs = groups * 2 * length * length // 2
    return pl.pallas_call(
        functools.partial(attention_forward_kernel, half=half, tile=tile),
        grid_spec=pltpu.PrefetchScalarGridSpec(
            num_scalar_prefetch=1,
            grid=(groups,),
            in_specs=[spec(0), spec(1), spec(2)],
            out_specs=pl.BlockSpec((length, 128), lambda g, order: (0, g)),
            scratch_shapes=[pltpu.VMEM((length, 128), jnp.bfloat16)] * 3,
        ),
        out_shape=jax.ShapeDtypeStruct((length, window), jnp.bfloat16),
        compiler_params=pltpu.CompilerParams(vmem_limit_bytes=VMEM_LIMIT),
        cost_estimate=pl.CostEstimate(
            flops=4 * pairs * HEAD_DIM * 4, bytes_accessed=length * window * 8, transcendentals=pairs
        ),
    )(order, qkv, qkv, qkv)


def attention_backward_kernel(
    order_ref, q_ref, k_ref, v_ref, d_ref, dq_ref, dk_ref, dv_ref, qs, ks, vs, ds, kt, dks, dvs, *, half, tile
):
    length = q_ref.shape[0]
    for p in range(length // half):
        rows = pl.ds(pl.multiple_of(order_ref[p] * half, half), half)
        here = slice(p * half, (p + 1) * half)
        qs[here, :] = q_ref[rows, :]
        ks[here, :] = k_ref[rows, :]
        vs[here, :] = v_ref[rows, :]
        ds[here, :] = d_ref[rows, :]
    kt[...] = ks[...].T
    dks[...] = jnp.zeros_like(dks)
    dvs[...] = jnp.zeros_like(dvs)
    visible = lax.broadcasted_iota(jnp.int32, (tile, tile), 0) <= lax.broadcasted_iota(
        jnp.int32, (tile, tile), 1
    )
    scale = 0.125 * LOG2E
    heads = q_ref.shape[1] // HEAD_DIM
    for i in range(length // tile):
        span = (i + 1) * tile
        outs, d_keys, d_values = [], [], []
        for h in range(heads):
            lanes = slice(h * HEAD_DIM, (h + 1) * HEAD_DIM)
            q = qs[i * tile : span, lanes]
            d_out = ds[i * tile : span, lanes]
            scores = contract_last(ks[:span, lanes], q)
            last = jnp.where(visible, scores[i * tile :, :], NEGATIVE)
            scores = jnp.concatenate([scores[: i * tile, :], last], axis=0) if i else last
            top = jnp.max(scores, axis=0, keepdims=True)
            raised = jnp.exp2(scores * scale - top * scale)
            weights = raised * (1.0 / jnp.sum(raised, axis=0, keepdims=True))
            d_weights = contract_last(vs[:span, lanes], d_out)
            row_dot = jnp.sum(weights * d_weights, axis=0, keepdims=True)
            d_scores = (weights * (d_weights - row_dot)).astype(jnp.bfloat16)
            d_values.append(
                jnp.dot(weights.astype(jnp.bfloat16), d_out, preferred_element_type=jnp.float32)
            )
            d_keys.append(jnp.dot(d_scores, q, preferred_element_type=jnp.float32))
            outs.append(
                jnp.dot(kt[lanes, :span], d_scores, preferred_element_type=jnp.float32)
            )
        dks[:span, :] += jnp.concatenate(d_keys, axis=1)
        dvs[:span, :] += jnp.concatenate(d_values, axis=1)
        merged = (jnp.concatenate(outs, axis=0) * 0.125).T.astype(dq_ref.dtype)
        for j in range(tile // half):
            rows = pl.ds(pl.multiple_of(order_ref[i * (tile // half) + j] * half, half), half)
            dq_ref[rows, :] = merged[j * half : (j + 1) * half, :]
    for p in range(length // half):
        rows = pl.ds(pl.multiple_of(order_ref[p] * half, half), half)
        here = slice(p * half, (p + 1) * half)
        dk_ref[rows, :] = (dks[here, :] * 0.125).astype(dk_ref.dtype)
        dv_ref[rows, :] = dvs[here, :].astype(dv_ref.dtype)


def attention_backward(order, qkv, d_attended, half, window):
    length = qkv.shape[0]
    groups = window // 128
    tile = 2 * half
    spec = lambda t: pl.BlockSpec((length, 128), lambda g, order: (0, t * groups + g))
    pairs = groups * 2 * length * length // 2
    return pl.pallas_call(
        functools.partial(attention_backward_kernel, half=half, tile=tile),
        grid_spec=pltpu.PrefetchScalarGridSpec(
            num_scalar_prefetch=1,
            grid=(groups,),
            in_specs=[spec(0), spec(1), spec(2), spec(0)],
            out_specs=[spec(0)] * 3,
            scratch_shapes=[pltpu.VMEM((length, 128), jnp.bfloat16)] * 4
            + [pltpu.VMEM((128, length), jnp.bfloat16)]
            + [pltpu.VMEM((length, 128), jnp.float32)] * 2,
        ),
        out_shape=[jax.ShapeDtypeStruct((length, window), jnp.bfloat16)] * 3,
        compiler_params=pltpu.CompilerParams(vmem_limit_bytes=VMEM_LIMIT),
        cost_estimate=pl.CostEstimate(
            flops=10 * pairs * HEAD_DIM * 4,
            bytes_accessed=length * window * 14,
            transcendentals=pairs,
        ),
    )(order, qkv, qkv, qkv, d_attended)


def per_device(
    tokens_in,
    block_index,
    norm_gains,
    norm_shifts,
    w_qkv,
    bias_model,
    w_out,
    w_up,
    bias_up,
    w_down,
    cotangent,
):
    seq_size, ctx_size = lax.axis_size("seq"), lax.axis_size("ctx")
    z, c = lax.axis_index("seq"), lax.axis_index("ctx")
    tok_rows, width = tokens_in.shape[1], tokens_in.shape[2]
    length = tok_rows * ctx_size
    half = length // block_index.shape[0]
    hidden = bias_up.shape[0]
    own_hidden = hidden // seq_size // ctx_size
    low = jnp.bfloat16

    plan = HeadPlan(seq_size, ctx_size, w_qkv.shape[0], width)
    window = plan.rows
    table = lambda values, *index: jnp.asarray(np.asarray(values, np.int32))[index]
    head_from = table(plan.window, c) * HEAD_DIM
    slot = jnp.arange(window, dtype=jnp.int32) // HEAD_DIM - table(plan.skip, c)
    used = (slot >= 0) & (slot < table(plan.count, c))
    order = jnp.sum(
        jnp.where(
            block_index[None, :] == jnp.arange(block_index.shape[0], dtype=jnp.int32)[:, None],
            jnp.arange(block_index.shape[0], dtype=jnp.int32)[None, :],
            0,
        ),
        axis=1,
    )

    gather_seq = lambda value: lax.all_gather(value, "seq", axis=0, tiled=True)
    qkv_pieces = gather_seq(
        lax.dynamic_slice_in_dim(w_qkv, table(plan.piece_start, z, c), window, 0)
    )
    own_qkv = jnp.concatenate(
        [
            lax.dynamic_slice_in_dim(qkv_pieces, table(plan.range_from, c, t), window, 0)
            for t in range(3)
        ]
    )
    own_out = gather_seq(
        jnp.where(used[None, :], lax.dynamic_slice_in_dim(w_out, head_from, window, 1), 0)
    )
    own_up = gather_seq(lax.dynamic_slice_in_dim(w_up, c * own_hidden, own_hidden, 0))
    split_hidden = lambda value: value.reshape(value.shape[0], seq_size, ctx_size, own_hidden)
    own_down = gather_seq(
        lax.dynamic_index_in_dim(split_hidden(w_down), c, 2, keepdims=False).reshape(
            w_down.shape[0], seq_size * own_hidden
        )
    )
    own_bias_up = lax.dynamic_index_in_dim(
        split_hidden(bias_up[None, :]), c, 2, keepdims=False
    ).reshape(-1)

    gather_ctx = lambda value: lax.all_gather(value, "ctx", axis=0, tiled=True)
    scatter_ctx = lambda value: lax.psum_scatter(
        value.astype(low), "ctx", scatter_dimension=0, tiled=True
    ).astype(jnp.float32)
    scatter_seq = lambda value: lax.psum_scatter(
        value.astype(low), "seq", scatter_dimension=0, tiled=True
    )

    tokens = tokens_in[0].astype(jnp.float32)
    normed1 = layer_norm(tokens, norm_gains[0], norm_shifts[0]).astype(low)
    all_normed1 = gather_ctx(normed1)
    own_bias = jnp.concatenate(
        [
            lax.dynamic_slice_in_dim(bias_model[0], head_from, window, 0),
            jnp.zeros((window,), jnp.float32),
            lax.dynamic_slice_in_dim(bias_model[1], head_from, window, 0),
        ]
    )
    qkv = (contract_last(all_normed1, own_qkv) + own_bias).astype(low)
    attended = attention_forward(order, qkv, half, window)
    resid = tokens + scatter_ctx(contract_last(attended, own_out)) + bias_model[2]
    normed2 = layer_norm(resid, norm_gains[1], norm_shifts[1]).astype(low)
    all_normed2 = gather_ctx(normed2)
    up_pre = contract_last(all_normed2, own_up) + own_bias_up
    act = jax.nn.gelu(up_pre, approximate=True).astype(low)
    down = scatter_ctx(contract_last(act, own_down))
    tokens_out = (resid + down + bias_model[3]).astype(low)[None]

    seq_cotangent = cotangent[0]
    all_cotangent = gather_ctx(seq_cotangent)
    cotangent_f = seq_cotangent.astype(jnp.float32)
    grad_down_bias = jnp.sum(cotangent_f, axis=0)
    grad_w_down = scatter_seq(contract_first(all_cotangent, act))
    d_act = jnp.dot(all_cotangent, own_down, preferred_element_type=jnp.float32)
    gelu_back = jax.vjp(lambda inner_up: jax.nn.gelu(inner_up, approximate=True), up_pre)[1]
    d_up = gelu_back(d_act)[0].astype(low)
    grad_up_bias = jnp.sum(d_up.astype(jnp.float32), axis=0)
    grad_w_up = scatter_seq(contract_first(d_up, all_normed2))
    d_normed2 = scatter_ctx(jnp.dot(d_up, own_up, preferred_element_type=jnp.float32))
    norm_back2 = jax.vjp(layer_norm, resid, norm_gains[1], norm_shifts[1])[1]
    d_resid_norm, grad_gain2, grad_shift2 = norm_back2(d_normed2)
    d_resid = cotangent_f + d_resid_norm
    d_branch = d_resid.astype(low)
    grad_out_bias = jnp.sum(d_branch.astype(jnp.float32), axis=0)
    all_branch = gather_ctx(d_branch)
    grad_w_out = scatter_seq(contract_first(all_branch, attended))
    d_attended = jnp.dot(all_branch, own_out, preferred_element_type=jnp.float32).astype(low)
    d_qkv = jnp.concatenate(attention_backward(order, qkv, d_attended, half, window), axis=1)
    sums = jnp.sum(d_qkv.astype(jnp.float32), axis=0)
    place = lambda part: lax.dynamic_update_slice(
        jnp.zeros((width,), jnp.float32), part, (head_from,)
    )
    grad_query_bias, grad_value_bias = place(sums[:window]), place(sums[2 * window :])
    part = contract_first(d_qkv, all_normed1).astype(low)
    part = jnp.pad(part, ((window, window), (0, 0)))
    grad_w_qkv = scatter_seq(
        jnp.concatenate(
            [
                lax.dynamic_slice_in_dim(part, table(plan.piece_from, c, s), window, 0)
                for s in range(seq_size)
            ]
        )
    )
    d_normed1 = scatter_ctx(jnp.dot(d_qkv, own_qkv, preferred_element_type=jnp.float32))
    norm_back1 = jax.vjp(layer_norm, tokens, norm_gains[0], norm_shifts[0])[1]
    d_tokens_norm, grad_gain1, grad_shift1 = norm_back1(d_normed1)
    grad_tokens = (d_resid + d_tokens_norm)[None]

    grad_w_up = gather_ctx(grad_w_up).astype(jnp.float32)
    gathered = lax.all_gather(grad_w_down, "ctx", axis=0)
    gathered = gathered.reshape(ctx_size, w_down.shape[0], seq_size, own_hidden)
    grad_w_down = (
        jnp.transpose(gathered, (1, 2, 0, 3)).reshape(w_down.shape).astype(jnp.float32)
    )
    gathered = lax.all_gather(grad_w_out, "ctx", axis=0)
    grad_w_out = jnp.concatenate(
        [
            gathered[i][
                :, plan.skip[i] * HEAD_DIM : (plan.skip[i] + plan.count[i]) * HEAD_DIM
            ]
            for i in range(ctx_size)
        ],
        axis=1,
    ).astype(jnp.float32)
    gathered = gather_ctx(grad_w_qkv)
    grain = math.gcd(w_qkv.shape[0], HEAD_DIM)
    groups = table(plan.source_row[:, ::grain] // grain, z)
    grad_w_qkv = (
        jnp.take(gathered.reshape(-1, grain, width), groups, axis=0)
        .reshape(w_qkv.shape)
        .astype(jnp.float32)
    )

    spread_up = jnp.zeros((seq_size, ctx_size, own_hidden), jnp.float32)
    grad_up_bias = lax.dynamic_update_slice(
        spread_up, grad_up_bias.reshape(seq_size, 1, own_hidden), (0, c, 0)
    ).reshape(-1)
    small = jnp.concatenate(
        [
            grad_gain1,
            grad_gain2,
            grad_shift1,
            grad_shift2,
            grad_query_bias,
            grad_value_bias,
            grad_out_bias,
            grad_down_bias,
            grad_up_bias,
        ]
    )
    small = lax.psum(small, ("seq", "ctx"))
    return (
        tokens_out,
        grad_tokens,
        small[: 2 * width].reshape(2, width),
        small[2 * width : 4 * width].reshape(2, width),
        grad_w_qkv,
        small[4 * width : 8 * width].reshape(4, width),
        grad_w_out,
        grad_w_up,
        small[8 * width :],
        grad_w_down,
    )


def solution(mesh):
    placed = (
        P("seq", "ctx", None),
        P(),
        P(),
        P(),
        P("seq", None),
        P(),
        P("seq", None),
        P("seq", None),
        P(),
        P("seq", None),
        P("seq", "ctx", None),
    )
    return jax.shard_map(
        per_device,
        mesh=mesh,
        in_specs=placed,
        out_specs=(
            P("seq", "ctx", None),
            P("seq", "ctx", None),
            P(),
            P(),
            P("seq", None),
            P(),
            P("seq", None),
            P("seq", None),
            P(),
            P("seq", None),
        ),
        check_vma=False,
    )
```

time: 2960 us -> 1280 us (0.43)
  waiting for transfers between devices: 2420 us -> 823 us
  matrix products: 295 us -> 117 us
  other arithmetic: 128 us -> 45.5 us
  local copies, waits for them, and re-layouts: 66.1 us -> 146 us
  Pallas kernels: 0 us -> 75.5 us
  blocking collectives: 0 us -> 32.8 us
    all_gather x6 -> x11, waiting for transfers between devices: 1070 us -> 368 us  [the longest x6 210 us: per_device(): gather_ctx = lambda value: lax.all_gather(value, 'ctx', axis=0, tiled=True)]
    reduce_scatter x3 -> x7, waiting for transfers between devices: 701 us -> 318 us  [the longest x4 231 us: per_device(): lax.psum_scatter(value.astype(low), 'ctx', scatter_dimension=0, tiled=True)]
    unnamed x13 -> x21, waiting for transfers between devices: 241 us -> 17.3 us
    dot_general x56 -> x8, matrix products: 249 us -> 77.7 us  [the longest x4 37.6 us: contract_first(): lax.dot_general(left, right, (((0,), (0,)), ((), ())), preferred_element_...]
    psum x2 -> x1, waiting for transfers between devices: 287 us -> 120 us  [per_device(): small = lax.psum(small, ('seq', 'ctx'))]
    ppermute x32 -> x0, waiting for transfers between devices: 121 us -> none  [shifted(): lax.ppermute(value, axis, [(i, (i + by) % count) for i in range(count)])]
    pallas_call x0 -> x2, Pallas kernels: none -> 75.5 us  [the longest x1 48.1 us: attention_backward(): pl.pallas_call(functools.partial(attention_backward_kernel, half=half, ti...]
    convert_element_type x38 -> x5, other arithmetic: 79.3 us -> 19.5 us  [the longest x1 7.34 us: per_device(): grad_w_up = gather_ctx(grad_w_up).astype(jnp.float32)]
  transfers between devices with their start and end apart: 44 -> 20, of which waited for: 27 -> 18; matrix products, arithmetic and copies ran while one was open for 14% -> 19% of each run, Pallas kernels for 0% -> 4%
where the time goes in v1:
time: 1280 us; the launch traced here: 1270 us
  waiting for transfers between devices  823 us (64%)
  local copies, waits for them, and re-layouts  146 us (11%)
  matrix products  117 us (9%)
  Pallas kernels  75.5 us (6%)
  other arithmetic  45.5 us (4%)
  blocking collectives  32.8 us (3%)
  between operations  30.2 us (2%)
    reduce_scatter x4, waiting for transfers between devices, per_device(): lax.psum_scatter(value.astype(low), 'ctx', scatter_dimension=0, tiled=True)  231 us
    all_gather x6, waiting for transfers between devices, per_device(): gather_ctx = lambda value: lax.all_gather(value, 'ctx', axis=0, tiled=True)  210 us
    psum x1, waiting for transfers between devices, per_device(): small = lax.psum(small, ('seq', 'ctx'))  120 us
    all_gather x3, waiting for transfers between devices, per_device(): gather_seq = lambda value: lax.all_gather(value, 'seq', axis=0, tiled=True)  106 us
    reduce_scatter x3, waiting for transfers between devices, per_device(): lax.psum_scatter(value.astype(low), 'seq', scatter_dimension=0, tiled=True)  87 us
    convert_element_type x3, local copies, waits for them, and re-layouts, per_device(): jnp.transpose(gathered, (1, 2, 0, 3)).reshape(w_down.shape)  49.1 us
    pallas_call x1, Pallas kernels, attention_backward(): pl.pallas_call(functools.partial(attention_backward_kernel, half=half, ti...  48.1 us
    all_gather x1, waiting for transfers between devices, per_device(): gathered = lax.all_gather(grad_w_down, 'ctx', axis=0)  44.9 us
  transfers between devices with their start and end apart: 20, of which 18 were waited for; matrix products, arithmetic and copies ran while one was open for 19% of the time, Pallas kernels for 4%

profile of v1, /device:TPU:0, one launch (start us, length us, event | category | flops | bytes accessed | tf_op | source)
XLA Modules:
  0.0 1270.2 jit_solution(7424233713111601673)
XLA Ops:
  10.6 2.1 constant_dynamic-slice_fusion.10
  27.6 32.8 %all_gather.44 = bf16[1600,256]{1,0:T(8,128)(2,1)S(1)} all-gather(bf16[400,256]{1,0:T(8,128)(2,1)S(1)} %dynamic-slice_select_fusion), channel_id=1, replica_groups=mesh['seq'=4,'ctx'=8] {'seq'}, dimensions={0}, use_global_device_ids=true | all-gather | bytes 1024000 | tf_op jit(solution)/shard_map/all_gather | solution.py:246
  60.4 36.0 %all-gather.17.cloned.1.call-done = bf16[1024,1600]{1,0:T(8,128)(2,1)} async-done(((bf16[256,1600]{1,0:T(8,128)(2,1)}), bf16[1024,1600]{1,0:T(8,128)(2,1)}) %all-gather.17.cloned.1.call-update) | async-done | bytes 3276816 | tf_op jit(solution)/shard_map/all_gather | solution.py:246
  96.4 2.8 constant_dynamic-slice_fusion.8
  99.2 46.2 %all-gather.15.cloned.1.call-done = bf16[2048,1600]{0,1:T(8,128)(2,1)} async-done(((bf16[256,1600]{0,1:T(8,128)(2,1)}), bf16[2048,1600]{0,1:T(8,128)(2,1)}) %all-gather.15.cloned.1.call-update) | async-done | bytes 6553616 | tf_op jit(solution)/shard_map/all_gather | solution.py:270
  145.4 9.5 add_convert_fusion.q_ref.k_ref.v_ref
  154.9 27.3 %shard_map.249 = bf16[2048,256]{1,0:T(8,128)(2,1)} custom-call(s32[16]{0:T(128)} %select_reduce_fusion.order_ref, bf16[2048,768]{1,0:T(8,128)(2,1)} %add_convert_fusion.q_ref.k_ref.v_ref, bf16[2048,768]{1,0:T(8,128)(2,1)} %add_convert_fusion.q_ref.k_ref.v_ref, bf16[2048,768]{1,0:T(8,128)(2,1)} %add_convert_fusion.q_ref.k_ref.v_ref), custom_call_target="tpu_custom_call" | custom-call | flops 8589934592 | bytes 4194304 | tf_op jit(solution)/shard_map/pallas_call | solution.py:110
  182.3 5.9 convolution_convert_fusion.2
  188.3 2.0 constant_dynamic-slice_fusion.3
  190.3 61.0 %reduce-scatter.13.cloned.1.call-done = bf16[256,1600]{0,1:T(8,128)(2,1)} async-done(((bf16[2048,1600]{0,1:T(8,128)(2,1)}), bf16[256,1600]{0,1:T(8,128)(2,1)}) %reduce-scatter.13.cloned.1.call-update) | async-done | bytes 819216 | tf_op jit(solution)/shard_map/reduce_scatter | solution.py:271
  254.4 1.8 add_convert_fusion.2
  256.4 21.4 %reshape.198 = bf16[400,4,8,200]{3,2,1,0:T(8,128)(2,1)} reshape(bf16[400,6400]{1,0:T(8,128)(2,1)} %param.27) | data formatting | bytes 10240000 | tf_op jit(solution)/shard_map/reshape | solution.py:260
  277.7 8.4 dynamic-slice_reduce_fusion
  288.7 20.3 %all-gather.21.cloned.1.call-done = bf16[800,1600]{1,0:T(8,128)(2,1)} async-done(((bf16[200,1600]{1,0:T(8,128)(2,1)}), bf16[800,1600]{1,0:T(8,128)(2,1)}) %all-gather.21.cloned.1.call-update) | async-done | bytes 2560016 | tf_op jit(solution)/shard_map/all_gather | solution.py:246
  308.9 49.1 %all-gather.19.cloned.1.call-done = bf16[2048,1600]{0,1:T(8,128)(2,1)} async-done(((bf16[256,1600]{0,1:T(8,128)(2,1)}), bf16[2048,1600]{0,1:T(8,128)(2,1)}) %all-gather.19.cloned.1.call-update) | async-done | bytes 6553616 | tf_op jit(solution)/shard_map/all_gather | solution.py:270
  358.0 10.9 fusion.58
  368.9 50.1 %all-gather.23.cloned.1.call-done = bf16[1600,800]{1,0:T(8,128)(2,1)} async-done(((bf16[400,800]{1,0:T(8,128)(2,1)}), bf16[1600,800]{1,0:T(8,128)(2,1)}) %all-gather.23.cloned.1.call-update) | async-done | bytes 2560016 | tf_op jit(solution)/shard_map/all_gather | solution.py:246
  419.0 48.6 %all-gather.31.cloned.1.call-done = bf16[1,2048,1600]{1,2,0:T(8,128)(2,1)} async-done(((bf16[1,256,1600]{1,2,0:T(8,128)(2,1)}), bf16[1,2048,1600]{1,2,0:T(8,128)(2,1)}) %all-gather.31.cloned.1.call-update) | async-done | bytes 6553616 | tf_op jit(solution)/shard_map/all_gather | solution.py:270
  467.6 14.9 %convert_reduce_fusion = (f32[800]{0:T(1024)S(1)}, bf16[2048,800]{0,1:T(8,128)(2,1)S(1)}) fusion(f32[2048,800]{0,1:T(8,128)} %fusion.58, f32[800]{0:T(1024)S(1)} %add.225, bf16[1600,800]{1,0:T(8,128)(2,1)} %all-gather.23.cloned.1.call-done, bf16[1,2048,1600]{1,2,0:T(8,128)(2,1)} %all-gather.31.cloned.1.call-done), kind=kOutput, calls=%fused_computation.23 | convolution fusion | flops 5280562176 | bytes 18950400 | tf_op jit(solution)/shard_map/dot_general | solution.py:303
  482.5 1.7 copy-done.27
  484.2 9.0 convolution_convert_fusion.3
  493.8 62.6 %reduce-scatter.17.cloned.1.call-done = bf16[256,1600]{0,1:T(8,128)(2,1)} async-done(((bf16[2048,1600]{0,1:T(8,128)(2,1)}), bf16[256,1600]{0,1:T(8,128)(2,1)}) %reduce-scatter.17.cloned.1.call-update) | async-done | bytes 819216 | tf_op jit(solution)/shard_map/reduce_scatter | solution.py:271
  556.4 2.1 convert_reduce_fusion.3
  558.5 2.4 fusion.38
  560.9 1.8 convert_reduce_fusion.6
  562.8 12.8 %fusion.18 = bf16[1600,800]{0,1:T(8,128)(2,1)} fusion(bf16[1,2048,1600]{1,2,0:T(8,128)(2,1)} %all-gather.31.cloned.1.call-done, f32[2048,800]{0,1:T(8,128)} %fusion.58, f32[800]{0:T(1024)S(1)} %add.225), kind=kOutput, calls=%fused_computation.37 | convolution fusion | flops 5260544000 | bytes 15670400 | tf_op jit(solution)/shard_map/dot_general | solution.py:33
  575.5 5.2 copy.56
  580.8 10.8 convolution_convert_fusion.4
  591.7 19.0 %all-gather.25.cloned.1.call-done = bf16[2048,1600]{0,1:T(8,128)(2,1)} async-done(((bf16[256,1600]{0,1:T(8,128)(2,1)}), bf16[2048,1600]{0,1:T(8,128)(2,1)}) %all-gather.25.cloned.1.call-update) | async-done | bytes 6553616 | tf_op jit(solution)/shard_map/all_gather | solution.py:270
  610.7 6.1 convolution_convert_fusion.7.d_ref
  616.8 48.1 %shard_map.250 = (bf16[2048,256]{1,0:T(8,128)(2,1)}, bf16[2048,256]{1,0:T(8,128)(2,1)}, bf16[2048,256]{1,0:T(8,128)(2,1)}) custom-call(s32[16]{0:T(128)} %select_reduce_fusion.order_ref, bf16[2048,768]{1,0:T(8,128)(2,1)} %add_convert_fusion.q_ref.k_ref.v_ref, bf16[2048,768]{1,0:T(8,128)(2,1)} %add_convert_fusion.q_ref.k_ref.v_ref, ...), custom_call_target="tpu_custom_call" | custom-call | flops 21474836480 | bytes 7340032 | tf_op jit(solution)/shard_map/pallas_call | solution.py:188
  665.0 2.3 constant_dynamic-update-slice_fusion.2
  667.3 5.7 convolution_convert_fusion.6
  673.1 2.5 constant_dynamic-update-slice_fusion.1
  675.6 2.4 constant_dynamic-update-slice_fusion
  678.0 10.1 convolution_convert_fusion.1
  695.5 8.3 convolution_convert_fusion.5
  703.9 1.8 pad_dynamic-slice_fusion.3
  705.7 2.0 pad_maximum_fusion
  708.3 15.8 %reduce-scatter.27.cloned.1.call-done = bf16[200,1600]{1,0:T(8,128)(2,1)} async-done(((bf16[800,1600]{1,0:T(8,128)(2,1)}), bf16[200,1600]{1,0:T(8,128)(2,1)}) %reduce-scatter.27.cloned.1.call-update) | async-done | bytes 640016
  724.2 26.6 %reduce-scatter.23.cloned.1.call-done = bf16[400,256]{1,0:T(8,128)(2,1)} async-done(((bf16[1600,256]{1,0:T(8,128)(2,1)}), bf16[400,256]{1,0:T(8,128)(2,1)}) %reduce-scatter.23.cloned.1.call-update) | async-done | bytes 204816 | tf_op jit(solution)/shard_map/reduce_scatter | solution.py:274
  750.8 12.9 %convolution_convert_fusion = bf16[2048,1600]{0,1:T(8,128)(2,1)} fusion(bf16[1600,800]{1,0:T(8,128)(2,1)} %all-gather.23.cloned.1.call-done, f32[2048,800]{0,1:T(8,128)} %fusion.58, f32[800]{0:T(1024)S(1)} %add.225), kind=kOutput, calls=%fused_computation.3 | convolution fusion | flops 5262540800 | bytes 15670400 | tf_op jit(solution)/shard_map/dot_general | solution.py:27
  764.4 2.9 convert_reduce_fusion.1
  767.5 49.6 %reduce-scatter.19.cloned.1.call-done = bf16[256,1600]{0,1:T(8,128)(2,1)} async-done(((bf16[2048,1600]{0,1:T(8,128)(2,1)}), bf16[256,1600]{0,1:T(8,128)(2,1)}) %reduce-scatter.19.cloned.1.call-update) | async-done | bytes 819216 | tf_op jit(solution)/shard_map/reduce_scatter | solution.py:271
  817.1 1.9 convert_reduce_fusion.2
  819.0 2.1 fusion.39
  821.9 60.4 %reduce-scatter.21.cloned.1.call-done = bf16[256,1600]{0,1:T(8,128)(2,1)} async-done(((bf16[1024,1600]{0,1:T(8,128)(2,1)}), bf16[256,1600]{0,1:T(8,128)(2,1)}) %reduce-scatter.21.cloned.1.call-update) | async-done | bytes 819216 | tf_op jit(solution)/shard_map/reduce_scatter | solution.py:274
  882.6 44.9 %all-gather.35.cloned.1.call-done = bf16[3200,800]{1,0:T(8,128)(2,1)} async-done(((bf16[400,800]{1,0:T(8,128)(2,1)}), bf16[3200,800]{1,0:T(8,128)(2,1)}) %all-gather.35.cloned.1.call-update) | async-done | bytes 5120016 | tf_op jit(solution)/shard_map/all_gather | solution.py:339
  927.5 8.7 copy.54
  936.2 17.2 %reshape.211 = f32[8,400,4,200]{1,0,3,2:T(8,128)} reshape(bf16[3200,800]{0,1:T(8,128)(2,1)} %copy.54) | data formatting | bytes 15360000 | tf_op jit(solution)/shard_map/convert_element_type | solution.py:342
  953.4 17.9 %copy.55 = f32[400,4,8,200]{3,2,1,0:T(8,128)} copy(f32[400,4,8,200]{0,2,3,1:T(8,128)} %bitcast.147) | data formatting | bytes 20480000 | tf_op jit(solution)/shard_map/convert_element_type | solution.py:342
  971.3 14.0 %reshape.209 = f32[400,6400]{1,0:T(8,128)} reshape(f32[400,4,8,200]{3,2,1,0:T(8,128)} %copy.55) | data formatting | bytes 20480000 | tf_op jit(solution)/shard_map/convert_element_type | solution.py:342
  985.3 7.3 convert_element_type.133
  992.7 6.1 all-gather.33.cloned.1.call-done
  998.8 2.6 fusion.55
  1001.3 3.6 concatenate.23
  1004.9 3.0 convert_element_type.131
  1007.9 57.6 %reduce-scatter.15.cloned.1.call-done = bf16[256,1600]{0,1:T(8,128)(2,1)} async-done(((bf16[2048,1600]{0,1:T(8,128)(2,1)}), bf16[256,1600]{0,1:T(8,128)(2,1)}) %reduce-scatter.15.cloned.1.call-update) | async-done | bytes 819216 | tf_op jit(solution)/shard_map/reduce_scatter | solution.py:271
  1065.5 4.5 add_bitcast_fusion
  1070.0 120.0 %all-reduce.4.cloned.1.call-done = f32[19200]{0:T(1024)} async-done(((f32[19200]{0:T(1024)}), f32[19200]{0:T(1024)}) %all-reduce.4.cloned.1.call-update) | async-done | bytes 76816 | tf_op jit(solution)/shard_map/psum | solution.py:380
  1194.3 47.2 %all-gather.27.cloned.1.call-done = bf16[2048,1600]{0,1:T(8,128)(2,1)} async-done(((bf16[256,1600]{0,1:T(8,128)(2,1)}), bf16[2048,1600]{0,1:T(8,128)(2,1)}) %all-gather.27.cloned.1.call-update) | async-done | bytes 6553616 | tf_op jit(solution)/shard_map/all_gather | solution.py:270
  1241.5 9.5 copy.52
  1251.0 6.2 gather_fusion
  1257.2 6.0 fusion.14
  (148 shorter events, 23.8 us)
Async XLA Ops:
  7.2 7.3 copy-start
  7.2 89.3 %all-gather.17.cloned.1.call-start = ((), (), s32[]{:S(2)}) async-start(), calls=%async_computation.9 | async-start | bytes 4259840 | tf_op jit(solution)/shard_map/all_gather | solution.py:246
  10.5 6.0 copy-start.22
  10.5 11.3 copy-start.26
  10.5 14.5 %copy-start.17 = (f32[4,1600]{1,0:T(4,128)S(1)}, f32[4,1600]{1,0:T(4,128)}, u32[]{:S(2)}) copy-start(f32[4,1600]{1,0:T(4,128)} %param.23) | copy-start | bytes 76804
  10.6 15.2 %copy-start.24 = (s32[16]{0:T(128)S(1)}, s32[16]{0:T(128)}, u32[]{:S(2)}) copy-start(s32[16]{0:T(128)} %param.19) | copy-start | bytes 196
  12.7 132.7 %all-gather.15.cloned.1.call-start = ((), (), s32[]{:S(2)}) async-start(), calls=%async_computation.8 | async-start | bytes 7372800 | tf_op jit(solution)/shard_map/all_gather | solution.py:270
  13.6 12.9 %copy-start.11 = (f32[1600]{0:T(1024)}, f32[1600]{0:T(1024)S(1)}, u32[]{:S(2)}) copy-start(f32[1600]{0:T(1024)S(1)} %get-tuple-element.26) | copy-start | bytes 19204
  14.7 11.8 copy-start.13
  15.0 11.5 copy-start.20
  15.0 11.5 copy-start.18
  16.4 234.9 %reduce-scatter.13.cloned.1.call-start = ((), (), s32[]{:S(2)}) async-start(), calls=%async_computation.10 | async-start | bytes 7372800 | tf_op jit(solution)/shard_map/reduce_scatter | solution.py:271
  60.4 121.8 %copy-start.4 = (bf16[1600,256]{1,0:T(8,128)(2,1)}, bf16[1600,256]{1,0:T(8,128)(2,1)S(1)}, u32[]{:S(2)}) copy-start(bf16[1600,256]{1,0:T(8,128)(2,1)S(1)} %all_gather.44) | copy-start | bytes 2457604
  99.2 55.7 %copy-start.6 = (bf16[256,1600]{1,0:T(8,128)(2,1)}, bf16[256,1600]{1,0:T(8,128)(2,1)S(1)}, u32[]{:S(2)}) copy-start(bf16[256,1600]{1,0:T(8,128)(2,1)S(1)} %get-tuple-element.32) | copy-start | bytes 2457604
  99.2 55.7 %copy-start.8 = (bf16[256,1600]{1,0:T(8,128)(2,1)}, bf16[256,1600]{1,0:T(8,128)(2,1)S(1)}, u32[]{:S(2)}) copy-start(bf16[256,1600]{1,0:T(8,128)(2,1)S(1)} %get-tuple-element.33) | copy-start | bytes 2457604
  188.2 120.7 %all-gather.21.cloned.1.call-start = ((), (), s32[]{:S(2)}) async-start(), calls=%async_computation.12 | async-start | bytes 3328000 | tf_op jit(solution)/shard_map/all_gather | solution.py:246
  190.3 167.7 %all-gather.19.cloned.1.call-start = ((), (), s32[]{:S(2)}) async-start(), calls=%async_computation.11 | async-start | bytes 7372800 | tf_op jit(solution)/shard_map/all_gather | solution.py:270
  251.3 3.1 copy-start.1
  256.3 162.7 %all-gather.23.cloned.1.call-start = ((), (), s32[]{:S(2)}) async-start(), calls=%async_computation.13 | async-start | bytes 3584000 | tf_op jit(solution)/shard_map/all_gather | solution.py:246
  277.7 10.7 copy-start.16
  287.6 180.0 %all-gather.31.cloned.1.call-start = ((), (), s32[]{:S(2)}) async-start(), calls=%async_computation.23 | async-start | bytes 7372800 | tf_op jit(solution)/shard_map/all_gather | solution.py:270
  288.4 268.0 %reduce-scatter.17.cloned.1.call-start = ((), (), s32[]{:S(2)}) async-start(), calls=%async_computation.15 | async-start | bytes 7372800 | tf_op jit(solution)/shard_map/reduce_scatter | solution.py:271
  467.6 16.6 %copy-start.23 = (bf16[800,1600]{1,0:T(8,128)(2,1)S(1)}, bf16[800,1600]{1,0:T(8,128)(2,1)}, u32[]{:S(2)}) copy-start(bf16[800,1600]{1,0:T(8,128)(2,1)} %all-gather.21.cloned.1.call-done) | copy-start | bytes 7680004
  482.5 1.7 copy-start.27
  493.3 67.6 %copy-start.2 = (bf16[1,256,1600]{1,2,0:T(8,128)(2,1)S(1)}, bf16[1,256,1600]{1,2,0:T(8,128)(2,1)}, u32[]{:S(2)}) copy-start(bf16[1,256,1600]{1,2,0:T(8,128)(2,1)} %param.28) | copy-start | bytes 2457604
  493.3 117.4 %all-gather.25.cloned.1.call-start = ((), (), s32[]{:S(2)}) async-start(), calls=%async_computation.16 | async-start | bytes 7372800 | tf_op jit(solution)/shard_map/all_gather | solution.py:270
  556.4 4.5 copy-start.3
  562.7 145.1 %reduce-scatter.25.cloned.1.call-start = ((), (), s32[]{:S(2)}) async-start(), calls=%async_computation.26 | async-start | bytes 3584000 | tf_op jit(solution)/shard_map/reduce_scatter | solution.py:274
  580.8 143.4 %reduce-scatter.27.cloned.1.call-start = ((), (), s32[]{:S(2)}) async-start(), calls=%async_computation.27 | async-start | bytes 3328000
  591.6 159.1 %reduce-scatter.23.cloned.1.call-start = ((), (), s32[]{:S(2)}) async-start(), calls=%async_computation.21 | async-start | bytes 1024000 | tf_op jit(solution)/shard_map/reduce_scatter | solution.py:274
  616.8 50.5 %copy-start.5 = (bf16[2048,256]{1,0:T(8,128)(2,1)S(1)}, bf16[2048,256]{1,0:T(8,128)(2,1)}, u32[]{:S(2)}) copy-start(bf16[2048,256]{1,0:T(8,128)(2,1)} %shard_map.249) | copy-start | bytes 3145732
  673.0 144.1 %reduce-scatter.19.cloned.1.call-start = ((), (), s32[]{:S(2)}) async-start(), calls=%async_computation.17 | async-start | bytes 7372800 | tf_op jit(solution)/shard_map/reduce_scatter | solution.py:271
  673.1 4.9 copy-start.7
  673.1 4.9 copy-start.9
  673.1 4.9 copy-start.10
  688.2 194.1 %reduce-scatter.21.cloned.1.call-start = ((), (), s32[]{:S(2)}) async-start(), calls=%async_computation.19 | async-start | bytes 4096000 | tf_op jit(solution)/shard_map/reduce_scatter | solution.py:274
  707.7 219.8 %all-gather.35.cloned.1.call-start = ((), (), s32[]{:S(2)}) async-start(), calls=%async_computation.25 | async-start | bytes 6451200 | tf_op jit(solution)/shard_map/all_gather | solution.py:339
  708.3 277.1 %all-gather.29.cloned.1.call-start = ((), (), s32[]{:S(2)}) async-start(), calls=%async_computation.22 | async-start | bytes 5990400 | tf_op jit(solution)/shard_map/all_gather | solution.py:270
  724.2 274.6 %all-gather.33.cloned.1.call-start = ((), (), s32[]{:S(2)}) async-start(), calls=%async_computation.24 | async-start | bytes 1843200 | tf_op jit(solution)/shard_map/all_gather | solution.py:344
  750.8 314.7 %reduce-scatter.15.cloned.1.call-start = ((), (), s32[]{:S(2)}) async-start(), calls=%async_computation.14 | async-start | bytes 7372800 | tf_op jit(solution)/shard_map/reduce_scatter | solution.py:271
  763.7 53.4 %copy-start.12 = (f32[1600]{0:T(1024)S(1)}, f32[1600]{0:T(1024)}, u32[]{:S(2)}) copy-start(f32[1600]{0:T(1024)} %copy-done.11) | copy-start | bytes 19204
  763.7 53.4 %copy-start.14 = (f32[256]{0:T(256)S(1)}, f32[256]{0:T(256)}, u32[]{:S(2)}) copy-start(f32[256]{0:T(256)} %copy-done.13) | copy-start | bytes 3076
  763.8 55.2 %copy-start.21 = (f32[256]{0:T(256)S(1)}, f32[256]{0:T(256)}, u32[]{:S(2)}) copy-start(f32[256]{0:T(256)} %copy-done.20) | copy-start | bytes 3076
  763.8 55.2 %copy-start.19 = (f32[256]{0:T(256)S(1)}, f32[256]{0:T(256)}, u32[]{:S(2)}) copy-start(f32[256]{0:T(256)} %copy-done.18) | copy-start | bytes 3076
  763.8 426.2 %all-reduce.4.cloned.1.call-start = ((), (), s32[]{:S(2)}) async-start(), calls=%async_computation.18 | async-start | bytes 155648 | tf_op jit(solution)/shard_map/psum | solution.py:380
  764.4 117.9 %copy-start.25 = (s32[4,75]{1,0:T(4,128)S(1)}, s32[4,75]{1,0:T(4,128)}, u32[]{:S(2)}) copy-start(s32[4,75]{1,0:T(4,128)} %constant.128.clone) | copy-start | bytes 3604
  821.9 419.6 %all-gather.27.cloned.1.call-start = ((), (), s32[]{:S(2)}) async-start(), calls=%async_computation.20 | async-start | bytes 7372800 | tf_op jit(solution)/shard_map/all_gather | solution.py:270
  998.8 2.6 slice-start
  1001.3 64.2 %copy-start.15 = (f32[1600]{0:T(1024)S(1)}, f32[1600]{0:T(1024)}, u32[]{:S(2)}) copy-start(f32[1600]{0:T(1024)} %get-tuple-element.24) | copy-start | bytes 19204
Sparse Core Ops, SparseCore 0:
  12.8 83.5 all-gather.16
  98.9 46.4 all-gather.14
  188.3 62.9 reduce-scatter.12
  253.4 55.4 all-gather.20
  311.4 46.5 all-gather.18
  360.1 58.9 all-gather.22
  421.1 46.5 all-gather.30
  493.4 62.9 reduce-scatter.16
  562.8 47.8 all-gather.24
  612.8 56.0 reduce-scatter.24
  671.8 52.2 reduce-scatter.26
  726.9 23.8 reduce-scatter.22
  754.8 62.2 reduce-scatter.18
  820.0 62.2 reduce-scatter.20
  884.2 43.2 all-gather.34
  929.4 41.4 all-gather.28
  972.8 25.9 all-gather.32
  1002.5 63.0 reduce-scatter.14
  1071.1 118.8 all-reduce.3
  1191.7 49.7 all-gather.26

commit v2 on v1

v2 whole, which is shorter than its diff:
```python
import functools
import math

import jax
import jax.numpy as jnp
import numpy as np
from jax import lax
from jax.experimental import pallas as pl
from jax.experimental.pallas import tpu as pltpu
from jax.sharding import PartitionSpec as P

HEADS = 25
HEAD_DIM = 64
LOG2E = 1.4426950408889634
NEGATIVE = -1e30
VMEM_LIMIT = 56 * 1024 * 1024


def contract_last(left, right):
    return lax.dot_general(
        left, right, (((1,), (1,)), ((), ())), preferred_element_type=jnp.float32
    )


def contract_first(left, right):
    return lax.dot_general(
        left, right, (((0,), (0,)), ((), ())), preferred_element_type=jnp.float32
    )


class HeadPlan:
    def __init__(self, seq_size, ctx_size, shard_rows, width, plane, below):
        first = [HEADS * c // ctx_size for c in range(ctx_size + 1)]
        self.count = [first[c + 1] - first[c] for c in range(ctx_size)]
        self.groups = (max(self.count) + 1) // 2
        self.window = [min(first[c], HEADS - 2 * self.groups) for c in range(ctx_size)]
        self.skip = [first[c] - self.window[c] for c in range(ctx_size)]
        self.rows = rows = 2 * HEAD_DIM
        self.grain = grain = math.gcd(shard_rows, HEAD_DIM)
        self.piece_start = np.zeros((self.groups, seq_size, ctx_size), np.int32)
        self.range_from = np.zeros((self.groups, ctx_size, 3), np.int32)
        self.piece_from = np.zeros((self.groups, ctx_size, seq_size), np.int32)
        owner = np.zeros((seq_size, shard_rows // grain, 3), np.int32)
        for c in range(ctx_size):
            for t in range(3):
                for g in range(self.groups):
                    begin = t * width + (self.window[c] + 2 * g) * HEAD_DIM
                    for z in range(seq_size):
                        low, high = z * shard_rows, (z + 1) * shard_rows
                        if begin + rows <= low or begin >= high:
                            continue
                        start = min(max(begin, low), high - rows)
                        self.piece_start[g, z, c] = start - low
                        self.piece_from[g, c, z] = rows + t * rows + start - begin
                        if low <= begin < high:
                            self.range_from[g, c, t] = z * rows + begin - start
                for head in range(first[c], first[c + 1]):
                    g = (head - self.window[c]) // 2
                    for row in range(t * width + head * HEAD_DIM, t * width + (head + 1) * HEAD_DIM, grain):
                        z = row // shard_rows
                        inside = row - z * shard_rows
                        owner[z, inside // grain] = g, c, inside - self.piece_start[g, z, c]
        self.source = np.zeros((seq_size, ctx_size, shard_rows // grain), np.int32)
        for c in range(ctx_size):
            for z in range(seq_size):
                for block in range(shard_rows // grain):
                    g, other, inside = owner[z, block]
                    stride = rows + (0 if g else below)
                    place = g * ctx_size * (rows + below) + plane.place(other ^ c) * stride + inside
                    self.source[z, c, block] = place // grain


def after(value, *others):
    one = jnp.float32(1.0)
    for other in others:
        sign = jnp.where(other[(0,) * other.ndim] > 0, jnp.float32(1.0), jnp.float32(-1.0))
        one = one * (sign * sign)
    return value * one.astype(value.dtype)


class Plane:
    def __init__(self, size):
        self.size = size
        self.even = list(range(0, size, 2))
        self.slots = self.even + [s + 1 for s in self.even]

    def place(self, slot):
        return self.slots.index(slot)

    def move(self, value, bits):
        return lax.ppermute(value, "ctx", [(i, i ^ bits) for i in range(self.size)])

    def send(self, value):
        if len(self.even) != 4:
            return [value] + [self.move(value, s) for s in self.even[1:]]
        half = value.shape[0] // 2
        first, second = self.move(value, 2), self.move(value, 4)
        return [value, first, second, self.move(first[:half], 4), self.move(second[half:], 2)]

    def share(self, near, order=()):
        last = held(near[-1:], order) if order else near[-1:]
        return near + [self.move(piece, 1) for piece in near[:-1] + last]

    def gather(self, value):
        return self.share(self.send(value))

    def other_half(self, lefts, rights, transposed, order=()):
        return product_rows(lefts, rights, transposed, len(self.even), [], order)

    def halves(self, lefts, rights, transposed, sent, order=()):
        sent = [self.move(part, 1) for part in sent]
        return product_rows(lefts, rights, transposed, len(self.even), sent, order)

    def exchange(self, parts):
        return [parts[0]] + [self.move(parts[i], s) for i, s in enumerate(self.even) if s]

    def scatter(self, lefts, rights, transposed, sent):
        return self.exchange(self.halves(lefts, rights, transposed, sent))


def total_by_bits(value, axis, size):
    bit = 1
    while bit < size:
        value = value + lax.ppermute(value, axis, [(i, i ^ bit) for i in range(size)])
        bit *= 2
    return value


def turn(value, by, size):
    return lax.ppermute(value, "seq", [(i, (i + by) % size) for i in range(size)])


def spread_line(pieces, size):
    return [pieces[0]] + [turn(pieces[k], k, size) for k in range(1, size)]


def scatter_line(pieces, size, order=()):
    return add_up(spread_line(pieces, size), order)


VMEM, SMEM, ANY = pltpu.VMEM, pltpu.SMEM, pl.ANY


def cost(micros):
    return pl.CostEstimate(flops=int(micros * 1.15e9), bytes_accessed=1 << 16, transcendentals=0)


def call(kernel, operands, shapes, scratch=(), scalars=0, order=(), micros=3):
    spaces = [SMEM] * scalars + [VMEM] * (len(operands) - scalars) + [ANY] * len(order)
    skipped = len(order)

    def body(*refs):
        count = len(operands)
        kernel(*refs[:count], *refs[count + skipped :])

    return pl.pallas_call(
        body,
        in_specs=[pl.BlockSpec(memory_space=space) for space in spaces],
        out_specs=[pl.BlockSpec(memory_space=VMEM) for _ in shapes],
        out_shape=[jax.ShapeDtypeStruct(shape, dtype) for shape, dtype in shapes],
        scratch_shapes=list(scratch),
        compiler_params=pltpu.CompilerParams(vmem_limit_bytes=VMEM_LIMIT),
        cost_estimate=cost(micros),
    )(*operands, *order)


def held(values, order):
    count = len(values)
    kept = pl.pallas_call(
        lambda *refs: None,
        in_specs=[pl.BlockSpec(memory_space=ANY)] * (count + len(order)),
        out_specs=[pl.BlockSpec(memory_space=ANY)] * count,
        out_shape=[jax.ShapeDtypeStruct(value.shape, value.dtype) for value in values],
        input_output_aliases={i: i for i in range(count)},
    )(*values, *order)
    return list(kept)


def padded(width):
    return -(-width // 128) * 128


def movable(grain):
    return jnp.bfloat16 if grain % 16 == 0 else jnp.float32


def blocks_of(refs, rows=512):
    found, offset = [], 0
    for ref in refs:
        step = ref.shape[0] if ref.shape[0] <= rows else math.gcd(ref.shape[0], rows)
        for start in range(0, ref.shape[0], step):
            at = offset + start
            found.append((ref, slice(start, start + step), slice(at, at + step)))
        offset += ref.shape[0]
    return found


def copy_kernel(in_ref, out_ref):
    out_ref[:, : in_ref.shape[1]] = in_ref[...]


def copied(value, order):
    rows, width = value.shape
    return call(copy_kernel, [value], [((rows, padded(width)), value.dtype)], order=order)[0]


def pack(share, columns, parts, order=()):
    high, width = share.shape
    rows, wide = columns.shape[0] // parts, columns.shape[1]

    def kernel(share_ref, columns_ref, out_ref):
        out_ref[:high, :width] = share_ref[...]
        for i in range(parts):
            out_ref[high:, i * wide : (i + 1) * wide] = columns_ref[i * rows : (i + 1) * rows, :]

    shape = (high + rows, padded(width))
    return call(kernel, [share, columns], [(shape, share.dtype)], order=order)[0]


def unpack(gathered, high, wide, parts, seq_size):
    step = gathered.shape[0] // seq_size
    rows = step - high

    def kernel(in_ref, out_ref):
        for s in range(seq_size):
            for i in range(parts):
                at = (s * parts + i) * rows
                out_ref[at : at + rows, :] = in_ref[
                    s * step + high : (s + 1) * step, i * wide : (i + 1) * wide
                ]

    shape = (seq_size * parts * rows, wide)
    return call(kernel, [gathered], [(shape, gathered.dtype)])[0]


def total_of(refs, width=None):
    total = refs[0][:, :width].astype(jnp.float32)
    for ref in refs[1:]:
        total = total + ref[:, :width].astype(jnp.float32)
    return total


def add_kernel(*refs):
    refs[-1][...] = total_of(refs[:-1]).astype(refs[-1].dtype)


def add_up(parts, order=()):
    return call(add_kernel, parts, [(parts[0].shape, jnp.bfloat16)], order=order)[0]


def centre(values):
    centered = values - jnp.mean(values, axis=-1, keepdims=True)
    inverse = lax.rsqrt(jnp.mean(centered * centered, axis=-1, keepdims=True) + 1e-05)
    return centered * inverse, inverse


def norm_kernel(tokens_ref, gain_ref, shift_ref, out_ref):
    hat, _ = centre(tokens_ref[...].astype(jnp.float32))
    out_ref[:, : hat.shape[1]] = (hat * gain_ref[...] + shift_ref[...]).astype(out_ref.dtype)


def branch_kernel(tokens_ref, bias_ref, gain_ref, shift_ref, *refs):
    *parts, resid_ref, out_ref = refs
    resid = tokens_ref[...].astype(jnp.float32) + total_of(parts, bias_ref.shape[1]) + bias_ref[...]
    resid_ref[...] = resid
    hat, _ = centre(resid)
    out_ref[:, : hat.shape[1]] = (hat * gain_ref[...] + shift_ref[...]).astype(out_ref.dtype)


def norm_back(values, upstream, gain):
    hat, inverse = centre(values)
    d_hat = upstream * gain
    back = inverse * (
        d_hat
        - jnp.mean(d_hat, axis=-1, keepdims=True)
        - hat * jnp.mean(d_hat * hat, axis=-1, keepdims=True)
    )
    return back, jnp.sum(upstream * hat, axis=0), jnp.sum(upstream, axis=0)


def branch_back_kernel(resid_ref, cotangent_ref, gain_ref, *refs):
    *parts, d_resid_ref, d_branch_ref, sums_ref = refs
    cotangent = cotangent_ref[...].astype(jnp.float32)
    back, d_gain, d_shift = norm_back(
        resid_ref[...], total_of(parts, gain_ref.shape[1]), gain_ref[...]
    )
    d_resid = cotangent + back
    d_branch = d_resid.astype(jnp.bfloat16)
    d_resid_ref[...] = d_resid
    d_branch_ref[:, : d_branch.shape[1]] = d_branch
    sums_ref[0, :] = d_gain
    sums_ref[1, :] = d_shift
    sums_ref[2, :] = jnp.sum(d_branch.astype(jnp.float32), axis=0)
    sums_ref[3, :] = jnp.sum(cotangent, axis=0)


def output_kernel(resid_ref, bias_ref, *refs):
    total = resid_ref[...] + total_of(refs[:-1], bias_ref.shape[1]) + bias_ref[...]
    refs[-1][...] = total.astype(refs[-1].dtype)


def product_rows(lefts, rights, transposed, parts, received, order=()):
    length = lefts[0].shape[0]
    rows = length // 2 // parts
    steps = parts // 2
    wide = rights[0].shape[0 if transposed else 1]
    sent = padded(wide)
    multiply = contract_last if transposed else (
        lambda left, right: jnp.dot(left, right, preferred_element_type=jnp.float32)
    )
    skipped = 0 if received else steps

    def kernel(*refs):
        left_refs, right_refs = refs[: len(lefts)], refs[len(lefts) : 2 * len(lefts)]
        rest = refs[2 * len(lefts) + len(order) :]
        got_refs, out_refs = rest[: len(received)], rest[len(received) :]
        total = multiply(left_refs[0][...], right_refs[0][...])
        for left_ref, right_ref in zip(left_refs[1:], right_refs[1:]):
            total = total + multiply(left_ref[...], right_ref[...])
        for i in range(parts):

            @pl.when(pl.program_id(0) == i // 2)
            def _():
                part = total[(i % 2) * rows : (i % 2 + 1) * rows]
                if got_refs:
                    part = part + got_refs[i][:, :wide].astype(jnp.float32)
                out_refs[i][:, :wide] = part.astype(jnp.bfloat16)

    whole = pl.BlockSpec((rows, sent), lambda i: (0, 0))
    return pl.pallas_call(
        kernel,
        grid=(steps,),
        in_specs=[
            pl.BlockSpec((2 * rows, left.shape[1]), lambda i: (i + skipped, 0)) for left in lefts
        ]
        + [pl.BlockSpec(right.shape, lambda i: (0, 0)) for right in rights]
        + [pl.BlockSpec(memory_space=ANY) for _ in order]
        + [whole for _ in received],
        out_specs=[whole] * parts,
        out_shape=[jax.ShapeDtypeStruct((rows, sent), jnp.bfloat16)] * parts,
        compiler_params=pltpu.CompilerParams(vmem_limit_bytes=VMEM_LIMIT),
        cost_estimate=cost(1),
    )(*lefts, *rights, *order, *received)


def row_products(pieces, right, order=()):
    length, wide = sum(piece.shape[0] for piece in pieces), right.shape[1]

    def kernel(*refs):
        *piece_refs, right_ref, out_ref = refs
        for ref, at, here in blocks_of(piece_refs):
            out_ref[here, :] = jnp.dot(
                ref[at, : right_ref.shape[0]], right_ref[...], preferred_element_type=jnp.float32
            ).astype(out_ref.dtype)

    return call(
        kernel, [*pieces, right], [((length, wide), jnp.bfloat16)], order=order, micros=1
    )[0]


def hidden_layer(pieces, weight, bias, d_act):
    length, wide = d_act.shape

    def kernel(*refs):
        *piece_refs, weight_ref, bias_ref, d_ref, act_ref, d_up_ref, sums_ref = refs
        sums = jnp.zeros((1, wide), jnp.float32)
        root = math.sqrt(2.0 / math.pi)
        for ref, at, here in blocks_of(piece_refs):
            up = contract_last(ref[at, : weight_ref.shape[1]], weight_ref[...]) + bias_ref[...]
            square = up * up
            bent = jnp.tanh(root * up * (1.0 + 0.044715 * square))
            act_ref[here, :] = (0.5 * up * (1.0 + bent)).astype(act_ref.dtype)
            slope = 0.5 * (1.0 + bent) + 0.5 * up * (1.0 - bent * bent) * root * (
                1.0 + 3.0 * 0.044715 * square
            )
            d_up = (d_ref[here, :].astype(jnp.float32) * slope).astype(jnp.bfloat16)
            d_up_ref[here, :] = d_up
            sums = sums + jnp.sum(d_up.astype(jnp.float32), axis=0, keepdims=True)
        sums_ref[...] = sums

    return call(
        kernel,
        [*pieces, weight, bias, d_act],
        [((length, wide), jnp.bfloat16)] * 2 + [((1, wide), jnp.float32)],
        micros=20,
    )


def row_sums(lefts, rights, high, wide, order=(), starts=None, rows=0, margin=0, grain=16, extra=None, micros=1):
    length = sum(left.shape[0] for left in lefts)
    cut = starts is not None
    added = [] if extra is None else [extra]
    count = starts.shape[0] // (1 + len(added)) if cut else 1
    below = extra.shape[0] // count if added else 0

    def kernel(*refs):
        if cut:
            starts_ref, *refs = refs
        left_refs, right_refs = refs[: len(lefts)], refs[len(lefts) : len(lefts) + len(rights)]
        scratch = list(refs[len(lefts) + len(rights) :])
        extra_refs = [scratch.pop(0) for _ in added]
        out_refs = [scratch.pop(0) for _ in range(count)]
        out_ref = scratch.pop() if cut else out_refs[0]
        sides = []
        for parts, columns in ((left_refs, high), (right_refs, wide)):
            if len(parts) == 1:
                sides.append(parts[0])
                continue
            whole = scratch.pop(0)
            for ref, at, here in blocks_of(parts):
                whole[here, :] = ref[at, :columns]
            sides.append(whole)
        for start in range(0, high, 256):
            stop = min(start + 256, high)
            out_ref[margin + start : margin + stop, :wide] = contract_first(
                sides[0][:, start:stop], sides[1][:, :wide]
            ).astype(out_ref.dtype)
        if cut:
            if margin:
                nothing = jnp.zeros((margin, padded(wide)), out_ref.dtype)
                out_ref[:margin, :] = nothing
                out_ref[margin + high :, :] = nothing
            for i, piece_ref in enumerate(out_refs):
                at = pl.ds(pl.multiple_of(starts_ref[i], grain), rows)
                piece_ref[:rows, :] = out_ref[at, :].astype(piece_ref.dtype)
                for extra_ref in extra_refs:
                    at = pl.ds(pl.multiple_of(starts_ref[count + i] * below, 16), below)
                    piece_ref[rows:, :] = extra_ref[at, :]

    scratch = [
        pltpu.VMEM((length, columns), jnp.bfloat16)
        for columns, parts in ((high, lefts), (wide, rights))
        if len(parts) > 1
    ]
    if not cut:
        shape = (high, padded(wide))
        return call(
            kernel, [*lefts, *rights], [(shape, jnp.bfloat16)], scratch, order=order, micros=micros
        )[0]
    scratch.append(pltpu.VMEM((high + 2 * margin, padded(wide)), movable(grain)))
    shapes = [((rows + below, padded(wide)), jnp.bfloat16)] * count
    return call(
        kernel, [starts, *lefts, *rights, *added], shapes, scratch, scalars=1, order=order, micros=micros
    )


def folded_sums(lefts, right, high, blocks, width, order=()):
    length, wide = right.shape
    count, parts, rows = blocks
    step = -(-rows // 32) * 32

    def kernel(*refs):
        *left_refs, right_ref, out_ref, whole, result = refs
        for ref, at, here in blocks_of(left_refs):
            whole[here, :] = ref[at, :high]
        for start in range(0, high, 256):
            stop = min(start + 256, high)
            result[start:stop, :] = contract_first(whole[:, start:stop], right_ref[...]).astype(
                result.dtype
            )
        out_ref[...] = jnp.zeros_like(out_ref)
        for s in range(count):
            for i in range(parts):
                at = (s * parts + i) * rows
                out_ref[s * step : s * step + rows, i * wide : (i + 1) * wide] = result[
                    at : at + rows, :
                ]

    return call(
        kernel,
        [*lefts, right],
        [((count * step, padded(width)), jnp.bfloat16)],
        [pltpu.VMEM((length, high), jnp.bfloat16), pltpu.VMEM((high, wide), jnp.bfloat16)],
        order=order,
        micros=1,
    )[0]


def final_rows(at, sources, places, groups, grain, heads, blocks, wide):
    count = sources.shape[1]
    heights = [sum(piece.shape[0] for piece in pieces) for pieces in groups]
    pieces = [piece for group in groups for piece in group]
    _, parts, rows = blocks
    positions = places.shape[1]
    stride = heights[0] // positions

    def kernel(at_ref, source_ref, place_ref, *refs):
        *piece_refs, qkv_ref, out_ref, whole = refs
        for ref, rows_at, here in blocks_of(piece_refs):
            whole[here, :] = ref[rows_at, :].astype(whole.dtype)
        for g in range(count):
            from_row = pl.ds(pl.multiple_of(source_ref[at_ref[0] * count + g] * grain, grain), grain)
            qkv_ref[g * grain : (g + 1) * grain, :] = whole[from_row, :wide].astype(jnp.float32)
        for i in range(parts):
            columns = []
            for p, (skip, used) in enumerate(heads):
                slot = place_ref[at_ref[1] * positions + p]
                from_row = pl.ds(pl.multiple_of(slot * stride + 2 * HEAD_DIM, 16), rows)
                start = i * blocks[0] + skip * HEAD_DIM
                columns.append(whole[from_row, start : start + used * HEAD_DIM].astype(jnp.float32))
            out_ref[i * rows : (i + 1) * rows, :] = jnp.concatenate(columns, axis=1)

    return call(
        kernel,
        [
            at,
            jnp.asarray(sources.reshape(-1)),
            jnp.asarray(places.reshape(-1)),
            *pieces,
        ],
        [((count * grain, wide), jnp.float32), ((parts * rows, wide), jnp.float32)],
        [pltpu.VMEM((sum(heights), pieces[0].shape[1]), movable(grain))],
        scalars=3,
        micros=8,
    )


def last_kernel(tokens_ref, d_resid_ref, gain_ref, *refs, terms):
    *parts, out_ref, sums_ref, share_ref = refs
    share_ref[...] = total_of(parts[terms:]).astype(share_ref.dtype)
    back, d_gain, d_shift = norm_back(
        tokens_ref[...].astype(jnp.float32), total_of(parts[:terms], gain_ref.shape[1]), gain_ref[...]
    )
    out_ref[...] = d_resid_ref[...] + back
    sums_ref[0, :] = d_gain
    sums_ref[1, :] = d_shift


def widen(gathered, rows, wide, order=()):
    count, high, columns = gathered.shape
    step = 8 // math.gcd(rows, 8)

    def kernel(in_ref, *refs):
        out_ref = refs[-1]
        for i in range(step):
            out_ref[i * rows : (i + 1) * rows, :] = in_ref[i, :rows, :wide].astype(jnp.float32)

    return pl.pallas_call(
        kernel,
        grid=(count // step,),
        in_specs=[pl.BlockSpec((step, high, columns), lambda i: (i, 0, 0))]
        + [pl.BlockSpec(memory_space=ANY) for _ in order],
        out_specs=pl.BlockSpec((step * rows, wide), lambda i: (i, 0)),
        out_shape=jax.ShapeDtypeStruct((count * rows, wide), jnp.float32),
        compiler_params=pltpu.CompilerParams(vmem_limit_bytes=VMEM_LIMIT),
        cost_estimate=cost(8),
    )(gathered, *order)


def columns_kernel(at_ref, in_ref, out_ref, *, pieces):
    out_ref[...] = jnp.concatenate(
        [in_ref[i ^ at_ref[0], :, start:stop].astype(jnp.float32) for i, start, stop in pieces],
        axis=1,
    )


def join_columns(at, gathered, pieces):
    count, rows, columns = gathered.shape
    wide = sum(stop - start for _, start, stop in pieces)
    block = math.gcd(rows, 80)
    return pl.pallas_call(
        functools.partial(columns_kernel, pieces=pieces),
        grid_spec=pltpu.PrefetchScalarGridSpec(
            num_scalar_prefetch=1,
            grid=(rows // block,),
            in_specs=[pl.BlockSpec((count, block, columns), lambda i, at: (0, i, 0))],
            out_specs=pl.BlockSpec((block, wide), lambda i, at: (i, 0)),
        ),
        out_shape=jax.ShapeDtypeStruct((rows, wide), jnp.float32),
        compiler_params=pltpu.CompilerParams(vmem_limit_bytes=VMEM_LIMIT),
        cost_estimate=cost(1),
    )(at.reshape(1), gathered)


def attention_forward_kernel(order_ref, *refs, half, grain, seq_size):
    from_ref, *piece_refs, bias_ref, out_ref, qkv_ref, weight_ref, qs, ks, vs, whole = refs
    length, wide = out_ref.shape
    piece_refs, share_refs = piece_refs[:-1], piece_refs[-1:]
    part = share_refs[0].shape[0] // seq_size
    for i in range(seq_size):
        here = slice(i * wide, (i + 1) * wide)
        whole[here, :] = share_refs[0][i * part : i * part + wide, : whole.shape[1]].astype(whole.dtype)
    for t in range(3):
        at = pl.ds(pl.multiple_of(from_ref[t], grain), wide)
        weight_ref[t * wide : (t + 1) * wide, :] = whole[at, :].astype(weight_ref.dtype)
    tile = 2 * half
    for ref, at, here in blocks_of(piece_refs):
        qkv_ref[here, :] = (
            contract_last(ref[at, : weight_ref.shape[1]], weight_ref[...]) + bias_ref[...]
        ).astype(qkv_ref.dtype)
    for p in range(length // half):
        rows = pl.ds(pl.multiple_of(order_ref[p] * half, half), half)
        here = slice(p * half, (p + 1) * half)
        qs[here, :] = qkv_ref[rows, :wide]
        ks[here, :] = qkv_ref[rows, wide : 2 * wide]
        vs[here, :] = qkv_ref[rows, 2 * wide :]
    visible = lax.broadcasted_iota(jnp.int32, (tile, tile), 1) <= lax.broadcasted_iota(
        jnp.int32, (tile, tile), 0
    )
    scale = 0.125 * LOG2E
    for i in range(length // tile):
        span = (i + 1) * tile
        outs = []
        for h in range(wide // HEAD_DIM):
            lanes = slice(h * HEAD_DIM, (h + 1) * HEAD_DIM)
            q = qs[i * tile : span, lanes]
            scores = contract_last(q, ks[:span, lanes])
            last = jnp.where(visible, scores[:, i * tile :], NEGATIVE)
            scores = jnp.concatenate([scores[:, : i * tile], last], axis=1) if i else last
            top = jnp.max(scores, axis=1, keepdims=True)
            raised = jnp.exp2(scores * scale - top * scale)
            total = jnp.sum(raised, axis=1, keepdims=True)
            weights = (raised * (1.0 / total)).astype(jnp.bfloat16)
            outs.append(
                jnp.dot(weights, vs[:span, lanes], preferred_element_type=jnp.float32)
            )
        merged = jnp.concatenate(outs, axis=1).astype(out_ref.dtype)
        for j in range(tile // half):
            rows = pl.ds(pl.multiple_of(order_ref[i * (tile // half) + j] * half, half), half)
            out_ref[rows, :] = merged[j * half : (j + 1) * half, :]


def attention_forward(block_order, pieces, starts, shares, bias, width, half, grain, seq_size, order=()):
    length = sum(piece.shape[0] for piece in pieces)
    wide = bias.shape[1] // 3
    return call(
        functools.partial(attention_forward_kernel, half=half, grain=grain, seq_size=seq_size),
        [block_order, starts, *pieces, shares, bias],
        [
            ((length, wide), jnp.bfloat16),
            ((length, 3 * wide), jnp.bfloat16),
            ((3 * wide, width), jnp.bfloat16),
        ],
        [pltpu.VMEM((length, wide), jnp.bfloat16)] * 3
        + [pltpu.VMEM((seq_size * wide, width), movable(grain))],
        scalars=2,
        micros=20,
        order=order,
    )


def attention_backward_kernel(order_ref, *refs, half):
    *piece_refs, weight_ref, qkv_ref, out_ref, sums_ref, qs, ks, vs, ds, kt, dks, dvs, raw = refs
    length, wide = qs.shape
    tile = 2 * half
    for ref, at, here in blocks_of(piece_refs):
        raw[here, :] = jnp.dot(
            ref[at, : weight_ref.shape[0]], weight_ref[...], preferred_element_type=jnp.float32
        ).astype(raw.dtype)
    for p in range(length // half):
        rows = pl.ds(pl.multiple_of(order_ref[p] * half, half), half)
        here = slice(p * half, (p + 1) * half)
        qs[here, :] = qkv_ref[rows, :wide]
        ks[here, :] = qkv_ref[rows, wide : 2 * wide]
        vs[here, :] = qkv_ref[rows, 2 * wide :]
        ds[here, :] = raw[rows, :]
    kt[...] = ks[...].T
    dks[...] = jnp.zeros_like(dks)
    dvs[...] = jnp.zeros_like(dvs)
    visible = lax.broadcasted_iota(jnp.int32, (tile, tile), 0) <= lax.broadcasted_iota(
        jnp.int32, (tile, tile), 1
    )
    scale = 0.125 * LOG2E
    heads = wide // HEAD_DIM
    for i in range(length // tile):
        span = (i + 1) * tile
        outs, d_keys, d_values = [], [], []
        for h in range(heads):
            lanes = slice(h * HEAD_DIM, (h + 1) * HEAD_DIM)
            q = qs[i * tile : span, lanes]
            d_out = ds[i * tile : span, lanes]
            scores = contract_last(ks[:span, lanes], q)
            last = jnp.where(visible, scores[i * tile :, :], NEGATIVE)
            scores = jnp.concatenate([scores[: i * tile, :], last], axis=0) if i else last
            top = jnp.max(scores, axis=0, keepdims=True)
            raised = jnp.exp2(scores * scale - top * scale)
            weights = raised * (1.0 / jnp.sum(raised, axis=0, keepdims=True))
            d_weights = contract_last(vs[:span, lanes], d_out)
            row_dot = jnp.sum(weights * d_weights, axis=0, keepdims=True)
            d_scores = (weights * (d_weights - row_dot)).astype(jnp.bfloat16)
            d_values.append(
                jnp.dot(weights.astype(jnp.bfloat16), d_out, preferred_element_type=jnp.float32)
            )
            d_keys.append(jnp.dot(d_scores, q, preferred_element_type=jnp.float32))
            outs.append(
                jnp.dot(kt[lanes, :span], d_scores, preferred_element_type=jnp.float32)
            )
        dks[:span, :] += jnp.concatenate(d_keys, axis=1)
        dvs[:span, :] += jnp.concatenate(d_values, axis=1)
        merged = (jnp.concatenate(outs, axis=0) * 0.125).T.astype(out_ref.dtype)
        for j in range(tile // half):
            rows = pl.ds(pl.multiple_of(order_ref[i * (tile // half) + j] * half, half), half)
            out_ref[rows, :wide] = merged[j * half : (j + 1) * half, :]
    for p in range(length // half):
        rows = pl.ds(pl.multiple_of(order_ref[p] * half, half), half)
        here = slice(p * half, (p + 1) * half)
        out_ref[rows, wide : 2 * wide] = (dks[here, :] * 0.125).astype(out_ref.dtype)
        out_ref[rows, 2 * wide :] = dvs[here, :].astype(out_ref.dtype)


    sums_ref[...] = jnp.sum(out_ref[...].astype(jnp.float32), axis=0, keepdims=True)


def attention_backward(block_order, pieces, weight, qkv, half, order=()):
    length = qkv.shape[0]
    wide = weight.shape[1]
    return call(
        functools.partial(attention_backward_kernel, half=half),
        [block_order, *pieces, weight, qkv],
        [((length, 3 * wide), jnp.bfloat16), ((1, 3 * wide), jnp.float32)],
        [pltpu.VMEM((length, wide), jnp.bfloat16)] * 4
        + [pltpu.VMEM((wide, length), jnp.bfloat16)]
        + [pltpu.VMEM((length, wide), jnp.float32)] * 2
        + [pltpu.VMEM((length, wide), jnp.bfloat16)],
        scalars=1,
        micros=28,
        order=order,
    )


def per_device(
    tokens_in,
    block_index,
    norm_gains,
    norm_shifts,
    w_qkv,
    bias_model,
    w_out,
    w_up,
    bias_up,
    w_down,
    cotangent,
):
    seq_size, ctx_size = lax.axis_size("seq"), lax.axis_size("ctx")
    z, c = lax.axis_index("seq"), lax.axis_index("ctx")
    tok_rows, width = tokens_in.shape[1], tokens_in.shape[2]
    length = tok_rows * ctx_size
    half = length // block_index.shape[0]
    hidden = bias_up.shape[0]
    own_hidden = hidden // seq_size // ctx_size
    kept_hidden = -(-own_hidden // 16) * 16
    low = jnp.bfloat16

    plane = Plane(ctx_size)
    out_blocks = (seq_size, 5, w_out.shape[0] // 5)
    below = -(-out_blocks[2] // 32) * 32
    plan = HeadPlan(seq_size, ctx_size, w_qkv.shape[0], width, plane, below)
    groups, rows = plan.groups, plan.rows
    window = groups * rows
    table = lambda values, *index: jnp.asarray(np.asarray(values, np.int32))[index]
    head_from = table(plan.window, c) * HEAD_DIM
    slot = jnp.arange(window, dtype=jnp.int32) // HEAD_DIM - table(plan.skip, c)
    used = (slot >= 0) & (slot < table(plan.count, c))
    blocks = block_index.shape[0]
    numbers = jnp.arange(blocks, dtype=jnp.int32)
    place_of = np.zeros((ctx_size, blocks), np.int32)
    for at in range(ctx_size):
        for b in range(blocks):
            place_of[at, b] = plane.place((b // 2) ^ at) * 2 + b % 2
    order = jnp.sum(
        jnp.where(block_index[None, :] == numbers[:, None], table(place_of, c)[None, :], 0), axis=1
    )
    row = lambda value: value.reshape(1, -1)
    shape, wide_shape = (tok_rows, width), (tok_rows, padded(width))

    tokens, own_cotangent = tokens_in[0], cotangent[0]
    gather_seq = lambda value: lax.all_gather(value, "seq", axis=0, tiled=True)
    shares = [
        lax.dynamic_slice_in_dim(w_qkv, table(plan.piece_start, g, z, c), rows, 0)
        for g in range(groups)
    ]
    normed1 = call(
        norm_kernel, [tokens, row(norm_gains[0]), row(norm_shifts[0])], [(wide_shape, low)]
    )[0]
    all_normed1 = plane.gather(normed1)
    out_share = jnp.where(
        used[None, :], lax.dynamic_slice_in_dim(w_out, head_from, window, 1), 0
    )
    shares[-1] = pack(shares[-1], out_share, 5, [normed1])
    qkv_pieces = [gather_seq(share) for share in shares]
    own_out = unpack(qkv_pieces[-1], rows, window, 5, seq_size)
    up_share = lax.dynamic_slice_in_dim(w_up, c * own_hidden, own_hidden, 0)
    fill = lambda value, axis: jnp.pad(
        value, [(0, kept_hidden - own_hidden if i == axis else 0) for i in range(value.ndim)]
    )
    up_share = fill(up_share, 0)
    down_share = jnp.concatenate(
        [
            fill(lax.dynamic_slice_in_dim(w_down, (s * ctx_size + c) * own_hidden, own_hidden, 1), 1)
            for s in range(seq_size)
        ],
        axis=1,
    )
    own_down = gather_seq(after(down_share, qkv_pieces[0]))
    own_up = gather_seq(after(up_share, qkv_pieces[0]))
    own_bias_up = jnp.concatenate(
        [
            fill(lax.dynamic_slice_in_dim(bias_up, (s * ctx_size + c) * own_hidden, own_hidden, 0), 0)
            for s in range(seq_size)
        ]
    )

    attended, qkv, own_qkv = [], [], []
    for g in range(groups):
        from_head = head_from + g * rows
        own_bias = jnp.concatenate(
            [
                lax.dynamic_slice_in_dim(bias_model[0], from_head, rows, 0),
                jnp.zeros((rows,), jnp.float32),
                lax.dynamic_slice_in_dim(bias_model[1], from_head, rows, 0),
            ]
        )
        if g == groups - 1:
            near = plane.send(copied(own_cotangent, all_normed1[-1:]))
            all_cotangent = plane.share(held(near, attended) if attended else near)
        out, kept, weight = attention_forward(
            order,
            all_normed1,
            table(plan.range_from, g, c),
            qkv_pieces[g],
            row(own_bias),
            width,
            half,
            plan.grain,
            seq_size,
            attended and all_cotangent[-1:],
        )
        own_qkv.append(weight)
        attended.append(out)
        qkv.append(kept)
    own_outs = [own_out[:, g * rows : (g + 1) * rows] for g in range(groups)]
    sent = plane.other_half(attended, own_outs, True)
    parts = plane.scatter(attended, own_outs, True, sent)
    d_act = row_products(all_cotangent, own_down)
    resid, normed2 = call(
        branch_kernel,
        [tokens, row(bias_model[2]), row(norm_gains[1]), row(norm_shifts[1]), *parts],
        [(shape, jnp.float32), (wide_shape, low)],
        order=[d_act],
    )
    all_normed2 = plane.gather(normed2)
    act, d_up, grad_up_bias = hidden_layer(all_normed2, own_up, row(own_bias_up), d_act)

    sent = plane.other_half([d_up], [own_up], False)
    parts = plane.scatter([d_up], [own_up], False, sent)
    part_down = row_sums(all_cotangent, [act], width, act.shape[1], parts[:1])
    part_up = row_sums([d_up], all_normed2, act.shape[1], width, parts[:1])
    down_sent = plane.other_half([act], [own_down], True, parts[:1])
    scatter_seq = lambda value: lax.psum_scatter(value, "seq", scatter_dimension=0, tiled=True)
    d_resid, d_branch, sums2 = call(
        branch_back_kernel,
        [resid, own_cotangent, row(norm_gains[1]), *parts],
        [(shape, jnp.float32), (wide_shape, low), ((4, width), jnp.float32)],
        order=[part_down, part_up, down_sent[0]],
    )
    grad_w_down, grad_w_up = (scatter_seq(part) for part in held([part_down, part_up], [d_branch]))
    near_branch = plane.send(d_branch)
    down_parts = plane.halves([act], [own_down], True, down_sent)
    all_branch = plane.share(near_branch, down_parts[:1])
    down_parts = plane.exchange(held(down_parts, all_branch[-1:]))
    turned = plan.piece_from[:, :, (np.arange(seq_size)[:, None] + np.arange(seq_size)) % seq_size]
    gather_ctx = lambda value: lax.all_gather(value, "ctx", axis=0)
    round_from = (z + jnp.arange(seq_size, dtype=jnp.int32)) % seq_size
    d_qkv, d_sums, early = [], [], []
    later = attention_backward(order, all_branch, own_outs[0], qkv[0], half, down_parts[:1])
    for g in range(groups):
        out, sums = later
        starts, extra = table(turned, g, c, z), None
        if g == 0:
            extra = folded_sums(
                all_branch, jnp.concatenate(attended, axis=1), width, out_blocks, width, [out]
            )
            starts = jnp.concatenate([starts, round_from])
        pieces = row_sums(
            [out],
            all_normed1,
            out.shape[1],
            width,
            early,
            starts=starts,
            rows=rows,
            margin=rows,
            grain=plan.grain,
            extra=extra,
        )
        if g == 0:
            grad_w_down = gather_ctx(held([grad_w_down], pieces[:1])[0])
            tokens_out = call(
                output_kernel, [resid, row(bias_model[3]), *down_parts], [(shape, low)], order=pieces[:1]
            )[0][None]
        if g < groups - 1:
            later = attention_backward(
                order, all_branch, own_outs[g + 1], qkv[g + 1], half, [pieces[0], tokens_out]
            )
            early.append(scatter_line(pieces, seq_size, later[:1]))
        d_qkv.append(out)
        d_sums.append(sums)
    grad_w_up = gather_ctx(held([grad_w_up], pieces[:1])[0])
    sent = plane.other_half(d_qkv, own_qkv, False, pieces[:1])
    gathered = [plane.send(share) for share in early]
    parts = plane.exchange(plane.halves(d_qkv, own_qkv, False, sent))
    gathered = [plane.share(near) for near in gathered]
    grad_w_down = join_columns(
        jnp.int32(0),
        grad_w_down,
        [
            (i, s * kept_hidden, s * kept_hidden + own_hidden)
            for s in range(seq_size)
            for i in range(ctx_size)
        ],
    )
    terms = spread_line(pieces, seq_size)
    grad_tokens, sums1, share = call(
        functools.partial(last_kernel, terms=len(parts)),
        [tokens, d_resid, row(norm_gains[0]), *parts, *terms],
        [(shape, jnp.float32), ((2, width), jnp.float32), (terms[0].shape, low)],
        order=[grad_w_down] + [piece for group in gathered for piece in group[-1:]],
    )
    grad_tokens = grad_tokens[None]
    near = plane.send(share)
    gathered.append(plane.share(near))
    grad_w_up = widen(grad_w_up, own_hidden, width, near[1:3])
    grad_w_qkv, grad_w_out = final_rows(
        jnp.stack([z * ctx_size + c, c]),
        plan.source.reshape(seq_size * ctx_size, -1),
        np.array([[plane.place(i ^ at) for i in range(ctx_size)] for at in range(ctx_size)], np.int32),
        gathered,
        plan.grain,
        list(zip(plan.skip, plan.count)),
        (window, *out_blocks[1:]),
        width,
    )

    place = lambda t: lax.dynamic_update_slice(
        jnp.zeros((1, width), jnp.float32),
        jnp.concatenate([part[:, t * rows : (t + 1) * rows] for part in d_sums], axis=1),
        (0, head_from),
    )
    spread_up = jnp.zeros((seq_size, ctx_size, own_hidden), jnp.float32)
    grad_up_bias = lax.dynamic_update_slice(
        spread_up, grad_up_bias.reshape(seq_size, 1, kept_hidden)[:, :, :own_hidden], (0, c, 0)
    ).reshape(-1, width)
    small = jnp.concatenate(
        [sums1[:1], sums2[:1], sums1[1:], sums2[1:2], place(0), place(2), sums2[2:], grad_up_bias]
    )
    small = total_by_bits(total_by_bits(small, "ctx", ctx_size), "seq", seq_size)
    return (
        tokens_out,
        grad_tokens,
        small[:2],
        small[2:4],
        grad_w_qkv,
        small[4:8],
        grad_w_out,
        grad_w_up,
        small[8:].reshape(-1),
        grad_w_down,
    )


def solution(mesh):
    placed = (
        P("seq", "ctx", None),
        P(),
        P(),
        P(),
        P("seq", None),
        P(),
        P("seq", None),
        P("seq", None),
        P(),
        P("seq", None),
        P("seq", "ctx", None),
    )
    return jax.shard_map(
        per_device,
        mesh=mesh,
        in_specs=placed,
        out_specs=(
            P("seq", "ctx", None),
            P("seq", "ctx", None),
            P(),
            P(),
            P("seq", None),
            P(),
            P("seq", None),
            P("seq", None),
            P(),
            P("seq", None),
        ),
        check_vma=False,
    )
```

time: 1280 us -> 717 us (0.56)
  waiting for transfers between devices: 823 us -> 244 us
  Pallas kernels: 75.5 us -> 309 us
  matrix products: 117 us -> 0 us
  local copies, waits for them, and re-layouts: 146 us -> 51.9 us
  starting transfers between devices: 1.28 us -> 79 us
  other arithmetic: 45.5 us -> 8.95 us
  blocking collectives: 32.8 us -> 0 us
    reduce_scatter x7 -> x2, waiting for transfers between devices: 318 us -> 0.02 us  [per_device(): lax.psum_scatter(value, 'seq', scatter_dimension=0, tiled=True)]
    all_gather x8 -> x2, waiting for transfers between devices: 261 us -> 0.02 us  [per_device(): gather_ctx = lambda value: lax.all_gather(value, 'ctx', axis=0)]
    ppermute x0 -> x93, waiting for transfers between devices: none -> 242 us  [the longest x82 215 us: move(): return lax.ppermute(value, 'ctx', [(i, i ^ bits) for i in range(self.size)])]
    pallas_call x2 -> x37, Pallas kernels: 75.5 us -> 309 us  [the longest x21 227 us: call(): pl.pallas_call(body, in_specs=[pl.BlockSpec(memory_space=space) for space...]
    psum x1 -> x0, waiting for transfers between devices: 120 us -> none  [per_device(): small = lax.psum(small, ('seq', 'ctx'))]
    dot_general x12 -> x0, matrix products: 117 us -> none  [the longest x4 39.2 us: contract_last(): lax.dot_general(left, right, (((1,), (1,)), ((), ())), preferred_element_...]
    all_gather x3 -> x4, waiting for transfers between devices: 106 us -> 1.42 us  [per_device(): gather_seq = lambda value: lax.all_gather(value, 'seq', axis=0, tiled=True)]
    ppermute x0 -> x93, starting transfers between devices: none -> 78.5 us  [the longest x82 54.3 us: move(): return lax.ppermute(value, 'ctx', [(i, i ^ bits) for i in range(self.size)])]
  transfers between devices with their start and end apart: 20 -> 101, of which waited for: 18 -> 40; matrix products, arithmetic and copies ran while one was open for 19% -> 6% of each run, Pallas kernels for 4% -> 36%
where the time goes in v2:
time: 717 us; the launch traced here: 712 us
  Pallas kernels  309 us (43%)
  waiting for transfers between devices  244 us (34%)
  starting transfers between devices  79 us (11%)
  local copies, waits for them, and re-layouts  51.9 us (7%)
  between operations  19.9 us (3%)
  other arithmetic  8.95 us (1%)
    pallas_call x21, Pallas kernels, call(): pl.pallas_call(body, in_specs=[pl.BlockSpec(memory_space=space) for space...  227 us
    ppermute x82, waiting for transfers between devices, move(): return lax.ppermute(value, 'ctx', [(i, i ^ bits) for i in range(self.size)])  215 us
    pallas_call x8, Pallas kernels, product_rows(): pl.pallas_call(kernel, grid=(steps,), in_specs=[pl.BlockSpec((2 * rows, l...  66 us
    ppermute x82, starting transfers between devices, move(): return lax.ppermute(value, 'ctx', [(i, i ^ bits) for i in range(self.size)])  54.3 us
    unnamed x171, local copies, waits for them, and re-layouts  24.3 us
    ppermute x6, starting transfers between devices, turn(): lax.ppermute(value, 'seq', [(i, (i + by) % size) for i in range(size)])  20.7 us
    ppermute x5, waiting for transfers between devices, total_by_bits(): lax.ppermute(value, axis, [(i, i ^ bit) for i in range(size)])  15.6 us
  transfers between devices with their start and end apart: 101, of which 40 were waited for; matrix products, arithmetic and copies ran while one was open for 6% of the time, Pallas kernels for 36%

profile of v2, /device:TPU:0, one launch (start us, length us, event | category | flops | bytes accessed | tf_op | source)
XLA Modules:
  0.0 712.5 jit_solution(14785267184001763796)
XLA Ops:
  19.7 2.7 shard_map.267.refs_2_
  24.4 3.1 collective-permute-start.1
  29.0 17.7 %collective-permute-done.1.refs_4_ = bf16[256,1664]{1,0:T(8,128)(2,1)S(1)} collective-permute-done((bf16[256,1664]{1,0:T(8,128)(2,1)}, bf16[256,1664]{1,0:T(8,128)(2,1)S(1)}, u32[]{:S(2)}, u32[]{:S(2)}) %collective-permute-start.1) | collective-permute-done | bytes 852000 | tf_op jit(solution)/shard_map/ppermute | solution.py:91
  48.5 9.4 %collective-permute-done.3.refs_6_ = bf16[128,1664]{1,0:T(8,128)(2,1)S(1)} collective-permute-done((bf16[128,1664]{1,0:T(8,128)(2,1)S(1)}, bf16[128,1664]{1,0:T(8,128)(2,1)S(1)}, u32[]{:S(2)}, u32[]{:S(2)}) %collective-permute-start.3) | collective-permute-done | bytes 426016 | tf_op jit(solution)/shard_map/ppermute | solution.py:91
  62.7 2.2 shard_map.270.refs_0_
  67.8 4.8 collective-permute-done.2.refs_5_
  77.7 2.5 constant_dynamic-slice_fusion.6
  80.2 5.5 collective-permute-done.9.refs_1_
  85.7 2.3 constant_dynamic-slice_fusion.2
  89.9 2.5 fusion.8
  95.9 21.3 %shard_map.268 = (bf16[2048,128]{1,0:T(8,128)(2,1)}, bf16[2048,384]{1,0:T(8,128)(2,1)}, bf16[384,1600]{1,0:T(8,128)(2,1)}) custom-call(s32[16]{0:T(128)} %select_reduce_fusion.refs_0_, s32[3]{0:T(128)} %get-tuple-element.209.refs_1_, bf16[256,1664]{1,0:T(8,128)(2,1)} %shard_map.267.refs_2_, bf16[256,1664]{1,0:T(8,128)(2,1)} %copy-done.6, ...), custom_call_target="tpu_custom_call" | custom-call | flops 23000000512 | bytes 65536 | tf_op jit(solution)/shard_map/pallas_call | solution.py:156
  118.1 2.7 shard_map.273
  120.8 2.2 fusion.24
  123.8 21.9 %shard_map.272 = (bf16[2048,128]{1,0:T(8,128)(2,1)}, bf16[2048,384]{1,0:T(8,128)(2,1)}, bf16[384,1600]{1,0:T(8,128)(2,1)}) custom-call(s32[16]{0:T(128)} %select_reduce_fusion.refs_0_, s32[3]{0:T(128)} %get-tuple-element.208.refs_1_, bf16[256,1664]{1,0:T(8,128)(2,1)} %shard_map.267.refs_2_, bf16[256,1664]{1,0:T(8,128)(2,1)} %copy-done.6, ...), custom_call_target="tpu_custom_call" | custom-call | flops 23000000512 | bytes 65536 | tf_op jit(solution)/shard_map/pallas_call | solution.py:156
  145.7 5.6 shard_map.274
  155.7 2.3 collective-permute-done.16.refs_6_
  158.2 2.3 collective-permute-done.17.refs_7_
  161.4 7.0 shard_map.275
  174.2 13.4 %shard_map.276.refs_8_.refs_12_ = bf16[2048,832]{1,0:T(8,128)(2,1)} custom-call(bf16[256,1664]{1,0:T(8,128)(2,1)} %get-tuple-element.95.refs_0_, bf16[256,1664]{1,0:T(8,128)(2,1)} %get-tuple-element.96.refs_1_, bf16[256,1664]{1,0:T(8,128)(2,1)} %get-tuple-element.97.refs_2_, bf16[128,1664]{1,0:T(8,128)(2,1)} %get-tuple-element.98.refs_3_, ...), custom_call_target="tpu_custom_call" | custom-call | flops 1150000000 | bytes 65536 | tf_op jit(solution)/shard_map/pallas_call | solution.py:156
  187.6 2.9 collective-permute-done.18.refs_5_
  190.5 17.8 %collective-permute-done.19.refs_6_ = bf16[256,1664]{1,0:T(8,128)(2,1)} collective-permute-done((bf16[256,1664]{1,0:T(8,128)(2,1)}, bf16[256,1664]{1,0:T(8,128)(2,1)}, u32[]{:S(2)}, u32[]{:S(2)}) %collective-permute-start.19) | collective-permute-done | bytes 852000 | tf_op jit(solution)/shard_map/ppermute | solution.py:91
  209.2 4.4 shard_map.277
  215.7 18.1 %collective-permute-done.25.refs_1_.refs_2_ = bf16[256,1664]{1,0:T(8,128)(2,1)S(1)} collective-permute-done((bf16[256,1664]{1,0:T(8,128)(2,1)}, bf16[256,1664]{1,0:T(8,128)(2,1)S(1)}, u32[]{:S(2)}, u32[]{:S(2)}) %collective-permute-start.25) | collective-permute-done | bytes 852000 | tf_op jit(solution)/shard_map/ppermute | solution.py:91
  236.8 7.2 %collective-permute-done.27.refs_3_.refs_4_ = bf16[128,1664]{1,0:T(8,128)(2,1)} collective-permute-done((bf16[128,1664]{1,0:T(8,128)(2,1)S(1)}, bf16[128,1664]{1,0:T(8,128)(2,1)}, u32[]{:S(2)}, u32[]{:S(2)}) %collective-permute-start.27) | collective-permute-done | bytes 426016 | tf_op jit(solution)/shard_map/ppermute | solution.py:91
  248.4 21.1 %shard_map.278 = (bf16[2048,832]{1,0:T(8,128)(2,1)}, bf16[2048,832]{1,0:T(8,128)(2,1)}, f32[1,832]{1,0:T(1,128)}) custom-call(bf16[256,1664]{1,0:T(8,128)(2,1)} %get-tuple-element.100.refs_0_.refs_1_, bf16[256,1664]{1,0:T(8,128)(2,1)} %copy-done.17, bf16[256,1664]{1,0:T(8,128)(2,1)} %copy-done.18, bf16[128,1664]{1,0:T(8,128)(2,1)} %collective-permute-done.27.refs_3_.refs_4_, ...), custom_call_target="tpu_custom_call" | custom-call | flops 23000000512 | bytes 65536 | tf_op jit(solution)/shard_map/pallas_call | solution.py:156
  269.6 8.3 %shard_map.279 = (bf16[256,1664]{1,0:T(8,128)(2,1)}, bf16[256,1664]{1,0:T(8,128)(2,1)}, bf16[256,1664]{1,0:T(8,128)(2,1)}, bf16[256,1664]{1,0:T(8,128)(2,1)}) custom-call(bf16[2048,832]{1,0:T(8,128)(2,1)} %get-tuple-element.102.refs_0_, bf16[832,1600]{1,0:T(8,128)(2,1)} %all-gather.15.cloned.1.call-done.refs_10_.refs_1_), custom_call_target="tpu_custom_call" | custom-call | flops 1150000000 | bytes 65536 | tf_op jit(solution)/shard_map/pallas_call | solution.py:330
  285.0 9.5 %shard_map.280 = (bf16[256,1664]{1,0:T(8,128)(2,1)}, bf16[256,1664]{1,0:T(8,128)(2,1)}, bf16[256,1664]{1,0:T(8,128)(2,1)}, bf16[256,1664]{1,0:T(8,128)(2,1)}) custom-call(bf16[2048,832]{1,0:T(8,128)(2,1)} %get-tuple-element.102.refs_0_, bf16[832,1600]{1,0:T(8,128)(2,1)} %all-gather.15.cloned.1.call-done.refs_10_.refs_1_, bf16[256,1664]{1,0:T(8,128)(2,1)} %copy-done.37, ...), custom_call_target="tpu_custom_call" | custom-call | flops 1150000000 | bytes 65536 | tf_op jit(solution)/shard_map/pallas_call | solution.py:330
  298.1 12.5 %shard_map.284.refs_8_.refs_1_ = bf16[832,1664]{1,0:T(8,128)(2,1)} custom-call(bf16[2048,832]{1,0:T(8,128)(2,1)} %get-tuple-element.102.refs_0_, bf16[256,1664]{1,0:T(8,128)(2,1)} %get-tuple-element.100.refs_0_.refs_1_, bf16[256,1664]{1,0:T(8,128)(2,1)} %copy-done.17, bf16[256,1664]{1,0:T(8,128)(2,1)} %copy-done.18, ...), custom_call_target="tpu_custom_call" | custom-call | flops 1150000000 | bytes 65536 | tf_op jit(solution)/shard_map/pallas_call | solution.py:156
  310.6 13.2 %shard_map.283.refs_7_.refs_0_ = bf16[1600,896]{1,0:T(8,128)(2,1)} custom-call(bf16[256,1664]{1,0:T(8,128)(2,1)} %get-tuple-element.95.refs_0_, bf16[256,1664]{1,0:T(8,128)(2,1)} %get-tuple-element.96.refs_1_, bf16[256,1664]{1,0:T(8,128)(2,1)} %get-tuple-element.97.refs_2_, bf16[128,1664]{1,0:T(8,128)(2,1)} %get-tuple-element.98.refs_3_, ...), custom_call_target="tpu_custom_call" | custom-call | flops 1150000000 | bytes 65536 | tf_op jit(solution)/shard_map/pallas_call | solution.py:156
  323.8 8.4 %shard_map.281 = (bf16[256,1664]{1,0:T(8,128)(2,1)}, bf16[256,1664]{1,0:T(8,128)(2,1)}, bf16[256,1664]{1,0:T(8,128)(2,1)}, bf16[256,1664]{1,0:T(8,128)(2,1)}) custom-call(bf16[2048,832]{1,0:T(8,128)(2,1)} %get-tuple-element.101.refs_0_.refs_10_, bf16[1600,832]{1,0:T(8,128)(2,1)} %all-gather.13.cloned.1.call-done.refs_10_.refs_1_, ...), custom_call_target="tpu_custom_call" | custom-call | flops 1150000000 | bytes 65536 | tf_op jit(solution)/shard_map/pallas_call | solution.py:330
  335.2 6.1 shard_map.285
  345.8 16.9 %collective-permute-done.45.refs_3_.refs_2_ = bf16[256,1664]{1,0:T(8,128)(2,1)S(1)} collective-permute-done((bf16[256,1664]{1,0:T(8,128)(2,1)S(1)}, bf16[256,1664]{1,0:T(8,128)(2,1)S(1)}, u32[]{:S(2)}, u32[]{:S(2)}) %collective-permute-start.45) | collective-permute-done | bytes 852000 | tf_op jit(solution)/shard_map/ppermute | solution.py:91
  369.5 10.0 %shard_map.282 = (bf16[256,1664]{1,0:T(8,128)(2,1)}, bf16[256,1664]{1,0:T(8,128)(2,1)}, bf16[256,1664]{1,0:T(8,128)(2,1)}, bf16[256,1664]{1,0:T(8,128)(2,1)}) custom-call(bf16[2048,832]{1,0:T(8,128)(2,1)} %get-tuple-element.101.refs_0_.refs_10_, bf16[1600,832]{1,0:T(8,128)(2,1)} %all-gather.13.cloned.1.call-done.refs_10_.refs_1_, ...), custom_call_target="tpu_custom_call" | custom-call | flops 1150000000 | bytes 65536 | tf_op jit(solution)/shard_map/pallas_call | solution.py:330
  383.3 28.8 %shard_map.288 = (bf16[2048,384]{1,0:T(8,128)(2,1)}, f32[1,384]{1,0:T(1,128)}) custom-call(s32[16]{0:T(128)} %select_reduce_fusion.refs_0_, bf16[256,1664]{1,0:T(8,128)(2,1)} %get-tuple-element.119.refs_1_.refs_0_.refs_2_, bf16[256,1664]{1,0:T(8,128)(2,1)} %collective-permute-done.51.refs_2_.refs_1_, bf16[256,1664]{1,0:T(8,128)(2,1)} %copy-done.16, ...), custom_call_target="tpu_custom_call" | custom-call | flops 32199999488 | bytes 65536 | tf_op jit(solution)/shard_map/pallas_call | solution.py:156
  412.1 6.8 shard_map.289.refs_12_
  418.9 8.6 %shard_map.290 = (bf16[224,1664]{1,0:T(8,128)(2,1)}, bf16[224,1664]{1,0:T(8,128)(2,1)}, bf16[224,1664]{1,0:T(8,128)(2,1)}, bf16[224,1664]{1,0:T(8,128)(2,1)}) custom-call(s32[8]{0:T(128)} %pad_add_fusion.refs_0_, bf16[2048,384]{1,0:T(8,128)(2,1)} %get-tuple-element.125.refs_11_.refs_1_.refs_0_, bf16[256,1664]{1,0:T(8,128)(2,1)} %shard_map.267.refs_2_, ...), custom_call_target="tpu_custom_call" | custom-call | flops 1150000000 | bytes 65536 | tf_op jit(solution)/shard_map/pallas_call | solution.py:156
  433.8 2.4 collective-permute-start.58
  436.2 14.2 %collective-permute-done.48.refs_3_ = bf16[256,1664]{1,0:T(8,128)(2,1)S(1)} collective-permute-done((bf16[256,1664]{1,0:T(8,128)(2,1)S(1)}, bf16[256,1664]{1,0:T(8,128)(2,1)S(1)}, u32[]{:S(2)}, u32[]{:S(2)}) %collective-permute-start.48) | collective-permute-done | bytes 852000 | tf_op jit(solution)/shard_map/ppermute | solution.py:91
  450.4 3.5 collective-permute-start.59
  453.9 14.8 %collective-permute-done.49.refs_4_ = bf16[256,1664]{1,0:T(8,128)(2,1)S(1)} collective-permute-done((bf16[256,1664]{1,0:T(8,128)(2,1)S(1)}, bf16[256,1664]{1,0:T(8,128)(2,1)S(1)}, u32[]{:S(2)}, u32[]{:S(2)}) %collective-permute-start.49) | collective-permute-done | bytes 852000 | tf_op jit(solution)/shard_map/ppermute | solution.py:91
  470.0 3.9 shard_map.291
  473.9 28.8 %shard_map.292 = (bf16[2048,384]{1,0:T(8,128)(2,1)}, f32[1,384]{1,0:T(1,128)}) custom-call(s32[16]{0:T(128)} %select_reduce_fusion.refs_0_, bf16[256,1664]{1,0:T(8,128)(2,1)} %get-tuple-element.119.refs_1_.refs_0_.refs_2_, bf16[256,1664]{1,0:T(8,128)(2,1)} %collective-permute-done.51.refs_2_.refs_1_, bf16[256,1664]{1,0:T(8,128)(2,1)} %copy-done.16, ...), custom_call_target="tpu_custom_call" | custom-call | flops 32199999488 | bytes 65536 | tf_op jit(solution)/shard_map/pallas_call | solution.py:156
  504.1 3.2 shard_map.293.refs_12_.refs_3_
  507.2 7.6 %shard_map.294 = (bf16[128,1664]{1,0:T(8,128)(2,1)}, bf16[128,1664]{1,0:T(8,128)(2,1)}, bf16[128,1664]{1,0:T(8,128)(2,1)}, bf16[128,1664]{1,0:T(8,128)(2,1)}) custom-call(s32[4]{0:T(128)} %get-tuple-element.190.refs_0_, bf16[2048,384]{1,0:T(8,128)(2,1)} %get-tuple-element.129.refs_4_.refs_1_, bf16[256,1664]{1,0:T(8,128)(2,1)} %shard_map.267.refs_2_, ...), custom_call_target="tpu_custom_call" | custom-call | flops 1150000000 | bytes 65536 | tf_op jit(solution)/shard_map/pallas_call | solution.py:156
  516.5 8.0 %shard_map.295 = (bf16[256,1664]{1,0:T(8,128)(2,1)}, bf16[256,1664]{1,0:T(8,128)(2,1)}, bf16[256,1664]{1,0:T(8,128)(2,1)}, bf16[256,1664]{1,0:T(8,128)(2,1)}) custom-call(bf16[2048,384]{1,0:T(8,128)(2,1)} %get-tuple-element.125.refs_11_.refs_1_.refs_0_, bf16[2048,384]{1,0:T(8,128)(2,1)} %get-tuple-element.129.refs_4_.refs_1_, ...), custom_call_target="tpu_custom_call" | custom-call | flops 1150000000 | bytes 65536 | tf_op jit(solution)/shard_map/pallas_call | solution.py:330
  525.6 20.4 %collective-permute-done.70.refs_5_ = bf16[224,1664]{1,0:T(8,128)(2,1)} collective-permute-done((bf16[224,1664]{1,0:T(8,128)(2,1)}, bf16[224,1664]{1,0:T(8,128)(2,1)}, u32[]{:S(2)}, u32[]{:S(2)}) %collective-permute-start.70) | collective-permute-done | bytes 745504 | tf_op jit(solution)/shard_map/ppermute | solution.py:91
  546.1 8.7 %collective-permute-start.67 = (bf16[128,1664]{1,0:T(8,128)(2,1)}, bf16[128,1664]{1,0:T(8,128)(2,1)}, u32[]{:S(2)}, u32[]{:S(2)}) collective-permute-start(bf16[128,1664]{1,0:T(8,128)(2,1)} %get-tuple-element.144), channel_id=1, source_target_pairs={{0,8},{8,16},{16,24},{24,0},{1,9},{9,17},{17,25},{25,1},{2,10},{10... | collective-permute-start | bytes 1277960 | tf_op jit(solution)/shard_map/ppermute | solution.py:130
  556.1 2.5 collective-permute-start.68
  561.8 9.3 %shard_map.296 = (bf16[256,1664]{1,0:T(8,128)(2,1)}, bf16[256,1664]{1,0:T(8,128)(2,1)}, bf16[256,1664]{1,0:T(8,128)(2,1)}, bf16[256,1664]{1,0:T(8,128)(2,1)}) custom-call(bf16[2048,384]{1,0:T(8,128)(2,1)} %get-tuple-element.125.refs_11_.refs_1_.refs_0_, bf16[2048,384]{1,0:T(8,128)(2,1)} %get-tuple-element.129.refs_4_.refs_1_, ...), custom_call_target="tpu_custom_call" | custom-call | flops 1150000000 | bytes 65536 | tf_op jit(solution)/shard_map/pallas_call | solution.py:330
  572.2 2.4 collective-permute-start.66
  574.7 10.2 %collective-permute-done.68.refs_9_ = bf16[128,1664]{1,0:T(8,128)(2,1)} collective-permute-done((bf16[128,1664]{1,0:T(8,128)(2,1)}, bf16[128,1664]{1,0:T(8,128)(2,1)}, u32[]{:S(2)}, u32[]{:S(2)}) %collective-permute-start.68) | collective-permute-done | bytes 426016 | tf_op jit(solution)/shard_map/ppermute | solution.py:130
  587.3 8.2 %shard_map.299.refs_11_ = f32[400,6400]{1,0:T(8,128)} custom-call(s32[1]{0:T(128)} %constant.103.clone.1.at_ref, bf16[8,400,896]{2,1,0:T(8,128)(2,1)} %bitcast.31), custom_call_target="tpu_custom_call" | custom-call | flops 1150000000 | bytes 65536 | tf_op jit(solution)/shard_map/pallas_call | solution.py:561
  598.6 8.1 %collective-permute-done.64.refs_4_ = bf16[256,1664]{1,0:T(8,128)(2,1)S(1)} collective-permute-done((bf16[256,1664]{1,0:T(8,128)(2,1)}, bf16[256,1664]{1,0:T(8,128)(2,1)S(1)}, u32[]{:S(2)}, u32[]{:S(2)}) %collective-permute-start.64) | collective-permute-done | bytes 852000 | tf_op jit(solution)/shard_map/ppermute | solution.py:91
  606.7 21.5 %collective-permute-done.66.refs_6_ = bf16[256,1664]{1,0:T(8,128)(2,1)S(1)} collective-permute-done((bf16[256,1664]{1,0:T(8,128)(2,1)}, bf16[256,1664]{1,0:T(8,128)(2,1)S(1)}, u32[]{:S(2)}, u32[]{:S(2)}) %collective-permute-start.66) | collective-permute-done | bytes 852000 | tf_op jit(solution)/shard_map/ppermute | solution.py:91
  629.2 6.2 shard_map.300
  636.4 6.8 collective-permute-done.78.refs_4_
  646.4 3.2 collective-permute-done.74
  651.2 5.5 collective-permute-done.75
  656.8 4.7 collective-permute-done.76
  665.5 2.2 collective-permute-done.77
  670.5 7.0 collective-permute-done.84.refs_14_.refs_0_
  682.3 3.0 collective-permute-done.86.refs_16_
  686.1 8.1 %shard_map.303 = f32[1600,1600]{1,0:T(8,128)} custom-call(bf16[8,208,1664]{2,1,0:T(8,128)(2,1)} %bitcast.41, bf16[128,1664]{1,0:T(8,128)(2,1)} %copy-done.54, bf16[128,1664]{1,0:T(8,128)(2,1)} %copy-done.55), custom_call_target="tpu_custom_call" | custom-call | flops 9200000000 | bytes 65536 | tf_op jit(solution)/shard_map/pallas_call | solution.py:538
  696.2 9.2 %shard_map.301 = (f32[1200,1600]{1,0:T(8,128)}, f32[400,1600]{1,0:T(8,128)}) custom-call(s32[2]{0:T(128)} %pad_add_fusion.1.refs_0_, s32[2400]{0:T(1024)} %constant.111.clone.refs_1_, s32[64]{0:T(128)} %constant.112.clone.refs_2_, bf16[224,1664]{1,0:T(8,128)(2,1)} %shard_map.293.refs_12_.refs_3_, bf16[224,1664]{1,0:T(8,128)(2,1)} %collective-permute-done.78.refs_4_, ...), custom_call_target="tpu_custom_call" | custom-call | flops 9200000000 | bytes 65536 | tf_op jit(solution)/shard_map/pallas_call | solution.py:156
  (421 shorter events, 127.0 us)
Async XLA Ops:
  7.2 80.8 %all-gather.9.cloned.1.call-start = ((), (), s32[]{:S(2)}) async-start(), calls=%async_computation.2 | async-start | bytes 2129920 | tf_op jit(solution)/shard_map/all_gather | solution.py:767
  14.6 103.5 %all-gather.11.cloned.1.call-start = ((), (), s32[]{:S(2)}) async-start(), calls=%async_computation.3 | async-start | bytes 3461120 | tf_op jit(solution)/shard_map/all_gather | solution.py:767
  24.4 149.9 %all-gather.13.cloned.1.call-start = ((), (), s32[]{:S(2)}) async-start(), calls=%async_computation.4 | async-start | bytes 3584000 | tf_op jit(solution)/shard_map/all_gather | solution.py:767
  24.4 22.2 %collective-permute-start.1 = (bf16[256,1664]{1,0:T(8,128)(2,1)}, bf16[256,1664]{1,0:T(8,128)(2,1)S(1)}, u32[]{:S(2)}, u32[]{:S(2)}) collective-permute-start(bf16[256,1664]{1,0:T(8,128)(2,1)} %shard_map.267.refs_2_), channel_id=1, source_target_pairs={{0,4},{1,5},{2,6},{3,7},{4,0},{5,1},{6,2},{7,3},{8,12},{9,13},{10,... | collective-permute-start | bytes 2555912 | tf_op jit(solution)/shard_map/ppermute | solution.py:91
  27.5 32.2 %collective-permute-start = (bf16[256,1664]{1,0:T(8,128)(2,1)}, bf16[256,1664]{1,0:T(8,128)(2,1)S(1)}, u32[]{:S(2)}, u32[]{:S(2)}) collective-permute-start(bf16[256,1664]{1,0:T(8,128)(2,1)} %shard_map.267.refs_2_), channel_id=1, source_target_pairs={{0,2},{1,3},{2,0},{3,1},{4,6},{5,7},{6,4},{7,5},{8,10},{9,11},{10,... | collective-permute-start | bytes 2555912 | tf_op jit(solution)/shard_map/ppermute | solution.py:91
  57.9 36.4 %collective-permute-start.4 = (bf16[256,1664]{1,0:T(8,128)(2,1)}, bf16[256,1664]{1,0:T(8,128)(2,1)}, u32[]{:S(2)}, u32[]{:S(2)}) collective-permute-start(bf16[256,1664]{1,0:T(8,128)(2,1)} %shard_map.267.refs_2_), channel_id=1, source_target_pairs={{0,1},{1,0},{2,3},{3,2},{4,5},{5,4},{6,7},{7,6},{8,9},{9,8},{10,11... | collective-permute-start | bytes 2555912 | tf_op jit(solution)/shard_map/ppermute | solution.py:91
  64.9 20.8 %collective-permute-start.9 = (bf16[256,1664]{1,0:T(8,128)(2,1)}, bf16[256,1664]{1,0:T(8,128)(2,1)S(1)}, u32[]{:S(2)}, u32[]{:S(2)}) collective-permute-start(bf16[256,1664]{1,0:T(8,128)(2,1)} %shard_map.270.refs_0_), channel_id=1, source_target_pairs={{0,2},{1,3},{2,0},{3,1},{4,6},{5,7},{6,4},{7,5},{8,10},{9,11},{10,... | collective-permute-start | bytes 2555912 | tf_op jit(solution)/shard_map/ppermute | solution.py:91
  67.2 28.7 %collective-permute-start.5 = (bf16[256,1664]{1,0:T(8,128)(2,1)S(1)}, bf16[256,1664]{1,0:T(8,128)(2,1)}, u32[]{:S(2)}, u32[]{:S(2)}) collective-permute-start(bf16[256,1664]{1,0:T(8,128)(2,1)S(1)} %collective-permute-done.refs_3_), channel_id=1, source_target_pairs={{0,1},{1,0},{2,3},{3,2},{4,5},{5,4},{6,7},{7,6},{8,9},{9,8},{10,11... | collective-permute-start | bytes 2555912 | tf_op jit(solution)/shard_map/ppermute | solution.py:91
  67.3 28.6 %collective-permute-start.6 = (bf16[256,1664]{1,0:T(8,128)(2,1)S(1)}, bf16[256,1664]{1,0:T(8,128)(2,1)}, u32[]{:S(2)}, u32[]{:S(2)}) collective-permute-start(bf16[256,1664]{1,0:T(8,128)(2,1)S(1)} %collective-permute-done.1.refs_4_), channel_id=1, source_target_pairs={{0,1},{1,0},{2,3},{3,2},{4,5},{5,4},{6,7},{7,6},{8,9},{9,8},{10,11... | collective-permute-start | bytes 2555912 | tf_op jit(solution)/shard_map/ppermute | solution.py:91
  72.6 20.2 %collective-permute-start.10 = (bf16[256,1664]{1,0:T(8,128)(2,1)}, bf16[256,1664]{1,0:T(8,128)(2,1)S(1)}, u32[]{:S(2)}, u32[]{:S(2)}) collective-permute-start(bf16[256,1664]{1,0:T(8,128)(2,1)} %shard_map.270.refs_0_), channel_id=1, source_target_pairs={{0,4},{1,5},{2,6},{3,7},{4,0},{5,1},{6,2},{7,3},{8,12},{9,13},{10,... | collective-permute-start | bytes 2555912 | tf_op jit(solution)/shard_map/ppermute | solution.py:91
  92.5 154.5 %all-gather.15.cloned.1.call-start = ((), (), s32[]{:S(2)}) async-start(), calls=%async_computation.5 | async-start | bytes 3461120 | tf_op jit(solution)/shard_map/all_gather | solution.py:767
  92.8 24.3 %collective-permute-start.11 = (bf16[128,1664]{1,0:T(8,128)(2,1)S(1)}, bf16[128,1664]{1,0:T(8,128)(2,1)S(1)}, u32[]{:S(2)}, u32[]{:S(2)}) collective-permute-start(bf16[128,1664]{1,0:T(8,128)(2,1)S(1)} %slice.155), channel_id=1, source_target_pairs={{0,4},{1,5},{2,6},{3,7},{4,0},{5,1},{6,2},{7,3},{8,12},{9,13},{10,... | collective-permute-start | bytes 1277960 | tf_op jit(solution)/shard_map/ppermute | solution.py:91
  94.3 22.9 %collective-permute-start.12 = (bf16[128,1664]{1,0:T(8,128)(2,1)S(1)}, bf16[128,1664]{1,0:T(8,128)(2,1)S(1)}, u32[]{:S(2)}, u32[]{:S(2)}) collective-permute-start(bf16[128,1664]{1,0:T(8,128)(2,1)S(1)} %slice.156), channel_id=1, source_target_pairs={{0,2},{1,3},{2,0},{3,1},{4,6},{5,7},{6,4},{7,5},{8,10},{9,11},{10,... | collective-permute-start | bytes 1277960 | tf_op jit(solution)/shard_map/ppermute | solution.py:91
  152.9 274.7 %reduce-scatter.3.cloned.1.call-start = ((), (), s32[]{:S(2)}) async-start(), calls=%async_computation.6 | async-start | bytes 3584000 | tf_op jit(solution)/shard_map/reduce_scatter | solution.py:849
  153.6 16.2 %collective-permute-start.21 = (bf16[256,1664]{1,0:T(8,128)(2,1)S(1)}, bf16[256,1664]{1,0:T(8,128)(2,1)S(1)}, u32[]{:S(2)}, u32[]{:S(2)}) collective-permute-start(bf16[256,1664]{1,0:T(8,128)(2,1)S(1)} %copy-done.4), channel_id=1, source_target_pairs={{0,1},{1,0},{2,3},{3,2},{4,5},{5,4},{6,7},{7,6},{8,9},{9,8},{10,11... | collective-permute-start | bytes 2555912 | tf_op jit(solution)/shard_map/ppermute | solution.py:91
  154.3 14.8 %collective-permute-start.24 = (bf16[128,1664]{1,0:T(8,128)(2,1)S(1)}, bf16[128,1664]{1,0:T(8,128)(2,1)S(1)}, u32[]{:S(2)}, u32[]{:S(2)}) collective-permute-start(bf16[128,1664]{1,0:T(8,128)(2,1)S(1)} %copy-done.9), channel_id=1, source_target_pairs={{0,1},{1,0},{2,3},{3,2},{4,5},{5,4},{6,7},{7,6},{8,9},{9,8},{10,11... | collective-permute-start | bytes 1277960 | tf_op jit(solution)/shard_map/ppermute | solution.py:91
  155.6 16.3 %collective-permute-start.22 = (bf16[256,1664]{1,0:T(8,128)(2,1)S(1)}, bf16[256,1664]{1,0:T(8,128)(2,1)S(1)}, u32[]{:S(2)}, u32[]{:S(2)}) collective-permute-start(bf16[256,1664]{1,0:T(8,128)(2,1)S(1)} %copy-done.1), channel_id=1, source_target_pairs={{0,1},{1,0},{2,3},{3,2},{4,5},{5,4},{6,7},{7,6},{8,9},{9,8},{10,11... | collective-permute-start | bytes 2555912 | tf_op jit(solution)/shard_map/ppermute | solution.py:91
  158.0 14.8 %collective-permute-start.23 = (bf16[256,1664]{1,0:T(8,128)(2,1)S(1)}, bf16[256,1664]{1,0:T(8,128)(2,1)}, u32[]{:S(2)}, u32[]{:S(2)}) collective-permute-start(bf16[256,1664]{1,0:T(8,128)(2,1)S(1)} %copy-done.3), channel_id=1, source_target_pairs={{0,1},{1,0},{2,3},{3,2},{4,5},{5,4},{6,7},{7,6},{8,9},{9,8},{10,11... | collective-permute-start | bytes 2555912 | tf_op jit(solution)/shard_map/ppermute | solution.py:91
  168.3 22.2 %collective-permute-start.18 = (bf16[256,1664]{1,0:T(8,128)(2,1)}, bf16[256,1664]{1,0:T(8,128)(2,1)}, u32[]{:S(2)}, u32[]{:S(2)}) collective-permute-start(bf16[256,1664]{1,0:T(8,128)(2,1)} %get-tuple-element.92), channel_id=1, source_target_pairs={{0,2},{1,3},{2,0},{3,1},{4,6},{5,7},{6,4},{7,5},{8,10},{9,11},{10,... | collective-permute-start | bytes 2555912 | tf_op jit(solution)/shard_map/ppermute | solution.py:91
  169.0 39.3 %collective-permute-start.19 = (bf16[256,1664]{1,0:T(8,128)(2,1)}, bf16[256,1664]{1,0:T(8,128)(2,1)}, u32[]{:S(2)}, u32[]{:S(2)}) collective-permute-start(bf16[256,1664]{1,0:T(8,128)(2,1)} %get-tuple-element.93), channel_id=1, source_target_pairs={{0,4},{1,5},{2,6},{3,7},{4,0},{5,1},{6,2},{7,3},{8,12},{9,13},{10,... | collective-permute-start | bytes 2555912 | tf_op jit(solution)/shard_map/ppermute | solution.py:91
  169.8 38.5 %collective-permute-start.20 = (bf16[256,1664]{1,0:T(8,128)(2,1)}, bf16[256,1664]{1,0:T(8,128)(2,1)S(1)}, u32[]{:S(2)}, u32[]{:S(2)}) collective-permute-start(bf16[256,1664]{1,0:T(8,128)(2,1)} %get-tuple-element.94), channel_id=1, source_target_pairs={{0,6},{1,7},{2,4},{3,5},{4,2},{5,3},{6,0},{7,1},{8,14},{9,15},{10,... | collective-permute-start | bytes 2555912 | tf_op jit(solution)/shard_map/ppermute | solution.py:91
  213.6 20.2 %collective-permute-start.25 = (bf16[256,1664]{1,0:T(8,128)(2,1)}, bf16[256,1664]{1,0:T(8,128)(2,1)S(1)}, u32[]{:S(2)}, u32[]{:S(2)}) collective-permute-start(bf16[256,1664]{1,0:T(8,128)(2,1)} %get-tuple-element.100.refs_0_.refs_1_), channel_id=1, source_target_pairs={{0,2},{1,3},{2,0},{3,1},{4,6},{5,7},{6,4},{7,5},{8,10},{9,11},{10,... | collective-permute-start | bytes 2555912 | tf_op jit(solution)/shard_map/ppermute | solution.py:91
  215.0 20.2 %collective-permute-start.26 = (bf16[256,1664]{1,0:T(8,128)(2,1)}, bf16[256,1664]{1,0:T(8,128)(2,1)S(1)}, u32[]{:S(2)}, u32[]{:S(2)}) collective-permute-start(bf16[256,1664]{1,0:T(8,128)(2,1)} %get-tuple-element.100.refs_0_.refs_1_), channel_id=1, source_target_pairs={{0,4},{1,5},{2,6},{3,7},{4,0},{5,1},{6,2},{7,3},{8,12},{9,13},{10,... | collective-permute-start | bytes 2555912 | tf_op jit(solution)/shard_map/ppermute | solution.py:91
  215.7 31.2 %collective-permute-start.29 = (bf16[256,1664]{1,0:T(8,128)(2,1)}, bf16[256,1664]{1,0:T(8,128)(2,1)S(1)}, u32[]{:S(2)}, u32[]{:S(2)}) collective-permute-start(bf16[256,1664]{1,0:T(8,128)(2,1)} %get-tuple-element.100.refs_0_.refs_1_), channel_id=1, source_target_pairs={{0,1},{1,0},{2,3},{3,2},{4,5},{5,4},{6,7},{7,6},{8,9},{9,8},{10,11... | collective-permute-start | bytes 2555912 | tf_op jit(solution)/shard_map/ppermute | solution.py:91
  294.6 37.6 %collective-permute-start.42 = (bf16[256,1664]{1,0:T(8,128)(2,1)}, bf16[256,1664]{1,0:T(8,128)(2,1)S(1)}, u32[]{:S(2)}, u32[]{:S(2)}) collective-permute-start(bf16[256,1664]{1,0:T(8,128)(2,1)} %get-tuple-element.116), channel_id=1, source_target_pairs={{0,2},{1,3},{2,0},{3,1},{4,6},{5,7},{6,4},{7,5},{8,10},{9,11},{10,... | collective-permute-start | bytes 2555912 | tf_op jit(solution)/shard_map/ppermute | solution.py:91
  294.9 37.3 %collective-permute-start.43 = (bf16[256,1664]{1,0:T(8,128)(2,1)}, bf16[256,1664]{1,0:T(8,128)(2,1)S(1)}, u32[]{:S(2)}, u32[]{:S(2)}) collective-permute-start(bf16[256,1664]{1,0:T(8,128)(2,1)} %get-tuple-element.117), channel_id=1, source_target_pairs={{0,4},{1,5},{2,6},{3,7},{4,0},{5,1},{6,2},{7,3},{8,12},{9,13},{10,... | collective-permute-start | bytes 2555912 | tf_op jit(solution)/shard_map/ppermute | solution.py:91
  296.3 38.0 %collective-permute-start.44 = (bf16[256,1664]{1,0:T(8,128)(2,1)}, bf16[256,1664]{1,0:T(8,128)(2,1)S(1)}, u32[]{:S(2)}, u32[]{:S(2)}) collective-permute-start(bf16[256,1664]{1,0:T(8,128)(2,1)} %get-tuple-element.118), channel_id=1, source_target_pairs={{0,6},{1,7},{2,4},{3,5},{4,2},{5,3},{6,0},{7,1},{8,14},{9,15},{10,... | collective-permute-start | bytes 2555912 | tf_op jit(solution)/shard_map/ppermute | solution.py:91
  341.3 173.5 %reduce-scatter.5.cloned.1.call-start = ((), (), s32[]{:S(2)}) async-start(), calls=%async_computation.7 | async-start | bytes 3461120 | tf_op jit(solution)/shard_map/reduce_scatter | solution.py:849
  342.5 20.2 %collective-permute-start.45 = (bf16[256,1664]{1,0:T(8,128)(2,1)S(1)}, bf16[256,1664]{1,0:T(8,128)(2,1)S(1)}, u32[]{:S(2)}, u32[]{:S(2)}) collective-permute-start(bf16[256,1664]{1,0:T(8,128)(2,1)S(1)} %copy-done.12), channel_id=1, source_target_pairs={{0,4},{1,5},{2,6},{3,7},{4,0},{5,1},{6,2},{7,3},{8,12},{9,13},{10,... | collective-permute-start | bytes 2555912 | tf_op jit(solution)/shard_map/ppermute | solution.py:91
  343.9 243.5 %all-gather.17.cloned.1.call-start = ((), (), s32[]{:S(2)}) async-start(), calls=%async_computation.8 | async-start | bytes 6451200 | tf_op jit(solution)/shard_map/all_gather | solution.py:862
  343.9 20.2 %collective-permute-start.51 = (bf16[256,1664]{1,0:T(8,128)(2,1)S(1)}, bf16[256,1664]{1,0:T(8,128)(2,1)}, u32[]{:S(2)}, u32[]{:S(2)}) collective-permute-start(bf16[256,1664]{1,0:T(8,128)(2,1)S(1)} %copy-done.12), channel_id=1, source_target_pairs={{0,2},{1,3},{2,0},{3,1},{4,6},{5,7},{6,4},{7,5},{8,10},{9,11},{10,... | collective-permute-start | bytes 2555912 | tf_op jit(solution)/shard_map/ppermute | solution.py:91
  345.2 21.0 %collective-permute-start.38 = (bf16[256,1664]{1,0:T(8,128)(2,1)}, bf16[256,1664]{1,0:T(8,128)(2,1)S(1)}, u32[]{:S(2)}, u32[]{:S(2)}) collective-permute-start(bf16[256,1664]{1,0:T(8,128)(2,1)} %get-tuple-element.108.refs_9_), channel_id=1, source_target_pairs={{0,1},{1,0},{2,3},{3,2},{4,5},{5,4},{6,7},{7,6},{8,9},{9,8},{10,11... | collective-permute-start | bytes 2555912 | tf_op jit(solution)/shard_map/ppermute | solution.py:91
  345.2 22.4 %collective-permute-start.39 = (bf16[256,1664]{1,0:T(8,128)(2,1)}, bf16[256,1664]{1,0:T(8,128)(2,1)S(1)}, u32[]{:S(2)}, u32[]{:S(2)}) collective-permute-start(bf16[256,1664]{1,0:T(8,128)(2,1)} %get-tuple-element.109), channel_id=1, source_target_pairs={{0,1},{1,0},{2,3},{3,2},{4,5},{5,4},{6,7},{7,6},{8,9},{9,8},{10,11... | collective-permute-start | bytes 2555912 | tf_op jit(solution)/shard_map/ppermute | solution.py:91
  345.7 21.9 %collective-permute-start.40 = (bf16[256,1664]{1,0:T(8,128)(2,1)}, bf16[256,1664]{1,0:T(8,128)(2,1)S(1)}, u32[]{:S(2)}, u32[]{:S(2)}) collective-permute-start(bf16[256,1664]{1,0:T(8,128)(2,1)} %get-tuple-element.110), channel_id=1, source_target_pairs={{0,1},{1,0},{2,3},{3,2},{4,5},{5,4},{6,7},{7,6},{8,9},{9,8},{10,11... | collective-permute-start | bytes 2555912 | tf_op jit(solution)/shard_map/ppermute | solution.py:91
  364.1 15.4 %collective-permute-start.46 = (bf16[128,1664]{1,0:T(8,128)(2,1)S(1)}, bf16[128,1664]{1,0:T(8,128)(2,1)S(1)}, u32[]{:S(2)}, u32[]{:S(2)}) collective-permute-start(bf16[128,1664]{1,0:T(8,128)(2,1)S(1)} %slice.162), channel_id=1, source_target_pairs={{0,2},{1,3},{2,0},{3,1},{4,6},{5,7},{6,4},{7,5},{8,10},{9,11},{10,... | collective-permute-start | bytes 1277960 | tf_op jit(solution)/shard_map/ppermute | solution.py:91
  366.2 14.5 %collective-permute-start.52 = (bf16[128,1664]{1,0:T(8,128)(2,1)}, bf16[128,1664]{1,0:T(8,128)(2,1)}, u32[]{:S(2)}, u32[]{:S(2)}) collective-permute-start(bf16[128,1664]{1,0:T(8,128)(2,1)} %slice.163), channel_id=1, source_target_pairs={{0,4},{1,5},{2,6},{3,7},{4,0},{5,1},{6,2},{7,3},{8,12},{9,13},{10,... | collective-permute-start | bytes 1277960 | tf_op jit(solution)/shard_map/ppermute | solution.py:91
  367.6 15.7 %collective-permute-start.53 = (bf16[256,1664]{1,0:T(8,128)(2,1)S(1)}, bf16[256,1664]{1,0:T(8,128)(2,1)}, u32[]{:S(2)}, u32[]{:S(2)}) collective-permute-start(bf16[256,1664]{1,0:T(8,128)(2,1)S(1)} %copy-done.12), channel_id=1, source_target_pairs={{0,1},{1,0},{2,3},{3,2},{4,5},{5,4},{6,7},{7,6},{8,9},{9,8},{10,11... | collective-permute-start | bytes 2555912 | tf_op jit(solution)/shard_map/ppermute | solution.py:91
  367.6 15.7 %collective-permute-start.54 = (bf16[256,1664]{1,0:T(8,128)(2,1)}, bf16[256,1664]{1,0:T(8,128)(2,1)}, u32[]{:S(2)}, u32[]{:S(2)}) collective-permute-start(bf16[256,1664]{1,0:T(8,128)(2,1)} %collective-permute-done.51.refs_2_.refs_1_), channel_id=1, source_target_pairs={{0,1},{1,0},{2,3},{3,2},{4,5},{5,4},{6,7},{7,6},{8,9},{9,8},{10,11... | collective-permute-start | bytes 2555912 | tf_op jit(solution)/shard_map/ppermute | solution.py:91
  368.1 15.2 %collective-permute-start.55 = (bf16[256,1664]{1,0:T(8,128)(2,1)S(1)}, bf16[256,1664]{1,0:T(8,128)(2,1)}, u32[]{:S(2)}, u32[]{:S(2)}) collective-permute-start(bf16[256,1664]{1,0:T(8,128)(2,1)S(1)} %collective-permute-done.45.refs_3_.refs_2_), channel_id=1, source_target_pairs={{0,1},{1,0},{2,3},{3,2},{4,5},{5,4},{6,7},{7,6},{8,9},{9,8},{10,11... | collective-permute-start | bytes 2555912 | tf_op jit(solution)/shard_map/ppermute | solution.py:91
  427.6 258.5 %all-gather.19.cloned.1.call-start = ((), (), s32[]{:S(2)}) async-start(), calls=%async_computation.9 | async-start | bytes 6230016 | tf_op jit(solution)/shard_map/all_gather | solution.py:862
  428.7 21.7 %collective-permute-start.48 = (bf16[256,1664]{1,0:T(8,128)(2,1)S(1)}, bf16[256,1664]{1,0:T(8,128)(2,1)S(1)}, u32[]{:S(2)}, u32[]{:S(2)}) collective-permute-start(bf16[256,1664]{1,0:T(8,128)(2,1)S(1)} %copy-done.42), channel_id=1, source_target_pairs={{0,2},{1,3},{2,0},{3,1},{4,6},{5,7},{6,4},{7,5},{8,10},{9,11},{10,... | collective-permute-start | bytes 2555912 | tf_op jit(solution)/shard_map/ppermute | solution.py:91
  429.5 39.3 %collective-permute-start.49 = (bf16[256,1664]{1,0:T(8,128)(2,1)S(1)}, bf16[256,1664]{1,0:T(8,128)(2,1)S(1)}, u32[]{:S(2)}, u32[]{:S(2)}) collective-permute-start(bf16[256,1664]{1,0:T(8,128)(2,1)S(1)} %copy-done.43), channel_id=1, source_target_pairs={{0,4},{1,5},{2,6},{3,7},{4,0},{5,1},{6,2},{7,3},{8,12},{9,13},{10,... | collective-permute-start | bytes 2555912 | tf_op jit(solution)/shard_map/ppermute | solution.py:91
  431.0 37.8 %collective-permute-start.50 = (bf16[256,1664]{1,0:T(8,128)(2,1)S(1)}, bf16[256,1664]{1,0:T(8,128)(2,1)S(1)}, u32[]{:S(2)}, u32[]{:S(2)}) collective-permute-start(bf16[256,1664]{1,0:T(8,128)(2,1)S(1)} %copy-done.44), channel_id=1, source_target_pairs={{0,6},{1,7},{2,4},{3,5},{4,2},{5,3},{6,0},{7,1},{8,14},{9,15},{10,... | collective-permute-start | bytes 2555912 | tf_op jit(solution)/shard_map/ppermute | solution.py:91
  432.2 70.5 %collective-permute-start.57 = (bf16[224,1664]{1,0:T(8,128)(2,1)}, bf16[224,1664]{1,0:T(8,128)(2,1)S(1)}, u32[]{:S(2)}, u32[]{:S(2)}) collective-permute-start(bf16[224,1664]{1,0:T(8,128)(2,1)} %get-tuple-element.132), channel_id=1, source_target_pairs={{0,8},{8,16},{16,24},{24,0},{1,9},{9,17},{17,25},{25,1},{2,10},{10... | collective-permute-start | bytes 2236424 | tf_op jit(solution)/shard_map/ppermute | solution.py:130
  433.8 68.9 %collective-permute-start.58 = (bf16[224,1664]{1,0:T(8,128)(2,1)}, bf16[224,1664]{1,0:T(8,128)(2,1)S(1)}, u32[]{:S(2)}, u32[]{:S(2)}) collective-permute-start(bf16[224,1664]{1,0:T(8,128)(2,1)} %get-tuple-element.133), channel_id=1, source_target_pairs={{0,16},{8,24},{16,0},{24,8},{1,17},{9,25},{17,1},{25,9},{2,18},{10... | collective-permute-start | bytes 2236424 | tf_op jit(solution)/shard_map/ppermute | solution.py:130
  450.4 52.3 %collective-permute-start.59 = (bf16[224,1664]{1,0:T(8,128)(2,1)}, bf16[224,1664]{1,0:T(8,128)(2,1)S(1)}, u32[]{:S(2)}, u32[]{:S(2)}) collective-permute-start(bf16[224,1664]{1,0:T(8,128)(2,1)} %get-tuple-element.134), channel_id=1, source_target_pairs={{0,24},{8,0},{16,8},{24,16},{1,25},{9,1},{17,9},{25,17},{2,26},{10... | collective-permute-start | bytes 2236424 | tf_op jit(solution)/shard_map/ppermute | solution.py:130
  514.9 31.2 %collective-permute-start.70 = (bf16[224,1664]{1,0:T(8,128)(2,1)}, bf16[224,1664]{1,0:T(8,128)(2,1)}, u32[]{:S(2)}, u32[]{:S(2)}) collective-permute-start(bf16[224,1664]{1,0:T(8,128)(2,1)} %shard_map.293.refs_12_.refs_3_), channel_id=1, source_target_pairs={{0,4},{1,5},{2,6},{3,7},{4,0},{5,1},{6,2},{7,3},{8,12},{9,13},{10,... | collective-permute-start | bytes 2236424 | tf_op jit(solution)/shard_map/ppermute | solution.py:91
  524.6 31.4 %collective-permute-start.60 = (bf16[256,1664]{1,0:T(8,128)(2,1)}, bf16[256,1664]{1,0:T(8,128)(2,1)S(1)}, u32[]{:S(2)}, u32[]{:S(2)}) collective-permute-start(bf16[256,1664]{1,0:T(8,128)(2,1)} %get-tuple-element.136), channel_id=1, source_target_pairs={{0,1},{1,0},{2,3},{3,2},{4,5},{5,4},{6,7},{7,6},{8,9},{9,8},{10,11... | collective-permute-start | bytes 2555912 | tf_op jit(solution)/shard_map/ppermute | solution.py:91
  524.6 34.0 %collective-permute-start.61 = (bf16[256,1664]{1,0:T(8,128)(2,1)}, bf16[256,1664]{1,0:T(8,128)(2,1)S(1)}, u32[]{:S(2)}, u32[]{:S(2)}) collective-permute-start(bf16[256,1664]{1,0:T(8,128)(2,1)} %get-tuple-element.137), channel_id=1, source_target_pairs={{0,1},{1,0},{2,3},{3,2},{4,5},{5,4},{6,7},{7,6},{8,9},{9,8},{10,11... | collective-permute-start | bytes 2555912 | tf_op jit(solution)/shard_map/ppermute | solution.py:91
  525.1 34.9 %collective-permute-start.62 = (bf16[256,1664]{1,0:T(8,128)(2,1)}, bf16[256,1664]{1,0:T(8,128)(2,1)S(1)}, u32[]{:S(2)}, u32[]{:S(2)}) collective-permute-start(bf16[256,1664]{1,0:T(8,128)(2,1)} %get-tuple-element.138), channel_id=1, source_target_pairs={{0,1},{1,0},{2,3},{3,2},{4,5},{5,4},{6,7},{7,6},{8,9},{9,8},{10,11... | collective-permute-start | bytes 2555912 | tf_op jit(solution)/shard_map/ppermute | solution.py:91
  525.1 34.9 %collective-permute-start.63 = (bf16[256,1664]{1,0:T(8,128)(2,1)}, bf16[256,1664]{1,0:T(8,128)(2,1)S(1)}, u32[]{:S(2)}, u32[]{:S(2)}) collective-permute-start(bf16[256,1664]{1,0:T(8,128)(2,1)} %get-tuple-element.139), channel_id=1, source_target_pairs={{0,1},{1,0},{2,3},{3,2},{4,5},{5,4},{6,7},{7,6},{8,9},{9,8},{10,11... | collective-permute-start | bytes 2555912 | tf_op jit(solution)/shard_map/ppermute | solution.py:91
  546.1 26.2 %collective-permute-start.67 = (bf16[128,1664]{1,0:T(8,128)(2,1)}, bf16[128,1664]{1,0:T(8,128)(2,1)}, u32[]{:S(2)}, u32[]{:S(2)}) collective-permute-start(bf16[128,1664]{1,0:T(8,128)(2,1)} %get-tuple-element.144), channel_id=1, source_target_pairs={{0,8},{8,16},{16,24},{24,0},{1,9},{9,17},{17,25},{25,1},{2,10},{10... | collective-permute-start | bytes 1277960 | tf_op jit(solution)/shard_map/ppermute | solution.py:130
  556.1 28.8 %collective-permute-start.68 = (bf16[128,1664]{1,0:T(8,128)(2,1)}, bf16[128,1664]{1,0:T(8,128)(2,1)}, u32[]{:S(2)}, u32[]{:S(2)}) collective-permute-start(bf16[128,1664]{1,0:T(8,128)(2,1)} %get-tuple-element.145), channel_id=1, source_target_pairs={{0,16},{8,24},{16,0},{24,8},{1,17},{9,25},{17,1},{25,9},{2,18},{10... | collective-permute-start | bytes 1277960 | tf_op jit(solution)/shard_map/ppermute | solution.py:130
  558.6 28.3 %collective-permute-start.71 = (bf16[112,1664]{1,0:T(8,128)(2,1)S(1)}, bf16[112,1664]{1,0:T(8,128)(2,1)}, u32[]{:S(2)}, u32[]{:S(2)}) collective-permute-start(bf16[112,1664]{1,0:T(8,128)(2,1)S(1)} %slice.164), channel_id=1, source_target_pairs={{0,2},{1,3},{2,0},{3,1},{4,6},{5,7},{6,4},{7,5},{8,10},{9,11},{10,... | collective-permute-start | bytes 1118216 | tf_op jit(solution)/shard_map/ppermute | solution.py:91
  571.1 35.6 %collective-permute-start.64 = (bf16[256,1664]{1,0:T(8,128)(2,1)}, bf16[256,1664]{1,0:T(8,128)(2,1)S(1)}, u32[]{:S(2)}, u32[]{:S(2)}) collective-permute-start(bf16[256,1664]{1,0:T(8,128)(2,1)} %get-tuple-element.141), channel_id=1, source_target_pairs={{0,2},{1,3},{2,0},{3,1},{4,6},{5,7},{6,4},{7,5},{8,10},{9,11},{10,... | collective-permute-start | bytes 2555912 | tf_op jit(solution)/shard_map/ppermute | solution.py:91
  571.7 35.0 %collective-permute-start.65 = (bf16[256,1664]{1,0:T(8,128)(2,1)}, bf16[256,1664]{1,0:T(8,128)(2,1)S(1)}, u32[]{:S(2)}, u32[]{:S(2)}) collective-permute-start(bf16[256,1664]{1,0:T(8,128)(2,1)} %get-tuple-element.142), channel_id=1, source_target_pairs={{0,4},{1,5},{2,6},{3,7},{4,0},{5,1},{6,2},{7,3},{8,12},{9,13},{10,... | collective-permute-start | bytes 2555912 | tf_op jit(solution)/shard_map/ppermute | solution.py:91
  572.2 56.0 %collective-permute-start.66 = (bf16[256,1664]{1,0:T(8,128)(2,1)}, bf16[256,1664]{1,0:T(8,128)(2,1)S(1)}, u32[]{:S(2)}, u32[]{:S(2)}) collective-permute-start(bf16[256,1664]{1,0:T(8,128)(2,1)} %get-tuple-element.143), channel_id=1, source_target_pairs={{0,6},{1,7},{2,4},{3,5},{4,2},{5,3},{6,0},{7,1},{8,14},{9,15},{10,... | collective-permute-start | bytes 2555912 | tf_op jit(solution)/shard_map/ppermute | solution.py:91
  597.1 46.1 %collective-permute-start.78 = (bf16[224,1664]{1,0:T(8,128)(2,1)}, bf16[224,1664]{1,0:T(8,128)(2,1)}, u32[]{:S(2)}, u32[]{:S(2)}) collective-permute-start(bf16[224,1664]{1,0:T(8,128)(2,1)} %shard_map.293.refs_12_.refs_3_), channel_id=1, source_target_pairs={{0,2},{1,3},{2,0},{3,1},{4,6},{5,7},{6,4},{7,5},{8,10},{9,11},{10,... | collective-permute-start | bytes 2236424 | tf_op jit(solution)/shard_map/ppermute | solution.py:91
  644.2 23.5 %collective-permute-start.79 = (bf16[112,1664]{1,0:T(8,128)(2,1)S(1)}, bf16[112,1664]{1,0:T(8,128)(2,1)}, u32[]{:S(2)}, u32[]{:S(2)}) collective-permute-start(bf16[112,1664]{1,0:T(8,128)(2,1)S(1)} %slice.168), channel_id=1, source_target_pairs={{0,4},{1,5},{2,6},{3,7},{4,0},{5,1},{6,2},{7,3},{8,12},{9,13},{10,... | collective-permute-start | bytes 1118216 | tf_op jit(solution)/shard_map/ppermute | solution.py:91
  646.4 32.8 %collective-permute-start.80 = (bf16[224,1664]{1,0:T(8,128)(2,1)}, bf16[224,1664]{1,0:T(8,128)(2,1)}, u32[]{:S(2)}, u32[]{:S(2)}) collective-permute-start(bf16[224,1664]{1,0:T(8,128)(2,1)} %shard_map.293.refs_12_.refs_3_), channel_id=1, source_target_pairs={{0,1},{1,0},{2,3},{3,2},{4,5},{5,4},{6,7},{7,6},{8,9},{9,8},{10,11... | collective-permute-start | bytes 2236424 | tf_op jit(solution)/shard_map/ppermute | solution.py:91
  663.4 18.2 %collective-permute-start.81 = (bf16[224,1664]{1,0:T(8,128)(2,1)}, bf16[224,1664]{1,0:T(8,128)(2,1)}, u32[]{:S(2)}, u32[]{:S(2)}) collective-permute-start(bf16[224,1664]{1,0:T(8,128)(2,1)} %collective-permute-done.78.refs_4_), channel_id=1, source_target_pairs={{0,1},{1,0},{2,3},{3,2},{4,5},{5,4},{6,7},{7,6},{8,9},{9,8},{10,11... | collective-permute-start | bytes 2236424 | tf_op jit(solution)/shard_map/ppermute | solution.py:91
  663.4 18.2 %collective-permute-start.82 = (bf16[224,1664]{1,0:T(8,128)(2,1)}, bf16[224,1664]{1,0:T(8,128)(2,1)}, u32[]{:S(2)}, u32[]{:S(2)}) collective-permute-start(bf16[224,1664]{1,0:T(8,128)(2,1)} %collective-permute-done.70.refs_5_), channel_id=1, source_target_pairs={{0,1},{1,0},{2,3},{3,2},{4,5},{5,4},{6,7},{7,6},{8,9},{9,8},{10,11... | collective-permute-start | bytes 2236424 | tf_op jit(solution)/shard_map/ppermute | solution.py:91
  681.7 12.6 %collective-permute-start.88 = (bf16[128,1664]{1,0:T(8,128)(2,1)}, bf16[128,1664]{1,0:T(8,128)(2,1)S(1)}, u32[]{:S(2)}, u32[]{:S(2)}) collective-permute-start(bf16[128,1664]{1,0:T(8,128)(2,1)} %get-tuple-element.154.refs_13_), channel_id=1, source_target_pairs={{0,1},{1,0},{2,3},{3,2},{4,5},{5,4},{6,7},{7,6},{8,9},{9,8},{10,11... | collective-permute-start | bytes 1277960 | tf_op jit(solution)/shard_map/ppermute | solution.py:91
  681.7 12.7 %collective-permute-start.89 = (bf16[128,1664]{1,0:T(8,128)(2,1)S(1)}, bf16[128,1664]{1,0:T(8,128)(2,1)S(1)}, u32[]{:S(2)}, u32[]{:S(2)}) collective-permute-start(bf16[128,1664]{1,0:T(8,128)(2,1)S(1)} %collective-permute-done.84.refs_14_.refs_0_), channel_id=1, source_target_pairs={{0,1},{1,0},{2,3},{3,2},{4,5},{5,4},{6,7},{7,6},{8,9},{9,8},{10,11... | collective-permute-start | bytes 1277960 | tf_op jit(solution)/shard_map/ppermute | solution.py:91
  (120 other events, 880.4 us)
Sparse Core Ops, SparseCore 0:
  14.7 41.9 all-gather.8
  58.9 56.1 all-gather.10
  116.6 57.6 all-gather.12
  176.2 55.9 all-gather.14
  341.4 56.8 reduce-scatter.2
  400.5 79.4 reduce-scatter.4
  482.1 67.9 all-gather.16
  552.1 61.6 all-gather.18

commit v3 on v2

--- a/solution.py
+++ b/solution.py
@@ -65,8 +65,8 @@
             for z in range(seq_size):
                 for block in range(shard_rows // grain):
                     g, other, inside = owner[z, block]
-                    stride = rows + (0 if g else below)
-                    place = g * ctx_size * (rows + below) + plane.place(other ^ c) * stride + inside
+                    place = plane.place(other ^ c) * (self.groups * rows + below) + inside
+                    place += g * rows + (below if g else 0)
                     self.source[z, c, block] = place // grain
 
 
@@ -90,11 +90,13 @@
     def move(self, value, bits):
         return lax.ppermute(value, "ctx", [(i, i ^ bits) for i in range(self.size)])
 
-    def send(self, value):
+    def send(self, value, order=()):
         if len(self.even) != 4:
             return [value] + [self.move(value, s) for s in self.even[1:]]
         half = value.shape[0] // 2
         first, second = self.move(value, 2), self.move(value, 4)
+        if order:
+            first, second = held([first, second], order)
         return [value, first, second, self.move(first[:half], 4), self.move(second[half:], 2)]
 
     def share(self, near, order=()):
@@ -204,7 +206,7 @@
     return call(copy_kernel, [value], [((rows, padded(width)), value.dtype)], order=order)[0]
 
 
-def pack(share, columns, parts, order=()):
+def pack(share, columns, parts):
     high, width = share.shape
     rows, wide = columns.shape[0] // parts, columns.shape[1]
 
@@ -214,7 +216,7 @@
             out_ref[high:, i * wide : (i + 1) * wide] = columns_ref[i * rows : (i + 1) * rows, :]
 
     shape = (high + rows, padded(width))
-    return call(kernel, [share, columns], [(shape, share.dtype)], order=order)[0]
+    return call(kernel, [share, columns], [(shape, share.dtype)])[0]
 
 
 def unpack(gathered, high, wide, parts, seq_size):
@@ -386,19 +388,16 @@
     )
 
 
-def row_sums(lefts, rights, high, wide, order=(), starts=None, rows=0, margin=0, grain=16, extra=None, micros=1):
+def row_sums(lefts, rights, high, wide, order=(), starts=None, rows=0, margin=0, grain=16, micros=1):
     length = sum(left.shape[0] for left in lefts)
     cut = starts is not None
-    added = [] if extra is None else [extra]
-    count = starts.shape[0] // (1 + len(added)) if cut else 1
-    below = extra.shape[0] // count if added else 0
+    count = starts.shape[0] if cut else 1
 
     def kernel(*refs):
         if cut:
             starts_ref, *refs = refs
         left_refs, right_refs = refs[: len(lefts)], refs[len(lefts) : len(lefts) + len(rights)]
         scratch = list(refs[len(lefts) + len(rights) :])
-        extra_refs = [scratch.pop(0) for _ in added]
         out_refs = [scratch.pop(0) for _ in range(count)]
         out_ref = scratch.pop() if cut else out_refs[0]
         sides = []
@@ -422,10 +421,7 @@
                 out_ref[margin + high :, :] = nothing
             for i, piece_ref in enumerate(out_refs):
                 at = pl.ds(pl.multiple_of(starts_ref[i], grain), rows)
-                piece_ref[:rows, :] = out_ref[at, :].astype(piece_ref.dtype)
-                for extra_ref in extra_refs:
-                    at = pl.ds(pl.multiple_of(starts_ref[count + i] * below, 16), below)
-                    piece_ref[rows:, :] = extra_ref[at, :]
+                piece_ref[...] = out_ref[at, :].astype(piece_ref.dtype)
 
     scratch = [
         pltpu.VMEM((length, columns), jnp.bfloat16)
@@ -438,51 +434,18 @@
             kernel, [*lefts, *rights], [(shape, jnp.bfloat16)], scratch, order=order, micros=micros
         )[0]
     scratch.append(pltpu.VMEM((high + 2 * margin, padded(wide)), movable(grain)))
-    shapes = [((rows + below, padded(wide)), jnp.bfloat16)] * count
+    shapes = [((rows, padded(wide)), jnp.bfloat16)] * count
     return call(
-        kernel, [starts, *lefts, *rights, *added], shapes, scratch, scalars=1, order=order, micros=micros
-    )
-
-
-def folded_sums(lefts, right, high, blocks, width, order=()):
-    length, wide = right.shape
-    count, parts, rows = blocks
-    step = -(-rows // 32) * 32
-
-    def kernel(*refs):
-        *left_refs, right_ref, out_ref, whole, result = refs
-        for ref, at, here in blocks_of(left_refs):
-            whole[here, :] = ref[at, :high]
-        for start in range(0, high, 256):
-            stop = min(start + 256, high)
-            result[start:stop, :] = contract_first(whole[:, start:stop], right_ref[...]).astype(
-                result.dtype
-            )
-        out_ref[...] = jnp.zeros_like(out_ref)
-        for s in range(count):
-            for i in range(parts):
-                at = (s * parts + i) * rows
-                out_ref[s * step : s * step + rows, i * wide : (i + 1) * wide] = result[
-                    at : at + rows, :
-                ]
-
-    return call(
-        kernel,
-        [*lefts, right],
-        [((count * step, padded(width)), jnp.bfloat16)],
-        [pltpu.VMEM((length, high), jnp.bfloat16), pltpu.VMEM((high, wide), jnp.bfloat16)],
-        order=order,
-        micros=1,
-    )[0]
-
-
-def final_rows(at, sources, places, groups, grain, heads, blocks, wide):
+        kernel, [starts, *lefts, *rights], shapes, scratch, scalars=1, order=order, micros=micros
+    )
+
+
+def final_rows(at, sources, places, pieces, grain, heads, blocks, wide, order=()):
     count = sources.shape[1]
-    heights = [sum(piece.shape[0] for piece in pieces) for pieces in groups]
-    pieces = [piece for group in groups for piece in group]
+    height = sum(piece.shape[0] for piece in pieces)
     _, parts, rows = blocks
     positions = places.shape[1]
-    stride = heights[0] // positions
+    stride = height // positions
 
     def kernel(at_ref, source_ref, place_ref, *refs):
         *piece_refs, qkv_ref, out_ref, whole = refs
@@ -495,7 +458,7 @@
             columns = []
             for p, (skip, used) in enumerate(heads):
                 slot = place_ref[at_ref[1] * positions + p]
-                from_row = pl.ds(pl.multiple_of(slot * stride + 2 * HEAD_DIM, 16), rows)
+                from_row = pl.ds(pl.multiple_of(slot * stride + 2 * HEAD_DIM, math.gcd(stride, 16)), rows)
                 start = i * blocks[0] + skip * HEAD_DIM
                 columns.append(whole[from_row, start : start + used * HEAD_DIM].astype(jnp.float32))
             out_ref[i * rows : (i + 1) * rows, :] = jnp.concatenate(columns, axis=1)
@@ -509,17 +472,38 @@
             *pieces,
         ],
         [((count * grain, wide), jnp.float32), ((parts * rows, wide), jnp.float32)],
-        [pltpu.VMEM((sum(heights), pieces[0].shape[1]), movable(grain))],
+        [pltpu.VMEM((height, pieces[0].shape[1]), movable(grain))],
         scalars=3,
+        order=order,
         micros=8,
     )
 
 
-def last_kernel(tokens_ref, d_resid_ref, gain_ref, *refs, terms):
-    *parts, out_ref, sums_ref, share_ref = refs
-    share_ref[...] = total_of(parts[terms:]).astype(share_ref.dtype)
+def join_shares(early, columns, parts, below, last, order=()):
+    rows, width = last[0].shape
+    high, wide = columns.shape[0] // parts, columns.shape[1]
+    height = (len(early) + 1) * rows + below
+
+    def kernel(*refs):
+        *refs, out_ref = refs
+        early_refs, columns_ref, last_refs = refs[: len(early)], refs[len(early)], refs[len(early) + 1 :]
+        shares = [ref[...] for ref in early_refs] + [total_of(last_refs).astype(out_ref.dtype)]
+        for g, share in enumerate(shares):
+            at = g * rows + (below if g else 0)
+            out_ref[at : at + rows, :] = share
+        out_ref[rows : rows + below, :] = jnp.zeros((below, width), out_ref.dtype)
+        for i in range(parts):
+            out_ref[rows : rows + high, i * wide : (i + 1) * wide] = columns_ref[
+                i * high : (i + 1) * high, :
+            ]
+
+    return call(kernel, [*early, columns, *last], [((height, width), jnp.bfloat16)], order=order)[0]
+
+
+def last_kernel(tokens_ref, d_resid_ref, gain_ref, *refs):
+    *parts, out_ref, sums_ref = refs
     back, d_gain, d_shift = norm_back(
-        tokens_ref[...].astype(jnp.float32), total_of(parts[:terms], gain_ref.shape[1]), gain_ref[...]
+        tokens_ref[...].astype(jnp.float32), total_of(parts, gain_ref.shape[1]), gain_ref[...]
     )
     out_ref[...] = d_resid_ref[...] + back
     sums_ref[0, :] = d_gain
@@ -776,9 +760,9 @@
     out_share = jnp.where(
         used[None, :], lax.dynamic_slice_in_dim(w_out, head_from, window, 1), 0
     )
-    shares[-1] = pack(shares[-1], out_share, 5, [normed1])
+    shares[0] = pack(shares[0], out_share, 5)
     qkv_pieces = [gather_seq(share) for share in shares]
-    own_out = unpack(qkv_pieces[-1], rows, window, 5, seq_size)
+    own_out = unpack(qkv_pieces[0], rows, window, 5, seq_size)
     up_share = lax.dynamic_slice_in_dim(w_up, c * own_hidden, own_hidden, 0)
     fill = lambda value, axis: jnp.pad(
         value, [(0, kept_hidden - own_hidden if i == axis else 0) for i in range(value.ndim)]
@@ -811,7 +795,7 @@
             ]
         )
         if g == groups - 1:
-            near = plane.send(copied(own_cotangent, all_normed1[-1:]))
+            near = plane.send(copied(own_cotangent, all_normed1[-1:]), attended)
             all_cotangent = plane.share(held(near, attended) if attended else near)
         out, kept, weight = attention_forward(
             order,
@@ -857,49 +841,52 @@
     near_branch = plane.send(d_branch)
     down_parts = plane.halves([act], [own_down], True, down_sent)
     all_branch = plane.share(near_branch, down_parts[:1])
-    down_parts = plane.exchange(held(down_parts, all_branch[-1:]))
+    down_parts = plane.exchange(held(down_parts, all_branch))
     turned = plan.piece_from[:, :, (np.arange(seq_size)[:, None] + np.arange(seq_size)) % seq_size]
     gather_ctx = lambda value: lax.all_gather(value, "ctx", axis=0)
-    round_from = (z + jnp.arange(seq_size, dtype=jnp.int32)) % seq_size
     d_qkv, d_sums, early = [], [], []
     later = attention_backward(order, all_branch, own_outs[0], qkv[0], half, down_parts[:1])
     for g in range(groups):
         out, sums = later
-        starts, extra = table(turned, g, c, z), None
+        behind = []
         if g == 0:
-            extra = folded_sums(
-                all_branch, jnp.concatenate(attended, axis=1), width, out_blocks, width, [out]
+            part_out = row_sums(
+                all_branch, [jnp.concatenate(attended, axis=1)], width, window, [out]
             )
-            starts = jnp.concatenate([starts, round_from])
+            tokens_out = call(
+                output_kernel, [resid, row(bias_model[3]), *down_parts], [(shape, low)], order=[part_out]
+            )[0][None]
+            behind = [tokens_out]
+        d_qkv.append(out)
+        d_sums.append(sums)
+        if g == groups - 1:
+            shares = [add_up(terms, [out]) for terms in early]
+            sent = plane.other_half(d_qkv, own_qkv, False, shares)
+            behind = [*behind, sent[0]]
         pieces = row_sums(
             [out],
             all_normed1,
             out.shape[1],
             width,
-            early,
-            starts=starts,
+            behind,
+            starts=table(turned, g, c, z),
             rows=rows,
             margin=rows,
             grain=plan.grain,
-            extra=extra,
         )
         if g == 0:
             grad_w_down = gather_ctx(held([grad_w_down], pieces[:1])[0])
-            tokens_out = call(
-                output_kernel, [resid, row(bias_model[3]), *down_parts], [(shape, low)], order=pieces[:1]
-            )[0][None]
         if g < groups - 1:
-            later = attention_backward(
-                order, all_branch, own_outs[g + 1], qkv[g + 1], half, [pieces[0], tokens_out]
-            )
-            early.append(scatter_line(pieces, seq_size, later[:1]))
-        d_qkv.append(out)
-        d_sums.append(sums)
+            later = attention_backward(order, all_branch, own_outs[g + 1], qkv[g + 1], half, pieces[:1])
+            early.append(spread_line(pieces, seq_size))
     grad_w_up = gather_ctx(held([grad_w_up], pieces[:1])[0])
-    sent = plane.other_half(d_qkv, own_qkv, False, pieces[:1])
-    gathered = [plane.send(share) for share in early]
-    parts = plane.exchange(plane.halves(d_qkv, own_qkv, False, sent))
-    gathered = [plane.share(near) for near in gathered]
+    halves = plane.halves(d_qkv, own_qkv, False, sent, [pieces[0], grad_w_down])
+    parts = plane.exchange(halves)
+    out_shard = scatter_seq(held([part_out], sent[:1])[0])
+    share = join_shares(
+        shares, out_shard, out_blocks[1], below, spread_line(pieces, seq_size), halves[:1]
+    )
+    gathered = plane.gather(share)
     grad_w_down = join_columns(
         jnp.int32(0),
         grad_w_down,
@@ -909,26 +896,29 @@
             for i in range(ctx_size)
         ],
     )
-    terms = spread_line(pieces, seq_size)
-    grad_tokens, sums1, share = call(
-        functools.partial(last_kernel, terms=len(parts)),
-        [tokens, d_resid, row(norm_gains[0]), *parts, *terms],
-        [(shape, jnp.float32), ((2, width), jnp.float32), (terms[0].shape, low)],
-        order=[grad_w_down] + [piece for group in gathered for piece in group[-1:]],
-    )
+    grad_tokens, sums1 = call(
+        last_kernel,
+        [tokens, d_resid, row(norm_gains[0]), *parts],
+        [(shape, jnp.float32), ((2, width), jnp.float32)],
+        order=[grad_w_down],
+    )
+    grad_w_up = widen(grad_w_up, own_hidden, width)
     grad_tokens = grad_tokens[None]
-    near = plane.send(share)
-    gathered.append(plane.share(near))
-    grad_w_up = widen(grad_w_up, own_hidden, width, near[1:3])
     grad_w_qkv, grad_w_out = final_rows(
         jnp.stack([z * ctx_size + c, c]),
         plan.source.reshape(seq_size * ctx_size, -1),
-        np.array([[plane.place(i ^ at) for i in range(ctx_size)] for at in range(ctx_size)], np.int32),
+        np.array(
+            [
+                [plane.place(i ^ at) for i in range(ctx_size)] for at in range(ctx_size)
+            ],
+            np.int32,
+        ),
         gathered,
         plan.grain,
         list(zip(plan.skip, plan.count)),
         (window, *out_blocks[1:]),
         width,
+        [grad_w_down, grad_w_up],
     )
 
     place = lambda t: lax.dynamic_update_slice(

time: 717 us -> 675 us (0.941)
  waiting for transfers between devices: 244 us -> 208 us
    ppermute x82 -> x73, waiting for transfers between devices: 215 us -> 111 us  [move(): return lax.ppermute(value, 'ctx', [(i, i ^ bits) for i in range(self.size)])]
    ppermute x5, waiting for transfers between devices: 15.6 us -> 39.2 us  [total_by_bits(): lax.ppermute(value, axis, [(i, i ^ bit) for i in range(size)])]
    all_gather x4, waiting for transfers between devices: 1.42 us -> 17.1 us  [per_device(): gather_seq = lambda value: lax.all_gather(value, 'seq', axis=0, tiled=True)]
    ppermute x6, waiting for transfers between devices: 11.8 us -> 24.4 us  [turn(): lax.ppermute(value, 'seq', [(i, (i + by) % size) for i in range(size)])]
    reduce_scatter x2 -> x3, waiting for transfers between devices: 0.02 us -> 11 us  [per_device(): lax.psum_scatter(value, 'seq', scatter_dimension=0, tiled=True)]
    ppermute x82 -> x73, starting transfers between devices: 54.3 us -> 47.3 us  [move(): return lax.ppermute(value, 'ctx', [(i, i ^ bits) for i in range(self.size)])]
    pallas_call x21 -> x22, Pallas kernels: 227 us -> 227 us  [call(): pl.pallas_call(body, in_specs=[pl.BlockSpec(memory_space=space) for space...]
    unnamed x171 -> x153, local copies, waits for them, and re-layouts: 24.3 us -> 24.6 us
  transfers between devices with their start and end apart: 101 -> 93, of which waited for: 40 -> 37; matrix products, arithmetic and copies ran while one was open for 6% -> 5% of each run, Pallas kernels for 36% -> 38%
where the time goes in v3:
time: 675 us; the launch traced here: 670 us
  Pallas kernels  311 us (46%)
  waiting for transfers between devices  208 us (31%)
  starting transfers between devices  72 us (11%)
  local copies, waits for them, and re-layouts  51.9 us (8%)
  between operations  19.4 us (3%)
  other arithmetic  8.31 us (1%)
    pallas_call x22, Pallas kernels, call(): pl.pallas_call(body, in_specs=[pl.BlockSpec(memory_space=space) for space...  227 us
    ppermute x73, waiting for transfers between devices, move(): return lax.ppermute(value, 'ctx', [(i, i ^ bits) for i in range(self.size)])  111 us
    pallas_call x8, Pallas kernels, product_rows(): pl.pallas_call(kernel, grid=(steps,), in_specs=[pl.BlockSpec((2 * rows, l...  66.9 us
    ppermute x73, starting transfers between devices, move(): return lax.ppermute(value, 'ctx', [(i, i ^ bits) for i in range(self.size)])  47.3 us
    ppermute x5, waiting for transfers between devices, total_by_bits(): lax.ppermute(value, axis, [(i, i ^ bit) for i in range(size)])  39.2 us
    unnamed x153, local copies, waits for them, and re-layouts  24.6 us
    ppermute x6, waiting for transfers between devices, turn(): lax.ppermute(value, 'seq', [(i, (i + by) % size) for i in range(size)])  24.4 us
    ppermute x6, starting transfers between devices, turn(): lax.ppermute(value, 'seq', [(i, (i + by) % size) for i in range(size)])  17.7 us
  transfers between devices with their start and end apart: 93, of which 37 were waited for; matrix products, arithmetic and copies ran while one was open for 5% of the time, Pallas kernels for 38%

profile of v3, /device:TPU:0, one launch (start us, length us, event | category | flops | bytes accessed | tf_op | source)
XLA Modules:
  0.0 669.9 jit_solution(504220243352096277)
XLA Ops:
  14.3 2.1 constant_dynamic-slice_fusion.9
  18.2 2.0 shard_map.268
  22.3 2.7 shard_map.267.refs_2_
  25.0 3.0 collective-permute-start.1
  29.6 17.5 %collective-permute-done.1.refs_4_ = bf16[256,1664]{1,0:T(8,128)(2,1)S(1)} collective-permute-done((bf16[256,1664]{1,0:T(8,128)(2,1)}, bf16[256,1664]{1,0:T(8,128)(2,1)S(1)}, u32[]{:S(2)}, u32[]{:S(2)}) %collective-permute-start.1) | collective-permute-done | bytes 852000 | tf_op jit(solution)/shard_map/ppermute | solution.py:91
  54.2 4.1 collective-permute-done.3.refs_6_
  64.4 2.2 shard_map.270.refs_0_
  68.0 12.4 %all-gather.9.cloned.1.call-done.refs_12_.refs_0_ = bf16[832,1664]{1,0:T(8,128)(2,1)} async-done(((bf16[208,1664]{1,0:T(8,128)(2,1)}), bf16[832,1664]{1,0:T(8,128)(2,1)}) %all-gather.9.cloned.1.call-update) | async-done | bytes 2768912 | tf_op jit(solution)/shard_map/all_gather | solution.py:751
  85.4 21.8 %shard_map.269 = (bf16[2048,128]{1,0:T(8,128)(2,1)}, bf16[2048,384]{1,0:T(8,128)(2,1)}, bf16[384,1600]{1,0:T(8,128)(2,1)}) custom-call(s32[16]{0:T(128)} %select_reduce_fusion.refs_0_, s32[3]{0:T(128)} %get-tuple-element.211.refs_1_, bf16[256,1664]{1,0:T(8,128)(2,1)} %shard_map.267.refs_2_, bf16[256,1664]{1,0:T(8,128)(2,1)} %collective-permute-done.refs_3_, ...), custom_call_target="tpu_custom_call" | custom-call | flops 23000000512 | bytes 65536 | tf_op jit(solution)/shard_map/pallas_call | solution.py:158
  112.4 2.0 constant_dynamic-slice_fusion.2
  115.0 2.7 shard_map.274
  117.8 2.8 collective-permute-done.11.refs_3_
  120.6 2.3 collective-permute-done.12.refs_4_
  126.4 22.0 %shard_map.273 = (bf16[2048,128]{1,0:T(8,128)(2,1)}, bf16[2048,384]{1,0:T(8,128)(2,1)}, bf16[384,1600]{1,0:T(8,128)(2,1)}) custom-call(s32[16]{0:T(128)} %select_reduce_fusion.refs_0_, s32[3]{0:T(128)} %get-tuple-element.210.refs_1_, bf16[256,1664]{1,0:T(8,128)(2,1)} %shard_map.267.refs_2_, bf16[256,1664]{1,0:T(8,128)(2,1)} %collective-permute-done.refs_3_, ...), custom_call_target="tpu_custom_call" | custom-call | flops 23000000512 | bytes 65536 | tf_op jit(solution)/shard_map/pallas_call | solution.py:158
  148.4 5.6 shard_map.275
  158.3 2.1 collective-permute-done.16.refs_6_
  160.7 2.1 collective-permute-done.17.refs_7_
  163.7 6.9 %shard_map.276 = (bf16[256,1664]{1,0:T(8,128)(2,1)}, bf16[256,1664]{1,0:T(8,128)(2,1)}, bf16[256,1664]{1,0:T(8,128)(2,1)}, bf16[256,1664]{1,0:T(8,128)(2,1)}) custom-call(bf16[2048,128]{1,0:T(8,128)(2,1)} %get-tuple-element.85.refs_2_.refs_5_.refs_0_, bf16[2048,128]{1,0:T(8,128)(2,1)} %get-tuple-element.89.refs_1_, ...), custom_call_target="tpu_custom_call" | custom-call | flops 1150000000 | bytes 65536 | tf_op jit(solution)/shard_map/pallas_call | solution.py:332
  171.3 2.9 collective-permute-start.20
  175.2 4.7 all-gather.13.cloned.1.call-done.refs_10_.refs_1_
  179.9 13.4 %shard_map.277.refs_8_.refs_12_ = bf16[2048,832]{1,0:T(8,128)(2,1)} custom-call(bf16[256,1664]{1,0:T(8,128)(2,1)} %get-tuple-element.98.refs_0_, bf16[256,1664]{1,0:T(8,128)(2,1)} %get-tuple-element.99.refs_1_, bf16[256,1664]{1,0:T(8,128)(2,1)} %get-tuple-element.100.refs_2_, bf16[128,1664]{1,0:T(8,128)(2,1)} %get-tuple-element.101.refs_3_, ...), custom_call_target="tpu_custom_call" | custom-call | flops 1150000000 | bytes 65536 | tf_op jit(solution)/shard_map/pallas_call | solution.py:158
  193.2 17.4 %collective-permute-done.19.refs_6_ = bf16[256,1664]{1,0:T(8,128)(2,1)} collective-permute-done((bf16[256,1664]{1,0:T(8,128)(2,1)}, bf16[256,1664]{1,0:T(8,128)(2,1)}, u32[]{:S(2)}, u32[]{:S(2)}) %collective-permute-start.19) | collective-permute-done | bytes 852000 | tf_op jit(solution)/shard_map/ppermute | solution.py:91
  211.5 4.4 shard_map.278
  217.9 18.4 %collective-permute-done.25.refs_1_.refs_2_ = bf16[256,1664]{1,0:T(8,128)(2,1)S(1)} collective-permute-done((bf16[256,1664]{1,0:T(8,128)(2,1)}, bf16[256,1664]{1,0:T(8,128)(2,1)S(1)}, u32[]{:S(2)}, u32[]{:S(2)}) %collective-permute-start.25) | collective-permute-done | bytes 852000 | tf_op jit(solution)/shard_map/ppermute | solution.py:91
  239.0 8.0 %collective-permute-done.27.refs_3_.refs_4_ = bf16[128,1664]{1,0:T(8,128)(2,1)} collective-permute-done((bf16[128,1664]{1,0:T(8,128)(2,1)S(1)}, bf16[128,1664]{1,0:T(8,128)(2,1)}, u32[]{:S(2)}, u32[]{:S(2)}) %collective-permute-start.27) | collective-permute-done | bytes 426016 | tf_op jit(solution)/shard_map/ppermute | solution.py:91
  251.6 21.2 %shard_map.279 = (bf16[2048,832]{1,0:T(8,128)(2,1)}, bf16[2048,832]{1,0:T(8,128)(2,1)}, f32[1,832]{1,0:T(1,128)}) custom-call(bf16[256,1664]{1,0:T(8,128)(2,1)} %get-tuple-element.103.refs_0_.refs_1_, bf16[256,1664]{1,0:T(8,128)(2,1)} %copy-done.20, bf16[256,1664]{1,0:T(8,128)(2,1)} %copy-done.21, bf16[128,1664]{1,0:T(8,128)(2,1)} %collective-permute-done.27.refs_3_.refs_4_, ...), custom_call_target="tpu_custom_call" | custom-call | flops 23000000512 | bytes 65536 | tf_op jit(solution)/shard_map/pallas_call | solution.py:158
  272.7 8.3 %shard_map.280 = (bf16[256,1664]{1,0:T(8,128)(2,1)}, bf16[256,1664]{1,0:T(8,128)(2,1)}, bf16[256,1664]{1,0:T(8,128)(2,1)}, bf16[256,1664]{1,0:T(8,128)(2,1)}) custom-call(bf16[2048,832]{1,0:T(8,128)(2,1)} %get-tuple-element.105.refs_0_, bf16[832,1600]{1,0:T(8,128)(2,1)} %all-gather.15.cloned.1.call-done.refs_10_.refs_1_), custom_call_target="tpu_custom_call" | custom-call | flops 1150000000 | bytes 65536 | tf_op jit(solution)/shard_map/pallas_call | solution.py:332
  288.2 9.5 %shard_map.281 = (bf16[256,1664]{1,0:T(8,128)(2,1)}, bf16[256,1664]{1,0:T(8,128)(2,1)}, bf16[256,1664]{1,0:T(8,128)(2,1)}, bf16[256,1664]{1,0:T(8,128)(2,1)}) custom-call(bf16[2048,832]{1,0:T(8,128)(2,1)} %get-tuple-element.105.refs_0_, bf16[832,1600]{1,0:T(8,128)(2,1)} %all-gather.15.cloned.1.call-done.refs_10_.refs_1_, bf16[256,1664]{1,0:T(8,128)(2,1)} %copy-done.36, ...), custom_call_target="tpu_custom_call" | custom-call | flops 1150000000 | bytes 65536 | tf_op jit(solution)/shard_map/pallas_call | solution.py:332
  299.4 1.9 collective-permute-start.44
  301.3 12.5 %shard_map.285.refs_8_.refs_1_ = bf16[832,1664]{1,0:T(8,128)(2,1)} custom-call(bf16[2048,832]{1,0:T(8,128)(2,1)} %get-tuple-element.105.refs_0_, bf16[256,1664]{1,0:T(8,128)(2,1)} %get-tuple-element.103.refs_0_.refs_1_, bf16[256,1664]{1,0:T(8,128)(2,1)} %copy-done.20, bf16[256,1664]{1,0:T(8,128)(2,1)} %copy-done.21, ...), custom_call_target="tpu_custom_call" | custom-call | flops 1150000000 | bytes 65536 | tf_op jit(solution)/shard_map/pallas_call | solution.py:158
  313.9 13.2 %shard_map.284.refs_7_.refs_0_ = bf16[1600,896]{1,0:T(8,128)(2,1)} custom-call(bf16[256,1664]{1,0:T(8,128)(2,1)} %get-tuple-element.98.refs_0_, bf16[256,1664]{1,0:T(8,128)(2,1)} %get-tuple-element.99.refs_1_, bf16[256,1664]{1,0:T(8,128)(2,1)} %get-tuple-element.100.refs_2_, bf16[128,1664]{1,0:T(8,128)(2,1)} %get-tuple-element.101.refs_3_, ...), custom_call_target="tpu_custom_call" | custom-call | flops 1150000000 | bytes 65536 | tf_op jit(solution)/shard_map/pallas_call | solution.py:158
  327.0 8.5 %shard_map.282 = (bf16[256,1664]{1,0:T(8,128)(2,1)}, bf16[256,1664]{1,0:T(8,128)(2,1)}, bf16[256,1664]{1,0:T(8,128)(2,1)}, bf16[256,1664]{1,0:T(8,128)(2,1)}) custom-call(bf16[2048,832]{1,0:T(8,128)(2,1)} %get-tuple-element.104.refs_0_.refs_10_, bf16[1600,832]{1,0:T(8,128)(2,1)} %all-gather.13.cloned.1.call-done.refs_10_.refs_1_, ...), custom_call_target="tpu_custom_call" | custom-call | flops 1150000000 | bytes 65536 | tf_op jit(solution)/shard_map/pallas_call | solution.py:332
  335.6 1.9 collective-permute-done.44.refs_6_
  338.4 6.1 shard_map.286
  348.9 16.9 %collective-permute-done.46.refs_6_.refs_3_.refs_2_ = bf16[256,1664]{1,0:T(8,128)(2,1)S(1)} collective-permute-done((bf16[256,1664]{1,0:T(8,128)(2,1)S(1)}, bf16[256,1664]{1,0:T(8,128)(2,1)S(1)}, u32[]{:S(2)}, u32[]{:S(2)}) %collective-permute-start.46) | collective-permute-done | bytes 852000 | tf_op jit(solution)/shard_map/ppermute | solution.py:91
  370.9 10.1 %shard_map.283 = (bf16[256,1664]{1,0:T(8,128)(2,1)}, bf16[256,1664]{1,0:T(8,128)(2,1)}, bf16[256,1664]{1,0:T(8,128)(2,1)}, bf16[256,1664]{1,0:T(8,128)(2,1)}) custom-call(bf16[2048,832]{1,0:T(8,128)(2,1)} %get-tuple-element.104.refs_0_.refs_10_, bf16[1600,832]{1,0:T(8,128)(2,1)} %all-gather.13.cloned.1.call-done.refs_10_.refs_1_, ...), custom_call_target="tpu_custom_call" | custom-call | flops 1150000000 | bytes 65536 | tf_op jit(solution)/shard_map/pallas_call | solution.py:332
  383.6 2.1 pad_maximum_fusion.refs_10_
  390.1 28.9 %shard_map.289 = (bf16[2048,384]{1,0:T(8,128)(2,1)}, f32[1,384]{1,0:T(1,128)}) custom-call(s32[16]{0:T(128)} %select_reduce_fusion.refs_0_, bf16[256,1664]{1,0:T(8,128)(2,1)} %get-tuple-element.122.refs_4_.refs_1_.refs_0_.refs_2_, bf16[256,1664]{1,0:T(8,128)(2,1)} %copy-done.10, bf16[256,1664]{1,0:T(8,128)(2,1)} %copy-done.9, ...), custom_call_target="tpu_custom_call" | custom-call | flops 32199999488 | bytes 65536 | tf_op jit(solution)/shard_map/pallas_call | solution.py:158
  419.0 6.2 shard_map.290.refs_6_.refs_0_
  428.1 4.0 shard_map.291
  432.1 7.7 %shard_map.292 = (bf16[128,1664]{1,0:T(8,128)(2,1)}, bf16[128,1664]{1,0:T(8,128)(2,1)}, bf16[128,1664]{1,0:T(8,128)(2,1)}, bf16[128,1664]{1,0:T(8,128)(2,1)}) custom-call(s32[4]{0:T(128)} %get-tuple-element.193.refs_0_, bf16[2048,384]{1,0:T(8,128)(2,1)} %get-tuple-element.128.refs_11_.refs_1_.refs_0_, bf16[256,1664]{1,0:T(8,128)(2,1)} %shard_map.267.refs_2_, ...), custom_call_target="tpu_custom_call" | custom-call | flops 1150000000 | bytes 65536 | tf_op jit(solution)/shard_map/pallas_call | solution.py:158
  442.1 2.7 collective-permute-start.59
  444.7 28.8 %shard_map.293 = (bf16[2048,384]{1,0:T(8,128)(2,1)}, f32[1,384]{1,0:T(1,128)}) custom-call(s32[16]{0:T(128)} %select_reduce_fusion.refs_0_, bf16[256,1664]{1,0:T(8,128)(2,1)} %get-tuple-element.122.refs_4_.refs_1_.refs_0_.refs_2_, bf16[256,1664]{1,0:T(8,128)(2,1)} %copy-done.10, bf16[256,1664]{1,0:T(8,128)(2,1)} %copy-done.9, ...), custom_call_target="tpu_custom_call" | custom-call | flops 32199999488 | bytes 65536 | tf_op jit(solution)/shard_map/pallas_call | solution.py:158
  473.5 8.6 %collective-permute-done.58.refs_2_ = bf16[128,1664]{1,0:T(8,128)(2,1)S(1)} collective-permute-done((bf16[128,1664]{1,0:T(8,128)(2,1)S(1)}, bf16[128,1664]{1,0:T(8,128)(2,1)S(1)}, u32[]{:S(2)}, u32[]{:S(2)}) %collective-permute-start.58) | collective-permute-done | bytes 426016 | tf_op jit(solution)/shard_map/ppermute | solution.py:132
  483.1 2.3 shard_map.294.refs_4_.refs_0_
  485.4 8.6 %shard_map.295 = (bf16[256,1664]{1,0:T(8,128)(2,1)}, bf16[256,1664]{1,0:T(8,128)(2,1)}, bf16[256,1664]{1,0:T(8,128)(2,1)}, bf16[256,1664]{1,0:T(8,128)(2,1)}) custom-call(bf16[2048,384]{1,0:T(8,128)(2,1)} %get-tuple-element.128.refs_11_.refs_1_.refs_0_, bf16[2048,384]{1,0:T(8,128)(2,1)} %get-tuple-element.132.refs_4_.refs_1_, ...), custom_call_target="tpu_custom_call" | custom-call | flops 1150000000 | bytes 65536 | tf_op jit(solution)/shard_map/pallas_call | solution.py:332
  494.1 7.7 %shard_map.296 = (bf16[128,1664]{1,0:T(8,128)(2,1)}, bf16[128,1664]{1,0:T(8,128)(2,1)}, bf16[128,1664]{1,0:T(8,128)(2,1)}, bf16[128,1664]{1,0:T(8,128)(2,1)}) custom-call(s32[4]{0:T(128)} %get-tuple-element.192.refs_0_, bf16[2048,384]{1,0:T(8,128)(2,1)} %get-tuple-element.132.refs_4_.refs_1_, bf16[256,1664]{1,0:T(8,128)(2,1)} %shard_map.267.refs_2_, ...), custom_call_target="tpu_custom_call" | custom-call | flops 1150000000 | bytes 65536 | tf_op jit(solution)/shard_map/pallas_call | solution.py:158
  504.2 9.4 %collective-permute-start.72 = (bf16[128,1664]{1,0:T(8,128)(2,1)}, bf16[128,1664]{1,0:T(8,128)(2,1)}, u32[]{:S(2)}, u32[]{:S(2)}) collective-permute-start(bf16[128,1664]{1,0:T(8,128)(2,1)} %get-tuple-element.154), channel_id=1, source_target_pairs={{0,8},{8,16},{16,24},{24,0},{1,9},{9,17},{17,25},{25,1},{2,10},{10... | collective-permute-start | bytes 1277960 | tf_op jit(solution)/shard_map/ppermute | solution.py:132
  514.8 3.4 collective-permute-start.74
  518.2 4.7 all-gather.17.cloned.1.call-done
  522.9 9.3 %shard_map.299 = (bf16[256,1664]{1,0:T(8,128)(2,1)}, bf16[256,1664]{1,0:T(8,128)(2,1)}, bf16[256,1664]{1,0:T(8,128)(2,1)}, bf16[256,1664]{1,0:T(8,128)(2,1)}) custom-call(bf16[2048,384]{1,0:T(8,128)(2,1)} %get-tuple-element.128.refs_11_.refs_1_.refs_0_, bf16[2048,384]{1,0:T(8,128)(2,1)} %get-tuple-element.132.refs_4_.refs_1_, ...), custom_call_target="tpu_custom_call" | custom-call | flops 1150000000 | bytes 65536 | tf_op jit(solution)/shard_map/pallas_call | solution.py:332
  536.2 13.7 %collective-permute-done.73.refs_4_ = bf16[128,1664]{1,0:T(8,128)(2,1)} collective-permute-done((bf16[128,1664]{1,0:T(8,128)(2,1)}, bf16[128,1664]{1,0:T(8,128)(2,1)}, u32[]{:S(2)}, u32[]{:S(2)}) %collective-permute-start.73) | collective-permute-done | bytes 426016 | tf_op jit(solution)/shard_map/ppermute | solution.py:132
  549.9 2.0 collective-permute-done.74.refs_5_
  551.9 10.9 %reduce-scatter.6.cloned.1.call-done.refs_1_ = bf16[400,256]{1,0:T(8,128)(2,1)} async-done(((bf16[1600,256]{1,0:T(8,128)(2,1)}), bf16[400,256]{1,0:T(8,128)(2,1)}) %reduce-scatter.6.cloned.1.call-update) | async-done | bytes 204816 | tf_op jit(solution)/shard_map/reduce_scatter | solution.py:833
  562.9 2.9 shard_map.303.refs_3_
  568.9 8.3 %shard_map.300.refs_7_.refs_13_ = f32[400,6400]{1,0:T(8,128)} custom-call(s32[1]{0:T(128)} %constant.91.clone.1.at_ref, bf16[8,400,896]{2,1,0:T(8,128)(2,1)} %bitcast.32), custom_call_target="tpu_custom_call" | custom-call | flops 1150000000 | bytes 65536 | tf_op jit(solution)/shard_map/pallas_call | solution.py:545
  578.7 5.5 shard_map.301
  587.1 28.5 %collective-permute-done.68 = f32[12,1600]{1,0:T(8,128)S(1)} collective-permute-done((f32[12,1600]{1,0:T(8,128)S(1)}, f32[12,1600]{1,0:T(8,128)S(1)}, u32[]{:S(2)}, u32[]{:S(2)}) %collective-permute-start.68) | collective-permute-done | bytes 76832 | tf_op jit(solution)/shard_map/ppermute | solution.py:126
  616.6 6.1 collective-permute-done.69
  624.3 3.2 collective-permute-done.70
  627.5 3.4 collective-permute-start.71
  636.5 8.3 %shard_map.305.refs_14_ = f32[1600,1600]{1,0:T(8,128)} custom-call(bf16[8,208,1664]{2,1,0:T(8,128)(2,1)} %bitcast.42), custom_call_target="tpu_custom_call" | custom-call | flops 9200000000 | bytes 65536 | tf_op jit(solution)/shard_map/pallas_call | solution.py:522
  646.4 3.3 collective-permute-done.77.refs_6_
  653.9 9.2 %shard_map.306 = (f32[1200,1600]{1,0:T(8,128)}, f32[400,1600]{1,0:T(8,128)}) custom-call(s32[2]{0:T(128)} %pad_add_fusion.refs_0_, s32[2400]{0:T(1024)} %constant.99.clone.refs_1_, s32[64]{0:T(128)} %constant.100.clone.refs_2_, bf16[352,1664]{1,0:T(8,128)(2,1)} %shard_map.303.refs_3_, bf16[352,1664]{1,0:T(8,128)(2,1)} %collective-permute-done.75.refs_4_, ...), custom_call_target="tpu_custom_call" | custom-call | flops 9200000000 | bytes 65536 | tf_op jit(solution)/shard_map/pallas_call | solution.py:158
  (387 shorter events, 115.1 us)
Async XLA Ops:
  7.2 73.2 %all-gather.9.cloned.1.call-start = ((), (), s32[]{:S(2)}) async-start(), calls=%async_computation.3 | async-start | bytes 3461120 | tf_op jit(solution)/shard_map/all_gather | solution.py:751
  20.2 104.3 %all-gather.11.cloned.1.call-start = ((), (), s32[]{:S(2)}) async-start(), calls=%async_computation.4 | async-start | bytes 2129920 | tf_op jit(solution)/shard_map/all_gather | solution.py:751
  25.0 22.1 %collective-permute-start.1 = (bf16[256,1664]{1,0:T(8,128)(2,1)}, bf16[256,1664]{1,0:T(8,128)(2,1)S(1)}, u32[]{:S(2)}, u32[]{:S(2)}) collective-permute-start(bf16[256,1664]{1,0:T(8,128)(2,1)} %shard_map.267.refs_2_), channel_id=1, source_target_pairs={{0,4},{1,5},{2,6},{3,7},{4,0},{5,1},{6,2},{7,3},{8,12},{9,13},{10,... | collective-permute-start | bytes 2555912 | tf_op jit(solution)/shard_map/ppermute | solution.py:91
  28.0 151.9 %all-gather.13.cloned.1.call-start = ((), (), s32[]{:S(2)}) async-start(), calls=%async_computation.5 | async-start | bytes 3584000 | tf_op jit(solution)/shard_map/all_gather | solution.py:751
  28.0 23.5 %collective-permute-start = (bf16[256,1664]{1,0:T(8,128)(2,1)}, bf16[256,1664]{1,0:T(8,128)(2,1)}, u32[]{:S(2)}, u32[]{:S(2)}) collective-permute-start(bf16[256,1664]{1,0:T(8,128)(2,1)} %shard_map.267.refs_2_), channel_id=1, source_target_pairs={{0,2},{1,3},{2,0},{3,1},{4,6},{5,7},{6,4},{7,5},{8,10},{9,11},{10,... | collective-permute-start | bytes 2555912 | tf_op jit(solution)/shard_map/ppermute | solution.py:91
  29.6 54.2 %collective-permute-start.4 = (bf16[256,1664]{1,0:T(8,128)(2,1)}, bf16[256,1664]{1,0:T(8,128)(2,1)}, u32[]{:S(2)}, u32[]{:S(2)}) collective-permute-start(bf16[256,1664]{1,0:T(8,128)(2,1)} %shard_map.267.refs_2_), channel_id=1, source_target_pairs={{0,1},{1,0},{2,3},{3,2},{4,5},{5,4},{6,7},{7,6},{8,9},{9,8},{10,11... | collective-permute-start | bytes 2555912 | tf_op jit(solution)/shard_map/ppermute | solution.py:91
  59.6 25.8 %collective-permute-start.5 = (bf16[256,1664]{1,0:T(8,128)(2,1)}, bf16[256,1664]{1,0:T(8,128)(2,1)}, u32[]{:S(2)}, u32[]{:S(2)}) collective-permute-start(bf16[256,1664]{1,0:T(8,128)(2,1)} %collective-permute-done.refs_3_), channel_id=1, source_target_pairs={{0,1},{1,0},{2,3},{3,2},{4,5},{5,4},{6,7},{7,6},{8,9},{9,8},{10,11... | collective-permute-start | bytes 2555912 | tf_op jit(solution)/shard_map/ppermute | solution.py:91
  60.1 25.3 %collective-permute-start.6 = (bf16[256,1664]{1,0:T(8,128)(2,1)S(1)}, bf16[256,1664]{1,0:T(8,128)(2,1)}, u32[]{:S(2)}, u32[]{:S(2)}) collective-permute-start(bf16[256,1664]{1,0:T(8,128)(2,1)S(1)} %collective-permute-done.1.refs_4_), channel_id=1, source_target_pairs={{0,1},{1,0},{2,3},{3,2},{4,5},{5,4},{6,7},{7,6},{8,9},{9,8},{10,11... | collective-permute-start | bytes 2555912 | tf_op jit(solution)/shard_map/ppermute | solution.py:91
  63.3 22.1 %collective-permute-start.7 = (bf16[128,1664]{1,0:T(8,128)(2,1)}, bf16[128,1664]{1,0:T(8,128)(2,1)}, u32[]{:S(2)}, u32[]{:S(2)}) collective-permute-start(bf16[128,1664]{1,0:T(8,128)(2,1)} %collective-permute-done.2.refs_5_), channel_id=1, source_target_pairs={{0,1},{1,0},{2,3},{3,2},{4,5},{5,4},{6,7},{7,6},{8,9},{9,8},{10,11... | collective-permute-start | bytes 1277960 | tf_op jit(solution)/shard_map/ppermute | solution.py:91
  66.6 40.6 %collective-permute-start.10 = (bf16[256,1664]{1,0:T(8,128)(2,1)}, bf16[256,1664]{1,0:T(8,128)(2,1)S(1)}, u32[]{:S(2)}, u32[]{:S(2)}) collective-permute-start(bf16[256,1664]{1,0:T(8,128)(2,1)} %shard_map.270.refs_0_), channel_id=1, source_target_pairs={{0,4},{1,5},{2,6},{3,7},{4,0},{5,1},{6,2},{7,3},{8,12},{9,13},{10,... | collective-permute-start | bytes 2555912 | tf_op jit(solution)/shard_map/ppermute | solution.py:91
  83.6 166.5 %all-gather.15.cloned.1.call-start = ((), (), s32[]{:S(2)}) async-start(), calls=%async_computation.6 | async-start | bytes 3461120 | tf_op jit(solution)/shard_map/all_gather | solution.py:751
  83.8 23.4 %collective-permute-start.9 = (bf16[256,1664]{1,0:T(8,128)(2,1)S(1)}, bf16[256,1664]{1,0:T(8,128)(2,1)S(1)}, u32[]{:S(2)}, u32[]{:S(2)}) collective-permute-start(bf16[256,1664]{1,0:T(8,128)(2,1)S(1)} %copy-done.6), channel_id=1, source_target_pairs={{0,2},{1,3},{2,0},{3,1},{4,6},{5,7},{6,4},{7,5},{8,10},{9,11},{10,... | collective-permute-start | bytes 2555912 | tf_op jit(solution)/shard_map/ppermute | solution.py:91
  155.2 284.7 %reduce-scatter.4.cloned.1.call-start = ((), (), s32[]{:S(2)}) async-start(), calls=%async_computation.7 | async-start | bytes 3584000 | tf_op jit(solution)/shard_map/reduce_scatter | solution.py:833
  156.2 15.1 %collective-permute-start.21 = (bf16[256,1664]{1,0:T(8,128)(2,1)S(1)}, bf16[256,1664]{1,0:T(8,128)(2,1)S(1)}, u32[]{:S(2)}, u32[]{:S(2)}) collective-permute-start(bf16[256,1664]{1,0:T(8,128)(2,1)S(1)} %copy-done.7), channel_id=1, source_target_pairs={{0,1},{1,0},{2,3},{3,2},{4,5},{5,4},{6,7},{7,6},{8,9},{9,8},{10,11... | collective-permute-start | bytes 2555912 | tf_op jit(solution)/shard_map/ppermute | solution.py:91
  156.8 14.1 %collective-permute-start.24 = (bf16[128,1664]{1,0:T(8,128)(2,1)S(1)}, bf16[128,1664]{1,0:T(8,128)(2,1)S(1)}, u32[]{:S(2)}, u32[]{:S(2)}) collective-permute-start(bf16[128,1664]{1,0:T(8,128)(2,1)S(1)} %copy-done.13), channel_id=1, source_target_pairs={{0,1},{1,0},{2,3},{3,2},{4,5},{5,4},{6,7},{7,6},{8,9},{9,8},{10,11... | collective-permute-start | bytes 1277960 | tf_op jit(solution)/shard_map/ppermute | solution.py:91
  157.9 16.3 %collective-permute-start.22 = (bf16[256,1664]{1,0:T(8,128)(2,1)S(1)}, bf16[256,1664]{1,0:T(8,128)(2,1)S(1)}, u32[]{:S(2)}, u32[]{:S(2)}) collective-permute-start(bf16[256,1664]{1,0:T(8,128)(2,1)S(1)} %copy-done.3), channel_id=1, source_target_pairs={{0,1},{1,0},{2,3},{3,2},{4,5},{5,4},{6,7},{7,6},{8,9},{9,8},{10,11... | collective-permute-start | bytes 2555912 | tf_op jit(solution)/shard_map/ppermute | solution.py:91
  160.3 14.8 %collective-permute-start.23 = (bf16[256,1664]{1,0:T(8,128)(2,1)S(1)}, bf16[256,1664]{1,0:T(8,128)(2,1)}, u32[]{:S(2)}, u32[]{:S(2)}) collective-permute-start(bf16[256,1664]{1,0:T(8,128)(2,1)S(1)} %copy-done.1), channel_id=1, source_target_pairs={{0,1},{1,0},{2,3},{3,2},{4,5},{5,4},{6,7},{7,6},{8,9},{9,8},{10,11... | collective-permute-start | bytes 2555912 | tf_op jit(solution)/shard_map/ppermute | solution.py:91
  170.6 22.6 %collective-permute-start.18 = (bf16[256,1664]{1,0:T(8,128)(2,1)}, bf16[256,1664]{1,0:T(8,128)(2,1)}, u32[]{:S(2)}, u32[]{:S(2)}) collective-permute-start(bf16[256,1664]{1,0:T(8,128)(2,1)} %get-tuple-element.95), channel_id=1, source_target_pairs={{0,2},{1,3},{2,0},{3,1},{4,6},{5,7},{6,4},{7,5},{8,10},{9,11},{10,... | collective-permute-start | bytes 2555912 | tf_op jit(solution)/shard_map/ppermute | solution.py:91
  170.9 39.7 %collective-permute-start.19 = (bf16[256,1664]{1,0:T(8,128)(2,1)}, bf16[256,1664]{1,0:T(8,128)(2,1)}, u32[]{:S(2)}, u32[]{:S(2)}) collective-permute-start(bf16[256,1664]{1,0:T(8,128)(2,1)} %get-tuple-element.96), channel_id=1, source_target_pairs={{0,4},{1,5},{2,6},{3,7},{4,0},{5,1},{6,2},{7,3},{8,12},{9,13},{10,... | collective-permute-start | bytes 2555912 | tf_op jit(solution)/shard_map/ppermute | solution.py:91
  171.3 39.3 %collective-permute-start.20 = (bf16[256,1664]{1,0:T(8,128)(2,1)}, bf16[256,1664]{1,0:T(8,128)(2,1)S(1)}, u32[]{:S(2)}, u32[]{:S(2)}) collective-permute-start(bf16[256,1664]{1,0:T(8,128)(2,1)} %get-tuple-element.97), channel_id=1, source_target_pairs={{0,6},{1,7},{2,4},{3,5},{4,2},{5,3},{6,0},{7,1},{8,14},{9,15},{10,... | collective-permute-start | bytes 2555912 | tf_op jit(solution)/shard_map/ppermute | solution.py:91
  215.9 20.3 %collective-permute-start.25 = (bf16[256,1664]{1,0:T(8,128)(2,1)}, bf16[256,1664]{1,0:T(8,128)(2,1)S(1)}, u32[]{:S(2)}, u32[]{:S(2)}) collective-permute-start(bf16[256,1664]{1,0:T(8,128)(2,1)} %get-tuple-element.103.refs_0_.refs_1_), channel_id=1, source_target_pairs={{0,2},{1,3},{2,0},{3,1},{4,6},{5,7},{6,4},{7,5},{8,10},{9,11},{10,... | collective-permute-start | bytes 2555912 | tf_op jit(solution)/shard_map/ppermute | solution.py:91
  217.6 20.4 %collective-permute-start.26 = (bf16[256,1664]{1,0:T(8,128)(2,1)}, bf16[256,1664]{1,0:T(8,128)(2,1)S(1)}, u32[]{:S(2)}, u32[]{:S(2)}) collective-permute-start(bf16[256,1664]{1,0:T(8,128)(2,1)} %get-tuple-element.103.refs_0_.refs_1_), channel_id=1, source_target_pairs={{0,4},{1,5},{2,6},{3,7},{4,0},{5,1},{6,2},{7,3},{8,12},{9,13},{10,... | collective-permute-start | bytes 2555912 | tf_op jit(solution)/shard_map/ppermute | solution.py:91
  217.9 32.2 %collective-permute-start.29 = (bf16[256,1664]{1,0:T(8,128)(2,1)}, bf16[256,1664]{1,0:T(8,128)(2,1)S(1)}, u32[]{:S(2)}, u32[]{:S(2)}) collective-permute-start(bf16[256,1664]{1,0:T(8,128)(2,1)} %get-tuple-element.103.refs_0_.refs_1_), channel_id=1, source_target_pairs={{0,1},{1,0},{2,3},{3,2},{4,5},{5,4},{6,7},{7,6},{8,9},{9,8},{10,11... | collective-permute-start | bytes 2555912 | tf_op jit(solution)/shard_map/ppermute | solution.py:91
  238.5 12.2 %collective-permute-start.30 = (bf16[256,1664]{1,0:T(8,128)(2,1)S(1)}, bf16[256,1664]{1,0:T(8,128)(2,1)S(1)}, u32[]{:S(2)}, u32[]{:S(2)}) collective-permute-start(bf16[256,1664]{1,0:T(8,128)(2,1)S(1)} %collective-permute-done.25.refs_1_.refs_2_), channel_id=1, source_target_pairs={{0,1},{1,0},{2,3},{3,2},{4,5},{5,4},{6,7},{7,6},{8,9},{9,8},{10,11... | collective-permute-start | bytes 2555912 | tf_op jit(solution)/shard_map/ppermute | solution.py:91
  238.5 12.2 %collective-permute-start.31 = (bf16[256,1664]{1,0:T(8,128)(2,1)S(1)}, bf16[256,1664]{1,0:T(8,128)(2,1)}, u32[]{:S(2)}, u32[]{:S(2)}) collective-permute-start(bf16[256,1664]{1,0:T(8,128)(2,1)S(1)} %collective-permute-done.26.refs_2_.refs_3_), channel_id=1, source_target_pairs={{0,1},{1,0},{2,3},{3,2},{4,5},{5,4},{6,7},{7,6},{8,9},{9,8},{10,11... | collective-permute-start | bytes 2555912 | tf_op jit(solution)/shard_map/ppermute | solution.py:91
  297.8 37.8 %collective-permute-start.42 = (bf16[256,1664]{1,0:T(8,128)(2,1)}, bf16[256,1664]{1,0:T(8,128)(2,1)S(1)}, u32[]{:S(2)}, u32[]{:S(2)}) collective-permute-start(bf16[256,1664]{1,0:T(8,128)(2,1)} %get-tuple-element.119), channel_id=1, source_target_pairs={{0,2},{1,3},{2,0},{3,1},{4,6},{5,7},{6,4},{7,5},{8,10},{9,11},{10,... | collective-permute-start | bytes 2555912 | tf_op jit(solution)/shard_map/ppermute | solution.py:91
  298.1 37.4 %collective-permute-start.43 = (bf16[256,1664]{1,0:T(8,128)(2,1)}, bf16[256,1664]{1,0:T(8,128)(2,1)S(1)}, u32[]{:S(2)}, u32[]{:S(2)}) collective-permute-start(bf16[256,1664]{1,0:T(8,128)(2,1)} %get-tuple-element.120), channel_id=1, source_target_pairs={{0,4},{1,5},{2,6},{3,7},{4,0},{5,1},{6,2},{7,3},{8,12},{9,13},{10,... | collective-permute-start | bytes 2555912 | tf_op jit(solution)/shard_map/ppermute | solution.py:91
  299.4 38.1 %collective-permute-start.44 = (bf16[256,1664]{1,0:T(8,128)(2,1)}, bf16[256,1664]{1,0:T(8,128)(2,1)S(1)}, u32[]{:S(2)}, u32[]{:S(2)}) collective-permute-start(bf16[256,1664]{1,0:T(8,128)(2,1)} %get-tuple-element.121), channel_id=1, source_target_pairs={{0,6},{1,7},{2,4},{3,5},{4,2},{5,3},{6,0},{7,1},{8,14},{9,15},{10,... | collective-permute-start | bytes 2555912 | tf_op jit(solution)/shard_map/ppermute | solution.py:91
  344.5 157.3 %reduce-scatter.8.cloned.1.call-start = ((), (), s32[]{:S(2)}) async-start(), calls=%async_computation.9 | async-start | bytes 3461120 | tf_op jit(solution)/shard_map/reduce_scatter | solution.py:833
  345.7 20.2 %collective-permute-start.46 = (bf16[256,1664]{1,0:T(8,128)(2,1)S(1)}, bf16[256,1664]{1,0:T(8,128)(2,1)S(1)}, u32[]{:S(2)}, u32[]{:S(2)}) collective-permute-start(bf16[256,1664]{1,0:T(8,128)(2,1)S(1)} %copy-done.5), channel_id=1, source_target_pairs={{0,4},{1,5},{2,6},{3,7},{4,0},{5,1},{6,2},{7,3},{8,12},{9,13},{10,... | collective-permute-start | bytes 2555912 | tf_op jit(solution)/shard_map/ppermute | solution.py:91
  347.0 175.9 %all-gather.17.cloned.1.call-start = ((), (), s32[]{:S(2)}) async-start(), calls=%async_computation.10 | async-start | bytes 6451200 | tf_op jit(solution)/shard_map/all_gather | solution.py:846
  347.1 20.0 %collective-permute-start.45 = (bf16[256,1664]{1,0:T(8,128)(2,1)S(1)}, bf16[256,1664]{1,0:T(8,128)(2,1)S(1)}, u32[]{:S(2)}, u32[]{:S(2)}) collective-permute-start(bf16[256,1664]{1,0:T(8,128)(2,1)S(1)} %copy-done.5), channel_id=1, source_target_pairs={{0,2},{1,3},{2,0},{3,1},{4,6},{5,7},{6,4},{7,5},{8,10},{9,11},{10,... | collective-permute-start | bytes 2555912 | tf_op jit(solution)/shard_map/ppermute | solution.py:91
  348.4 19.8 %collective-permute-start.38 = (bf16[256,1664]{1,0:T(8,128)(2,1)}, bf16[256,1664]{1,0:T(8,128)(2,1)S(1)}, u32[]{:S(2)}, u32[]{:S(2)}) collective-permute-start(bf16[256,1664]{1,0:T(8,128)(2,1)} %get-tuple-element.111.refs_9_), channel_id=1, source_target_pairs={{0,1},{1,0},{2,3},{3,2},{4,5},{5,4},{6,7},{7,6},{8,9},{9,8},{10,11... | collective-permute-start | bytes 2555912 | tf_op jit(solution)/shard_map/ppermute | solution.py:91
  348.4 19.8 %collective-permute-start.39 = (bf16[256,1664]{1,0:T(8,128)(2,1)}, bf16[256,1664]{1,0:T(8,128)(2,1)S(1)}, u32[]{:S(2)}, u32[]{:S(2)}) collective-permute-start(bf16[256,1664]{1,0:T(8,128)(2,1)} %get-tuple-element.112), channel_id=1, source_target_pairs={{0,1},{1,0},{2,3},{3,2},{4,5},{5,4},{6,7},{7,6},{8,9},{9,8},{10,11... | collective-permute-start | bytes 2555912 | tf_op jit(solution)/shard_map/ppermute | solution.py:91
  348.9 20.8 %collective-permute-start.40 = (bf16[256,1664]{1,0:T(8,128)(2,1)}, bf16[256,1664]{1,0:T(8,128)(2,1)S(1)}, u32[]{:S(2)}, u32[]{:S(2)}) collective-permute-start(bf16[256,1664]{1,0:T(8,128)(2,1)} %get-tuple-element.113), channel_id=1, source_target_pairs={{0,1},{1,0},{2,3},{3,2},{4,5},{5,4},{6,7},{7,6},{8,9},{9,8},{10,11... | collective-permute-start | bytes 2555912 | tf_op jit(solution)/shard_map/ppermute | solution.py:91
  367.1 13.9 %collective-permute-start.48 = (bf16[128,1664]{1,0:T(8,128)(2,1)S(1)}, bf16[128,1664]{1,0:T(8,128)(2,1)S(1)}, u32[]{:S(2)}, u32[]{:S(2)}) collective-permute-start(bf16[128,1664]{1,0:T(8,128)(2,1)S(1)} %slice.153), channel_id=1, source_target_pairs={{0,2},{1,3},{2,0},{3,1},{4,6},{5,7},{6,4},{7,5},{8,10},{9,11},{10,... | collective-permute-start | bytes 1277960 | tf_op jit(solution)/shard_map/ppermute | solution.py:91
  368.2 17.5 %collective-permute-start.49 = (bf16[256,1664]{1,0:T(8,128)(2,1)S(1)}, bf16[256,1664]{1,0:T(8,128)(2,1)}, u32[]{:S(2)}, u32[]{:S(2)}) collective-permute-start(bf16[256,1664]{1,0:T(8,128)(2,1)S(1)} %copy-done.5), channel_id=1, source_target_pairs={{0,1},{1,0},{2,3},{3,2},{4,5},{5,4},{6,7},{7,6},{8,9},{9,8},{10,11... | collective-permute-start | bytes 2555912 | tf_op jit(solution)/shard_map/ppermute | solution.py:91
  368.2 13.8 %collective-permute-start.47 = (bf16[128,1664]{1,0:T(8,128)(2,1)}, bf16[128,1664]{1,0:T(8,128)(2,1)}, u32[]{:S(2)}, u32[]{:S(2)}) collective-permute-start(bf16[128,1664]{1,0:T(8,128)(2,1)} %slice.152), channel_id=1, source_target_pairs={{0,4},{1,5},{2,6},{3,7},{4,0},{5,1},{6,2},{7,3},{8,12},{9,13},{10,... | collective-permute-start | bytes 1277960 | tf_op jit(solution)/shard_map/ppermute | solution.py:91
  369.6 16.1 %collective-permute-start.50 = (bf16[256,1664]{1,0:T(8,128)(2,1)S(1)}, bf16[256,1664]{1,0:T(8,128)(2,1)}, u32[]{:S(2)}, u32[]{:S(2)}) collective-permute-start(bf16[256,1664]{1,0:T(8,128)(2,1)S(1)} %collective-permute-done.45.refs_5_.refs_2_.refs_1_), channel_id=1, source_target_pairs={{0,1},{1,0},{2,3},{3,2},{4,5},{5,4},{6,7},{7,6},{8,9},{9,8},{10,11... | collective-permute-start | bytes 2555912 | tf_op jit(solution)/shard_map/ppermute | solution.py:91
  369.8 16.0 %collective-permute-start.51 = (bf16[256,1664]{1,0:T(8,128)(2,1)S(1)}, bf16[256,1664]{1,0:T(8,128)(2,1)}, u32[]{:S(2)}, u32[]{:S(2)}) collective-permute-start(bf16[256,1664]{1,0:T(8,128)(2,1)S(1)} %collective-permute-done.46.refs_6_.refs_3_.refs_2_), channel_id=1, source_target_pairs={{0,1},{1,0},{2,3},{3,2},{4,5},{5,4},{6,7},{7,6},{8,9},{9,8},{10,11... | collective-permute-start | bytes 2555912 | tf_op jit(solution)/shard_map/ppermute | solution.py:91
  386.6 38.6 %collective-permute-start.54 = (bf16[256,1664]{1,0:T(8,128)(2,1)}, bf16[256,1664]{1,0:T(8,128)(2,1)S(1)}, u32[]{:S(2)}, u32[]{:S(2)}) collective-permute-start(bf16[256,1664]{1,0:T(8,128)(2,1)} %get-tuple-element.124), channel_id=1, source_target_pairs={{0,2},{1,3},{2,0},{3,1},{4,6},{5,7},{6,4},{7,5},{8,10},{9,11},{10,... | collective-permute-start | bytes 2555912 | tf_op jit(solution)/shard_map/ppermute | solution.py:91
  387.6 39.3 %collective-permute-start.55 = (bf16[256,1664]{1,0:T(8,128)(2,1)}, bf16[256,1664]{1,0:T(8,128)(2,1)S(1)}, u32[]{:S(2)}, u32[]{:S(2)}) collective-permute-start(bf16[256,1664]{1,0:T(8,128)(2,1)} %get-tuple-element.125), channel_id=1, source_target_pairs={{0,4},{1,5},{2,6},{3,7},{4,0},{5,1},{6,2},{7,3},{8,12},{9,13},{10,... | collective-permute-start | bytes 2555912 | tf_op jit(solution)/shard_map/ppermute | solution.py:91
  389.0 37.9 %collective-permute-start.56 = (bf16[256,1664]{1,0:T(8,128)(2,1)}, bf16[256,1664]{1,0:T(8,128)(2,1)S(1)}, u32[]{:S(2)}, u32[]{:S(2)}) collective-permute-start(bf16[256,1664]{1,0:T(8,128)(2,1)} %get-tuple-element.126), channel_id=1, source_target_pairs={{0,6},{1,7},{2,4},{3,5},{4,2},{5,3},{6,0},{7,1},{8,14},{9,15},{10,... | collective-permute-start | bytes 2555912 | tf_op jit(solution)/shard_map/ppermute | solution.py:91
  439.9 122.9 %reduce-scatter.6.cloned.1.call-start = ((), (), s32[]{:S(2)}) async-start(), calls=%async_computation.8 | async-start | bytes 1024000 | tf_op jit(solution)/shard_map/reduce_scatter | solution.py:833
  440.8 32.7 %collective-permute-start.57 = (bf16[128,1664]{1,0:T(8,128)(2,1)S(1)}, bf16[128,1664]{1,0:T(8,128)(2,1)S(1)}, u32[]{:S(2)}, u32[]{:S(2)}) collective-permute-start(bf16[128,1664]{1,0:T(8,128)(2,1)S(1)} %copy-done.69), channel_id=1, source_target_pairs={{0,8},{8,16},{16,24},{24,0},{1,9},{9,17},{17,25},{25,1},{2,10},{10... | collective-permute-start | bytes 1277960 | tf_op jit(solution)/shard_map/ppermute | solution.py:132
  441.0 41.1 %collective-permute-start.58 = (bf16[128,1664]{1,0:T(8,128)(2,1)S(1)}, bf16[128,1664]{1,0:T(8,128)(2,1)S(1)}, u32[]{:S(2)}, u32[]{:S(2)}) collective-permute-start(bf16[128,1664]{1,0:T(8,128)(2,1)S(1)} %copy-done.68), channel_id=1, source_target_pairs={{0,16},{8,24},{16,0},{24,8},{1,17},{9,25},{17,1},{25,9},{2,18},{10... | collective-permute-start | bytes 1277960 | tf_op jit(solution)/shard_map/ppermute | solution.py:132
  442.1 40.1 %collective-permute-start.59 = (bf16[128,1664]{1,0:T(8,128)(2,1)S(1)}, bf16[128,1664]{1,0:T(8,128)(2,1)S(1)}, u32[]{:S(2)}, u32[]{:S(2)}) collective-permute-start(bf16[128,1664]{1,0:T(8,128)(2,1)S(1)} %copy-done.67), channel_id=1, source_target_pairs={{0,24},{8,0},{16,8},{24,16},{1,25},{9,1},{17,9},{25,17},{2,26},{10... | collective-permute-start | bytes 1277960 | tf_op jit(solution)/shard_map/ppermute | solution.py:132
  494.0 142.5 %all-gather.19.cloned.1.call-start = ((), (), s32[]{:S(2)}) async-start(), calls=%async_computation.11 | async-start | bytes 6230016 | tf_op jit(solution)/shard_map/all_gather | solution.py:846
  503.4 14.8 %collective-permute-start.62 = (bf16[256,1664]{1,0:T(8,128)(2,1)}, bf16[256,1664]{1,0:T(8,128)(2,1)S(1)}, u32[]{:S(2)}, u32[]{:S(2)}) collective-permute-start(bf16[256,1664]{1,0:T(8,128)(2,1)} %get-tuple-element.142), channel_id=1, source_target_pairs={{0,1},{1,0},{2,3},{3,2},{4,5},{5,4},{6,7},{7,6},{8,9},{9,8},{10,11... | collective-permute-start | bytes 2555912 | tf_op jit(solution)/shard_map/ppermute | solution.py:91
  503.4 14.8 %collective-permute-start.63 = (bf16[256,1664]{1,0:T(8,128)(2,1)}, bf16[256,1664]{1,0:T(8,128)(2,1)}, u32[]{:S(2)}, u32[]{:S(2)}) collective-permute-start(bf16[256,1664]{1,0:T(8,128)(2,1)} %get-tuple-element.143), channel_id=1, source_target_pairs={{0,1},{1,0},{2,3},{3,2},{4,5},{5,4},{6,7},{7,6},{8,9},{9,8},{10,11... | collective-permute-start | bytes 2555912 | tf_op jit(solution)/shard_map/ppermute | solution.py:91
  504.2 30.1 %collective-permute-start.72 = (bf16[128,1664]{1,0:T(8,128)(2,1)}, bf16[128,1664]{1,0:T(8,128)(2,1)}, u32[]{:S(2)}, u32[]{:S(2)}) collective-permute-start(bf16[128,1664]{1,0:T(8,128)(2,1)} %get-tuple-element.154), channel_id=1, source_target_pairs={{0,8},{8,16},{16,24},{24,0},{1,9},{9,17},{17,25},{25,1},{2,10},{10... | collective-permute-start | bytes 1277960 | tf_op jit(solution)/shard_map/ppermute | solution.py:132
  513.7 36.2 %collective-permute-start.73 = (bf16[128,1664]{1,0:T(8,128)(2,1)}, bf16[128,1664]{1,0:T(8,128)(2,1)}, u32[]{:S(2)}, u32[]{:S(2)}) collective-permute-start(bf16[128,1664]{1,0:T(8,128)(2,1)} %get-tuple-element.155), channel_id=1, source_target_pairs={{0,16},{8,24},{16,0},{24,8},{1,17},{9,25},{17,1},{25,9},{2,18},{10... | collective-permute-start | bytes 1277960 | tf_op jit(solution)/shard_map/ppermute | solution.py:132
  514.8 37.2 %collective-permute-start.74 = (bf16[128,1664]{1,0:T(8,128)(2,1)}, bf16[128,1664]{1,0:T(8,128)(2,1)}, u32[]{:S(2)}, u32[]{:S(2)}) collective-permute-start(bf16[128,1664]{1,0:T(8,128)(2,1)} %get-tuple-element.156), channel_id=1, source_target_pairs={{0,24},{8,0},{16,8},{24,16},{1,25},{9,1},{17,9},{25,17},{2,26},{10... | collective-permute-start | bytes 1277960 | tf_op jit(solution)/shard_map/ppermute | solution.py:132
  532.3 44.8 %collective-permute-start.64 = (bf16[256,1664]{1,0:T(8,128)(2,1)}, bf16[256,1664]{1,0:T(8,128)(2,1)S(1)}, u32[]{:S(2)}, u32[]{:S(2)}) collective-permute-start(bf16[256,1664]{1,0:T(8,128)(2,1)} %get-tuple-element.145), channel_id=1, source_target_pairs={{0,2},{1,3},{2,0},{3,1},{4,6},{5,7},{6,4},{7,5},{8,10},{9,11},{10,... | collective-permute-start | bytes 2555912 | tf_op jit(solution)/shard_map/ppermute | solution.py:91
  533.8 43.4 %collective-permute-start.65 = (bf16[256,1664]{1,0:T(8,128)(2,1)}, bf16[256,1664]{1,0:T(8,128)(2,1)S(1)}, u32[]{:S(2)}, u32[]{:S(2)}) collective-permute-start(bf16[256,1664]{1,0:T(8,128)(2,1)} %get-tuple-element.146), channel_id=1, source_target_pairs={{0,4},{1,5},{2,6},{3,7},{4,0},{5,1},{6,2},{7,3},{8,12},{9,13},{10,... | collective-permute-start | bytes 2555912 | tf_op jit(solution)/shard_map/ppermute | solution.py:91
  534.3 42.8 %collective-permute-start.66 = (bf16[256,1664]{1,0:T(8,128)(2,1)}, bf16[256,1664]{1,0:T(8,128)(2,1)S(1)}, u32[]{:S(2)}, u32[]{:S(2)}) collective-permute-start(bf16[256,1664]{1,0:T(8,128)(2,1)} %get-tuple-element.147), channel_id=1, source_target_pairs={{0,6},{1,7},{2,4},{3,5},{4,2},{5,3},{6,0},{7,1},{8,14},{9,15},{10,... | collective-permute-start | bytes 2555912 | tf_op jit(solution)/shard_map/ppermute | solution.py:91
  565.8 67.0 %collective-permute-start.75 = (bf16[352,1664]{1,0:T(8,128)(2,1)}, bf16[352,1664]{1,0:T(8,128)(2,1)}, u32[]{:S(2)}, u32[]{:S(2)}) collective-permute-start(bf16[352,1664]{1,0:T(8,128)(2,1)} %shard_map.303.refs_3_), channel_id=1, source_target_pairs={{0,2},{1,3},{2,0},{3,1},{4,6},{5,7},{6,4},{7,5},{8,10},{9,11},{10,... | collective-permute-start | bytes 3514376 | tf_op jit(solution)/shard_map/ppermute | solution.py:91
  567.3 66.9 %collective-permute-start.76 = (bf16[352,1664]{1,0:T(8,128)(2,1)}, bf16[352,1664]{1,0:T(8,128)(2,1)}, u32[]{:S(2)}, u32[]{:S(2)}) collective-permute-start(bf16[352,1664]{1,0:T(8,128)(2,1)} %shard_map.303.refs_3_), channel_id=1, source_target_pairs={{0,4},{1,5},{2,6},{3,7},{4,0},{5,1},{6,2},{7,3},{8,12},{9,13},{10,... | collective-permute-start | bytes 3514376 | tf_op jit(solution)/shard_map/ppermute | solution.py:91
  586.5 29.1 %collective-permute-start.68 = (f32[12,1600]{1,0:T(8,128)S(1)}, f32[12,1600]{1,0:T(8,128)S(1)}, u32[]{:S(2)}, u32[]{:S(2)}) collective-permute-start(f32[12,1600]{1,0:T(8,128)S(1)} %add.131), channel_id=1, source_target_pairs={{0,2},{1,3},{2,0},{3,1},{4,6},{5,7},{6,4},{7,5},{8,10},{9,11},{10,... | collective-permute-start | bytes 230408 | tf_op jit(solution)/shard_map/ppermute | solution.py:126
  632.8 20.1 %collective-permute-start.79 = (bf16[352,1664]{1,0:T(8,128)(2,1)}, bf16[352,1664]{1,0:T(8,128)(2,1)}, u32[]{:S(2)}, u32[]{:S(2)}) collective-permute-start(bf16[352,1664]{1,0:T(8,128)(2,1)} %shard_map.303.refs_3_), channel_id=1, source_target_pairs={{0,1},{1,0},{2,3},{3,2},{4,5},{5,4},{6,7},{7,6},{8,9},{9,8},{10,11... | collective-permute-start | bytes 3514376 | tf_op jit(solution)/shard_map/ppermute | solution.py:91
  633.9 15.8 %collective-permute-start.77 = (bf16[176,1664]{1,0:T(8,128)(2,1)S(1)}, bf16[176,1664]{1,0:T(8,128)(2,1)}, u32[]{:S(2)}, u32[]{:S(2)}) collective-permute-start(bf16[176,1664]{1,0:T(8,128)(2,1)S(1)} %slice.157), channel_id=1, source_target_pairs={{0,4},{1,5},{2,6},{3,7},{4,0},{5,1},{6,2},{7,3},{8,12},{9,13},{10,... | collective-permute-start | bytes 1757192 | tf_op jit(solution)/shard_map/ppermute | solution.py:91
  635.3 15.6 %collective-permute-start.78 = (bf16[176,1664]{1,0:T(8,128)(2,1)S(1)}, bf16[176,1664]{1,0:T(8,128)(2,1)}, u32[]{:S(2)}, u32[]{:S(2)}) collective-permute-start(bf16[176,1664]{1,0:T(8,128)(2,1)S(1)} %slice.158), channel_id=1, source_target_pairs={{0,2},{1,3},{2,0},{3,1},{4,6},{5,7},{6,4},{7,5},{8,10},{9,11},{10,... | collective-permute-start | bytes 1757192 | tf_op jit(solution)/shard_map/ppermute | solution.py:91
  636.0 17.1 %collective-permute-start.80 = (bf16[352,1664]{1,0:T(8,128)(2,1)}, bf16[352,1664]{1,0:T(8,128)(2,1)}, u32[]{:S(2)}, u32[]{:S(2)}) collective-permute-start(bf16[352,1664]{1,0:T(8,128)(2,1)} %collective-permute-done.75.refs_4_), channel_id=1, source_target_pairs={{0,1},{1,0},{2,3},{3,2},{4,5},{5,4},{6,7},{7,6},{8,9},{9,8},{10,11... | collective-permute-start | bytes 3514376 | tf_op jit(solution)/shard_map/ppermute | solution.py:91
  636.0 17.1 %collective-permute-start.81 = (bf16[352,1664]{1,0:T(8,128)(2,1)}, bf16[352,1664]{1,0:T(8,128)(2,1)}, u32[]{:S(2)}, u32[]{:S(2)}) collective-permute-start(bf16[352,1664]{1,0:T(8,128)(2,1)} %collective-permute-done.76.refs_5_), channel_id=1, source_target_pairs={{0,1},{1,0},{2,3},{3,2},{4,5},{5,4},{6,7},{7,6},{8,9},{9,8},{10,11... | collective-permute-start | bytes 3514376 | tf_op jit(solution)/shard_map/ppermute | solution.py:91
  (103 other events, 592.7 us)
Sparse Core Ops, SparseCore 0:
  20.4 59.9 all-gather.8
  82.5 37.9 all-gather.10
  122.1 57.7 all-gather.12
  181.9 55.9 all-gather.14
  344.7 53.9 reduce-scatter.3
  400.8 70.0 reduce-scatter.7
  472.9 49.9 all-gather.16
  525.9 36.9 reduce-scatter.5
  564.9 59.5 all-gather.18
